TPU v7x, 256 devices: a whole 4x4x8 slice. The times are simulated.
256 devices in a mesh: ctx: 32 (over y, z), ch: 8 (over x, core).
Axes of the slice: x: 4, y: 4, z: 8, core: 2. Of those that a mesh axis runs over, the one named last changes fastest.
Arguments:
- query_in: bfloat16 [4096, 8192], P('ch', 'ctx'), may hold values from -6 to 6
- key_in: bfloat16 [4096, 8192], P('ch', 'ctx'), may hold values from -6 to 6
- value_in: bfloat16 [4096, 8192], P('ch', 'ctx'), may hold values from -6 to 6
- short_taps: float32 [3, 4096, 3], P(None, 'ch'), may hold values from -3 to 3
- modal_residue: float32 [4096, 16], P('ch'), may hold values from -2.5 to 2.5
- mode_damping_speed: float32 [4096, 16], P('ch'), may hold values from 6.1035156e-05 to 0.05
- skip_gain: float32 [4096], P('ch'), may hold values from 0.5 to 1.5
- out_weight: bfloat16 [4096, 4096], P('ch'), may hold values from -0.125 to 0.125
Outputs:
- mixed: bfloat16 [4096, 8192], P('ch', 'ctx')
All inputs are finite; a program needn't handle non-finite values.
Results may differ from a plain program's by a relative error of at most 0.01.
Values may be sent and summed in bfloat16 or wider, within the bound.
No kernel may reach another device: no remote copies, remote signals or barrier semaphores. Data moves between devices by JAX's collectives and lax.ppermute only.
A program may use at most 128 MiB of HBM per device.

v0:
```python
import functools

import jax
import jax.numpy as jnp
from jax import lax
from jax.experimental import pallas as pl
from jax.experimental.pallas import tpu as pltpu
from jax.sharding import PartitionSpec as P

SEGMENTS = 8
LANES = 128
ORDER = 16
ROW = 8
SCOPED = 16 * 2**20
F32 = jnp.float32
BF16 = jnp.bfloat16
NT = (((1,), (1,)), ((), ()))
TN = (((0,), (0,)), ((), ()))

STEPS = ((1, 1), (2, 2), (4, 7))
DECAY, FADE, WEIGHT, GROWTH, OVER_Z, OVER_Y = 0, 1, 4, 5, 7, 22
TABLES = 28
SKIP, GROWN, FIRST = 9, 10, 11
EDGES = 32


def call(kernel, name, out, scratch=(), held=True, outside=(), unread=()):
    whole = pl.BlockSpec(memory_space=pltpu.VMEM)
    place = (lambda o: pltpu.VMEM(o.shape, o.dtype)) if held else (lambda o: o)

    def run(*args):
        spaces = [
            pl.ANY if i in unread else pltpu.HBM if i in outside else pltpu.VMEM
            for i in range(len(args))
        ]
        return pl.pallas_call(
            kernel,
            in_specs=[pl.BlockSpec(memory_space=space) for space in spaces],
            out_specs=jax.tree.map(lambda _: whole, out),
            out_shape=jax.tree.map(place, out),
            scratch_shapes=list(scratch),
            compiler_params=pltpu.CompilerParams(vmem_limit_bytes=SCOPED),
            name=name,
        )(*(pltpu.with_memory_space_constraint(a, space) for a, space in zip(args, spaces)))

    return run


def order_matrix(span):
    steps = span // SEGMENTS
    row = lax.broadcasted_iota(jnp.int32, (span, span), 0)
    col = lax.broadcasted_iota(jnp.int32, (span, span), 1)
    return jnp.where(col == (row & (SEGMENTS - 1)) * steps + (row >> 3), 1.0, 0.0).astype(BF16)


def segment_index():
    return lax.broadcasted_iota(jnp.int32, (SEGMENTS, LANES), 0)


def by_group(channels, body):
    def step(g, nothing):
        body(pl.ds(pl.multiple_of(g * LANES, LANES), LANES))
        return nothing

    lax.fori_loop(0, channels // LANES, step, 0)


def place_of():
    here = lax.axis_index("ctx")
    return here // ROW, lax.rem(here, ROW)


def fill_tables(damping, residue, span, tables):
    y, z = place_of()

    def fade(by):
        return jnp.exp(-damping * by)

    def only(flag, value):
        return jnp.where(flag, value, 0.0)

    tables[DECAY] = fade(1.0)
    for i in range(3):
        tables[FADE + i] = fade(float((span // SEGMENTS) << i))
    tables[WEIGHT] = residue * jnp.sqrt(damping)
    tables[GROWTH] = fade(-1.0)
    tables[GROWTH + 1] = fade(-2.0)
    for j, (size, _) in enumerate(STEPS):
        at = OVER_Z + 5 * j
        older = (z & size) != 0
        ahead = (z & (size - 1)) * span
        whole = fade(float(size * span))
        tables[at] = only(older, fade(ahead.astype(F32)))
        seen = jnp.maximum(ahead - 2, 0).astype(F32)
        tables[at + 1] = only(older & (ahead > 0), fade(seen))
        tables[at + 2] = jnp.where(older, whole, 1.0)
        tables[at + 3] = jnp.where(older, 1.0, whole)
        tables[at + 4] = fade(float(size * span - 2))
    for s in range(3):
        ahead = (ROW * s + z) * span
        tables[OVER_Y + s] = only(y >= s + 1, fade(ahead.astype(F32)))
        seen = jnp.maximum(ahead - 2, 0).astype(F32)
        tables[OVER_Y + 3 + s] = only((y >= s + 1) & (ahead > 0), fade(seen))


def states_kernel(
    key_hbm,
    value_hbm,
    query_hbm,
    taps_hbm,
    damping_hbm,
    residue_hbm,
    skip_hbm,
    message,
    gated,
    params,
    tables,
    raw,
    tail,
    taps_in,
    damping,
    residue,
    skip,
    streams,
    state,
    edges,
    sems,
):
    channels, span = key_hbm.shape
    steps = span // SEGMENTS
    copies = [
        pltpu.make_async_copy(src, dst, sems.at[i])
        for i, (src, dst) in enumerate(
            (
                (damping_hbm, damping),
                (residue_hbm, residue),
                (key_hbm, raw.at[0]),
                (value_hbm, raw.at[1]),
                (taps_hbm, taps_in),
                (skip_hbm, skip),
                (query_hbm.at[:, span - LANES :], tail),
            )
        )
    ]
    for c in copies:
        c.start()
    order = order_matrix(span)
    for c in copies[:2]:
        c.wait()
    fill_tables(damping[...], residue[...], span, tables)
    for c in copies[2:]:
        c.wait()
    for s in range(2):
        streams[s] = lax.dot_general(order, raw[s], NT, preferred_element_type=F32)
    segment = segment_index()
    params[...] = jnp.zeros_like(params)
    for i in range(9):
        params[i : i + 1, :] = taps_in[(1 + i // 3) % 3, i % 3, :][None, :]
    params[SKIP : SKIP + 1, :] = skip[...]
    params[GROWN : GROWN + 1, :] = jnp.sum(
        tables[WEIGHT] * tables[GROWTH], axis=0, keepdims=True
    )

    def group(lanes):
        taps = [params[i : i + 1, lanes] for i in range(6)]
        decay = [tables[DECAY, r : r + 1, lanes] for r in range(ORDER)]

        def at(s, a):
            if a >= 0:
                return streams[s, a * SEGMENTS : (a + 1) * SEGMENTS, lanes]
            rolled = pltpu.roll(at(s, a + steps), 1, 0)
            return jnp.where(segment == 0, 0.0, rolled)

        held = [jnp.zeros((SEGMENTS, LANES), F32) for _ in range(ORDER)]
        for a in range(steps):
            f = [
                taps[3 * s] * at(s, a)
                + taps[3 * s + 1] * at(s, a - 1)
                + taps[3 * s + 2] * at(s, a - 2)
                for s in range(2)
            ]
            u = f[0] * f[1]
            if a < 2:
                params[FIRST + a : FIRST + a + 1, lanes] = f[0][0:1]
                params[FIRST + 2 + a : FIRST + 3 + a, lanes] = f[1][0:1]
                u = jnp.where(segment == 0, 0.0, u)
            gated[a * SEGMENTS : (a + 1) * SEGMENTS, lanes] = u
            for r in range(ORDER):
                held[r] = held[r] * decay[r] + u
        for r in range(ORDER):
            total = held[r]
            for i in range(3):
                fade = tables[FADE + i, r : r + 1, lanes]
                total = total + fade * pltpu.roll(total, 1 << i, 0)
            state[r : r + 1, lanes] = total[SEGMENTS - 1 :]

    by_group(channels, group)
    high = state[...].astype(BF16)
    message[0:ORDER, :] = high
    message[ORDER:EDGES, :] = (state[...] - high.astype(F32)).astype(BF16)
    edges[...] = jnp.zeros_like(edges)
    for s in range(2):
        edges[2 * s : 2 * s + 1, :] = streams[s, 0:1, :]
        edges[2 * s + 1 : 2 * s + 2, :] = streams[s, SEGMENTS : SEGMENTS + 1, :]
        edges[4 + 2 * s : 5 + 2 * s, :] = streams[s, span - SEGMENTS - 1 : span - SEGMENTS, :]
        edges[5 + 2 * s : 6 + 2 * s, :] = streams[s, span - 1 : span, :]
    row = lax.broadcasted_iota(jnp.int32, (8, LANES), 0)
    col = lax.broadcasted_iota(jnp.int32, (8, LANES), 1)
    pick = jnp.where(col == LANES - 2 + row, 1.0, 0.0).astype(BF16)
    edges[8:16, :] = lax.dot_general(pick, tail[...], NT, preferred_element_type=F32)
    message[EDGES:, :] = edges[...].astype(BF16)


def states(key_in, value_in, query_in, taps, damping, residue, skip):
    channels, span = key_in.shape
    shape = jax.ShapeDtypeStruct
    out = [
        shape((EDGES + 16, channels), BF16),
        shape((span, channels), F32),
        shape((16, channels), F32),
        shape((TABLES, ORDER, channels), F32),
    ]
    scratch = [
        pltpu.VMEM((2, channels, span), BF16),
        pltpu.VMEM((channels, LANES), BF16),
        pltpu.VMEM(taps.shape, F32),
        pltpu.VMEM(damping.shape, F32),
        pltpu.VMEM(residue.shape, F32),
        pltpu.VMEM(skip.shape, F32),
        pltpu.VMEM((2, span, channels), F32),
        pltpu.VMEM((ORDER, channels), F32),
        pltpu.VMEM((16, channels), F32),
        pltpu.SemaphoreType.DMA((7,)),
    ]
    return call(states_kernel, "states", out, scratch, outside=range(7))(
        key_in, value_in, query_in, taps, damping, residue, skip
    )


def local_kernel(
    gated, query_hbm, params, tables, after, local, gate, carry, reach, raw, stream, sem
):
    channels, span = query_hbm.shape
    steps = span // SEGMENTS
    copy = pltpu.make_async_copy(query_hbm, raw, sem)
    copy.start()
    order = order_matrix(span)
    copy.wait()
    stream[...] = lax.dot_general(order, raw[...], NT, preferred_element_type=F32)
    segment = segment_index()

    def group(lanes):
        taps = [params[6 + i : 7 + i, lanes] for i in range(3)]
        skip = params[SKIP : SKIP + 1, lanes]
        decay = [tables[DECAY, r : r + 1, lanes] for r in range(ORDER)]
        weight = [tables[WEIGHT, r : r + 1, lanes] for r in range(ORDER)]

        def at(a):
            if a >= 0:
                return stream[a * SEGMENTS : (a + 1) * SEGMENTS, lanes]
            rolled = pltpu.roll(at(a + steps), 1, 0)
            return jnp.where(segment == 0, 0.0, rolled)

        held = [jnp.zeros((SEGMENTS, LANES), F32) for _ in range(ORDER)]
        for a in range(steps):
            here = slice(a * SEGMENTS, (a + 1) * SEGMENTS)
            u = gated[here, lanes]
            parts = [skip * u, None, None, None]
            for r in range(ORDER):
                held[r] = held[r] * decay[r] + u
                term = weight[r] * held[r]
                parts[r % 4] = term if parts[r % 4] is None else parts[r % 4] + term
            local[here, lanes] = (parts[0] + parts[1]) + (parts[2] + parts[3])
            gate[here, lanes] = taps[0] * at(a) + taps[1] * at(a - 1) + taps[2] * at(a - 2)
        for r in range(ORDER):
            total = held[r]
            far = jnp.ones((SEGMENTS, LANES), F32)
            for i in range(3):
                fade = tables[FADE + i, r : r + 1, lanes]
                by = 1 << i
                total = total + jnp.where(segment < by, 0.0, fade * pltpu.roll(total, by, 0))
                far = jnp.where((segment & by) != 0, far * fade, far)
            total = jnp.where(segment < 1, 0.0, pltpu.roll(total, 1, 0))
            here = slice(r * SEGMENTS, (r + 1) * SEGMENTS)
            scale = weight[r] * decay[r]
            carry[here, lanes] = scale * total
            reach[here, lanes] = scale * far

    by_group(channels, group)


def local_scan(gated, query_in, params, tables, after):
    channels, span = query_in.shape
    shape = jax.ShapeDtypeStruct
    out = [
        shape((span, channels), F32),
        shape((span, channels), F32),
        shape((ORDER * SEGMENTS, channels), F32),
        shape((ORDER * SEGMENTS, channels), F32),
    ]
    scratch = [
        pltpu.VMEM((channels, span), BF16),
        pltpu.VMEM((span, channels), F32),
        pltpu.SemaphoreType.DMA,
    ]
    return call(local_kernel, "local_scan", out, scratch, outside=(1,), unread=(4,))(
        gated, query_in, params, tables, after
    )


def unpack(message):
    state = message[0:ORDER, :].astype(F32) + message[ORDER:EDGES, :].astype(F32)
    return state, message[EDGES:, :].astype(F32)


def gated_start(params, new, old):
    out = []
    for s in range(2):
        near, mid, far = (params[3 * s + i : 3 * s + i + 1, :] for i in range(3))
        first, second = new[2 * s : 2 * s + 1], new[2 * s + 1 : 2 * s + 2]
        before, last = old[4 + 2 * s : 5 + 2 * s], old[5 + 2 * s : 6 + 2 * s]
        out.append(
            (near * first + mid * last + far * before, near * second + mid * first + far * last)
        )
    (k0, k1), (v0, v1) = out
    return k0 * v0, k1 * v1


def merge_kernel(
    j, mine, theirs, before, border, params, tables, after, message, before_out, border_out
):
    size = STEPS[j][0]
    at = OVER_Z + 5 * j
    _, z = place_of()
    older = (z & size) != 0
    first = (z & (size - 1)) == 0
    my_state, my_edges = unpack(mine)
    state, edges = unpack(theirs)
    new = jnp.where(older, my_edges, edges)
    old = jnp.where(older, edges, my_edges)
    u0, u1 = gated_start(params, new, old)
    seam = tables[DECAY] * u0 + u1
    total = tables[at + 2] * state + tables[at + 3] * my_state + tables[at + 4] * seam
    high = total.astype(BF16)
    message[0:ORDER, :] = high
    message[ORDER:EDGES, :] = (total - high.astype(F32)).astype(BF16)
    row = lax.broadcasted_iota(jnp.int32, my_edges.shape, 0)
    message[EDGES:, :] = jnp.where(row < 4, old, new).astype(BF16)
    before_out[...] = before[...] + tables[at] * state + tables[at + 1] * seam
    border_out[...] = jnp.where(older & first, edges, border[...])


def merge(j, mine, theirs, before, border, params, tables, after):
    shape = jax.ShapeDtypeStruct
    out = [shape(mine.shape, BF16), shape(before.shape, F32), shape(border.shape, F32)]
    return call(functools.partial(merge_kernel, j), f"merge{j}", out, unread=(6,))(
        mine, theirs, before, border, params, tables, after
    )


def gate_kernel(
    mine,
    row1,
    row2,
    row3,
    before_in,
    border_in,
    local,
    gate,
    carry,
    reach,
    params,
    tables,
    out,
    before,
    starts,
):
    span, channels = local.shape
    steps = span // SEGMENTS
    y, z = place_of()
    rows = [unpack(m) for m in (mine, row1, row2, row3)]
    total = before_in[...]
    for s in range(3):
        u0, u1 = gated_start(params, rows[s][1], rows[s + 1][1])
        total = total + tables[OVER_Y + s] * rows[s + 1][0]
        total = total + tables[OVER_Y + 3 + s] * (tables[DECAY] * u0 + u1)
    border = jnp.where((z == 0) & (y >= 1), rows[1][1], border_in[...])
    u = [None, None]
    p = lambda i: params[i : i + 1, :]
    e = lambda i: border[4 + i : 5 + i]
    u[0] = (p(FIRST) + p(1) * e(1) + p(2) * e(0)) * (p(FIRST + 2) + p(4) * e(3) + p(5) * e(2))
    u[1] = (p(FIRST + 1) + p(2) * e(1)) * (p(FIRST + 3) + p(5) * e(3))
    before[...] = total + tables[GROWTH] * u[0] + tables[GROWTH + 1] * u[1]
    starts[0:1, :] = p(SKIP) * u[0] - p(GROWN) * u[1]
    starts[1:2, :] = p(SKIP) * u[1]
    starts[2:3, :] = p(7) * e(5) + p(8) * e(4)
    starts[3:4, :] = p(8) * e(5)
    segment = segment_index()

    def group(lanes):
        decay, term = [], []
        for r in range(ORDER):
            here = slice(r * SEGMENTS, (r + 1) * SEGMENTS)
            term.append(carry[here, lanes] + reach[here, lanes] * before[r : r + 1, lanes])
            decay.append(tables[DECAY, r : r + 1, lanes])
        for pair in range(steps // 2):
            both = []
            for a in (2 * pair, 2 * pair + 1):
                here = slice(a * SEGMENTS, (a + 1) * SEGMENTS)
                parts = [local[here, lanes], None, None, None]
                times = gate[here, lanes]
                if a < 2:
                    first = segment == 0
                    parts[0] = parts[0] + jnp.where(first, starts[a : a + 1, lanes], 0.0)
                    times = times + jnp.where(first, starts[2 + a : 3 + a, lanes], 0.0)
                for r in range(ORDER):
                    parts[r % 4] = term[r] if parts[r % 4] is None else parts[r % 4] + term[r]
                    term[r] = term[r] * decay[r]
                both.append(((parts[0] + parts[1]) + (parts[2] + parts[3])) * times)
            here = slice(pair * 2 * SEGMENTS, (pair + 1) * 2 * SEGMENTS)
            out[here, lanes] = jnp.concatenate(both, axis=0).astype(BF16)

    by_group(channels, group)


def gate_all(messages, before, border, local, gate, carry, reach, params, tables):
    out = jax.ShapeDtypeStruct(local.shape, BF16)
    scratch = [pltpu.VMEM(before.shape, F32), pltpu.VMEM((8, before.shape[1]), F32)]
    return call(gate_kernel, "gated", out, scratch)(
        *messages, before, border, local, gate, carry, reach, params, tables
    )


def blocks_kernel(weight_hbm, after, out, sems):
    columns = out.shape[1] // sems.shape[0]
    me = lax.axis_index("ch")
    copies = []
    for k in range(sems.shape[0]):
        at = pl.ds(pl.multiple_of((me ^ (2 * k)) * columns, columns), columns)
        copies.append(
            pltpu.make_async_copy(
                weight_hbm.at[:, at], out.at[:, k * columns : (k + 1) * columns], sems.at[k]
            )
        )
    for c in copies:
        c.start()
    for c in copies:
        c.wait()


def weight_blocks(weight, after):
    channels, width = weight.shape
    chips = lax.axis_size("ch") // 2
    out = jax.ShapeDtypeStruct((channels, width // 2), BF16)
    scratch = [pltpu.SemaphoreType.DMA((chips,))]
    return call(blocks_kernel, "weight_blocks", out, scratch, outside=(0,), unread=(1,))(weight, after)


def project(mine, other, weight, far, k, dtype):
    columns = far.shape[1] // lax.axis_size("ch")

    def kernel(mine_ref, other_ref, weight_ref, far_ref, out_ref):
        block = lax.axis_index("ch") ^ (2 * k)
        at = pl.ds(pl.multiple_of(block * columns, columns), columns)
        near = weight_ref[:, k * columns : (k + 1) * columns]
        total = jnp.dot(mine_ref[...], near, preferred_element_type=F32)
        total = total + jnp.dot(other_ref[...], far_ref[:, at], preferred_element_type=F32)
        out_ref[...] = total.astype(out_ref.dtype)

    out = jax.ShapeDtypeStruct((mine.shape[0], columns), dtype)
    return call(kernel, f"project{k}", out)(mine, other, weight, far)


def finish_kernel(own, a, b, c, out):
    total = own[...] + a[...].astype(F32)
    total = total + (b[...].astype(F32) + c[...].astype(F32))
    out[...] = lax.dot_general(
        total.astype(BF16), order_matrix(total.shape[0]), TN, preferred_element_type=F32
    ).astype(BF16)


def finish(own, received):
    span, columns = own.shape
    out = jax.ShapeDtypeStruct((columns, span), BF16)
    return call(finish_kernel, "finish", out, held=False)(own, *received)


def per_device(
    query_in, key_in, value_in, short_taps, modal_residue, mode_damping_speed, skip_gain, out_weight
):
    channels = query_in.shape[0]
    n_ctx, n_ch = lax.axis_size("ctx"), lax.axis_size("ch")
    sibling = [(i, i ^ 1) for i in range(n_ch)]
    far = lax.ppermute(out_weight, "ch", sibling)

    message, gated, params, tables = states(
        key_in,
        value_in,
        query_in,
        jnp.transpose(short_taps, (0, 2, 1)),
        mode_damping_speed.T,
        modal_residue.T,
        skip_gain[None, :],
    )
    before = jnp.zeros((ORDER, channels), F32)
    border = jnp.zeros((16, channels), F32)
    for j, (_, by) in enumerate(STEPS):
        theirs = lax.ppermute(message, "ctx", [(i, i ^ by) for i in range(n_ctx)])
        if j == 0:
            local, gate, carry, reach = local_scan(gated, query_in, params, tables, message)
            done = local
        if j == 1:
            done = weight = weight_blocks(out_weight, message)
        message, before, border = merge(j, message, theirs, before, border, params, tables, done)
    messages = [message]
    for s in range(1, n_ctx // ROW):
        pairs = [(i, i + s * ROW) for i in range(n_ctx - s * ROW)]
        messages.append(lax.ppermute(message, "ctx", pairs))

    own = gate_all(messages, before, border, local, gate, carry, reach, params, tables)
    other = lax.ppermute(own, "ch", sibling)
    received = []
    for k in (2, 1, 3):
        part = project(own, other, weight, far, k, BF16)
        received.append(lax.ppermute(part, "ch", [(i, i ^ (2 * k)) for i in range(n_ch)]))
    kept = project(own, other, weight, far, 0, F32)
    return finish(kept, received)


def solution(mesh):
    placed = (
        P("ch", "ctx"),
        P("ch", "ctx"),
        P("ch", "ctx"),
        P(None, "ch", None),
        P("ch", None),
        P("ch", None),
        P("ch"),
        P("ch", None),
    )
    return jax.shard_map(
        per_device, mesh=mesh, in_specs=placed, out_specs=P("ch", "ctx"), check_vma=False
    )
```

profile of v0, /device:TPU:32, one launch (start us, length us, event | category | flops | bytes accessed | tf_op | source)
XLA Modules:
  0.0 50.4 jit_solution(12211780289812623264)
XLA Ops:
  0.0 0.0 collective-permute-start.7
  0.0 2.5 %states.1 = (bf16[48,512]{1,0:T(8,128)(2,1)S(1)}, f32[256,512]{1,0:T(8,128)S(1)}, f32[16,512]{1,0:T(8,128)S(1)}, f32[28,16,512]{2,1,0:T(8,128)S(1)}) custom-call(bf16[512,256]{1,0:T(8,128)(2,1)} %key_hbm.1, bf16[512,256]{1,0:T(8,128)(2,1)} %value_hbm.1, bf16[512,256]{1,0:T(8,128)(2,1)} %query_hbm.3, f32[3,3,512]{2,1,0:T(4,128)} %bitcast.6, ...), custom_call_target="tpu_custom_call" | custom-call | tf_op jit(solution)/shard_map/states/pallas_call | solution.py:36
  2.6 1.9 %collective-permute-start = (bf16[48,512]{1,0:T(8,128)(2,1)S(1)}, bf16[48,512]{1,0:T(8,128)(2,1)S(1)}, u32[]{:S(2)}, u32[]{:S(2)}) collective-permute-start(bf16[48,512]{1,0:T(8,128)(2,1)S(1)} %get-tuple-element.22.after.mine), channel_id=1, source_target_pairs={{0,8},{8,0},{16,24},{24,16},{32,40},{40,32},{48,56},{56,48},{64,72... | collective-permute-start | bytes 147464 | tf_op jit(solution)/shard_map/ppermute | solution.py:508
  4.5 2.7 %local_scan.1 = (f32[256,512]{1,0:T(8,128)S(1)}, f32[256,512]{1,0:T(8,128)S(1)}, f32[128,512]{1,0:T(8,128)S(1)}, f32[128,512]{1,0:T(8,128)S(1)}) custom-call(f32[256,512]{1,0:T(8,128)S(1)} %get-tuple-element.25.gated, bf16[512,256]{1,0:T(8,128)(2,1)} %query_hbm.3, f32[16,512]{1,0:T(8,128)S(1)} %get-tuple-element.23.params, ...), custom_call_target="tpu_custom_call" | custom-call | tf_op jit(solution)/shard_map/local_scan/pallas_call | solution.py:36
  7.2 0.0 collective-permute-done.theirs
  7.2 3.0 %collective-permute-start.1 = (bf16[48,512]{1,0:T(8,128)(2,1)S(1)}, bf16[48,512]{1,0:T(8,128)(2,1)S(1)}, u32[]{:S(2)}, u32[]{:S(2)}) collective-permute-start(bf16[48,512]{1,0:T(8,128)(2,1)S(1)} %get-tuple-element.27.after.mine), channel_id=1, source_target_pairs={{0,16},{8,24},{16,0},{24,8},{32,48},{40,56},{48,32},{56,40},{64,80... | collective-permute-start | bytes 147464 | tf_op jit(solution)/shard_map/ppermute | solution.py:508
  10.2 1.6 %weight_blocks.1.after.weight_ref = bf16[512,2048]{1,0:T(8,128)(2,1)S(1)} custom-call(bf16[512,4096]{1,0:T(8,128)(2,1)} %weight_hbm.1, bf16[48,512]{1,0:T(8,128)(2,1)S(1)} %get-tuple-element.27.after.mine), custom_call_target="tpu_custom_call" | custom-call | tf_op jit(solution)/shard_map/weight_blocks/pallas_call | solution.py:36
  11.8 0.7 %collective-permute-done.1.theirs = bf16[48,512]{1,0:T(8,128)(2,1)S(1)} collective-permute-done((bf16[48,512]{1,0:T(8,128)(2,1)S(1)}, bf16[48,512]{1,0:T(8,128)(2,1)S(1)}, u32[]{:S(2)}, u32[]{:S(2)}) %collective-permute-start.1) | collective-permute-done | bytes 49184 | tf_op jit(solution)/shard_map/ppermute | solution.py:508
  12.5 5.5 %collective-permute-start.2 = (bf16[48,512]{1,0:T(8,128)(2,1)S(1)}, bf16[48,512]{1,0:T(8,128)(2,1)S(1)}, u32[]{:S(2)}, u32[]{:S(2)}) collective-permute-start(bf16[48,512]{1,0:T(8,128)(2,1)S(1)} %get-tuple-element.30.mine), channel_id=1, source_target_pairs={{0,56},{8,48},{16,40},{24,32},{32,24},{40,16},{48,8},{56,0},{64,12... | collective-permute-start | bytes 147464 | tf_op jit(solution)/shard_map/ppermute | solution.py:508
  18.0 2.1 %collective-permute-done.2.theirs = bf16[48,512]{1,0:T(8,128)(2,1)S(1)} collective-permute-done((bf16[48,512]{1,0:T(8,128)(2,1)S(1)}, bf16[48,512]{1,0:T(8,128)(2,1)S(1)}, u32[]{:S(2)}, u32[]{:S(2)}) %collective-permute-start.2) | collective-permute-done | bytes 49184 | tf_op jit(solution)/shard_map/ppermute | solution.py:508
  20.1 4.9 %collective-permute-start.5 = (bf16[48,512]{1,0:T(8,128)(2,1)S(1)}, bf16[48,512]{1,0:T(8,128)(2,1)S(1)}, u32[]{:S(2)}, u32[]{:S(2)}) collective-permute-start(bf16[48,512]{1,0:T(8,128)(2,1)S(1)} %get-tuple-element.33.mine), channel_id=1, source_target_pairs={{0,192},{8,200},{16,208},{24,216},{32,224},{40,232},{48,240},{56,2... | collective-permute-start | bytes 147464 | tf_op jit(solution)/shard_map/ppermute | solution.py:518
  25.0 1.3 %collective-permute-start.4 = (bf16[48,512]{1,0:T(8,128)(2,1)S(1)}, bf16[48,512]{1,0:T(8,128)(2,1)S(1)}, u32[]{:S(2)}, u32[]{:S(2)}) collective-permute-start(bf16[48,512]{1,0:T(8,128)(2,1)S(1)} %get-tuple-element.33.mine), channel_id=1, source_target_pairs={{0,128},{8,136},{16,144},{24,152},{32,160},{40,168},{48,176},{56,1... | collective-permute-start | bytes 147464 | tf_op jit(solution)/shard_map/ppermute | solution.py:518
  26.3 2.8 %collective-permute-start.3 = (bf16[48,512]{1,0:T(8,128)(2,1)S(1)}, bf16[48,512]{1,0:T(8,128)(2,1)S(1)}, u32[]{:S(2)}, u32[]{:S(2)}) collective-permute-start(bf16[48,512]{1,0:T(8,128)(2,1)S(1)} %get-tuple-element.33.mine), channel_id=1, source_target_pairs={{0,64},{8,72},{16,80},{24,88},{32,96},{40,104},{48,112},{56,120},{... | collective-permute-start | bytes 147464 | tf_op jit(solution)/shard_map/ppermute | solution.py:518
  29.1 0.0 collective-permute-done.5.row3
  29.1 0.0 collective-permute-done.4.row2
  29.1 1.7 %collective-permute-done.3.row1 = bf16[48,512]{1,0:T(8,128)(2,1)S(1)} collective-permute-done((bf16[48,512]{1,0:T(8,128)(2,1)S(1)}, bf16[48,512]{1,0:T(8,128)(2,1)S(1)}, u32[]{:S(2)}, u32[]{:S(2)}) %collective-permute-start.3) | collective-permute-done | bytes 49184 | tf_op jit(solution)/shard_map/ppermute | solution.py:518
  30.8 0.7 %gated.1.mine_ref = bf16[256,512]{1,0:T(8,128)(2,1)S(1)} custom-call(bf16[48,512]{1,0:T(8,128)(2,1)S(1)} %get-tuple-element.33.mine, bf16[48,512]{1,0:T(8,128)(2,1)S(1)} %collective-permute-done.3.row1, bf16[48,512]{1,0:T(8,128)(2,1)S(1)} %collective-permute-done.4.row2, bf16[48,512]{1,0:T(8,128)(2,1)S(1)} %collective-permute-done.5.row3, ...), custom_call_target="tpu_custom_call" | custom-call | tf_op jit(solution)/shard_map/gated/pallas_call | solution.py:36
  31.6 0.1 collective-permute-start.6
  31.7 1.5 %collective-permute-done.6.other_ref = bf16[256,512]{1,0:T(8,128)(2,1)S(1)} collective-permute-done((bf16[256,512]{1,0:T(8,128)(2,1)S(1)}, bf16[256,512]{1,0:T(8,128)(2,1)S(1)}, u32[]{:S(2)}, u32[]{:S(2)}) %collective-permute-start.6) | collective-permute-done | bytes 262176 | tf_op jit(solution)/shard_map/ppermute | solution.py:521
  33.2 0.0 collective-permute-done.7.far_ref
  33.2 0.4 project2.1
  33.6 3.1 %collective-permute-start.8 = (bf16[256,512]{1,0:T(8,128)(2,1)S(1)}, bf16[256,512]{1,0:T(8,128)(2,1)S(1)}, u32[]{:S(2)}, u32[]{:S(2)}) collective-permute-start(bf16[256,512]{1,0:T(8,128)(2,1)S(1)} %project2.1), channel_id=1, source_target_pairs={{0,4},{1,5},{2,6},{3,7},{4,0},{5,1},{6,2},{7,3},{8,12},{9,13},{10,... | collective-permute-start | bytes 786440 | tf_op jit(solution)/shard_map/ppermute | solution.py:525
  36.8 0.4 project1.1
  37.2 0.7 %collective-permute-start.9 = (bf16[256,512]{1,0:T(8,128)(2,1)S(1)}, bf16[256,512]{1,0:T(8,128)(2,1)S(1)}, u32[]{:S(2)}, u32[]{:S(2)}) collective-permute-start(bf16[256,512]{1,0:T(8,128)(2,1)S(1)} %project1.1), channel_id=1, source_target_pairs={{0,2},{1,3},{2,0},{3,1},{4,6},{5,7},{6,4},{7,5},{8,10},{9,11},{10,... | collective-permute-start | bytes 786440 | tf_op jit(solution)/shard_map/ppermute | solution.py:525
  37.9 0.4 project3.1
  38.3 0.7 %collective-permute-start.10 = (bf16[256,512]{1,0:T(8,128)(2,1)S(1)}, bf16[256,512]{1,0:T(8,128)(2,1)S(1)}, u32[]{:S(2)}, u32[]{:S(2)}) collective-permute-start(bf16[256,512]{1,0:T(8,128)(2,1)S(1)} %project3.1), channel_id=1, source_target_pairs={{0,6},{1,7},{2,4},{3,5},{4,2},{5,3},{6,0},{7,1},{8,14},{9,15},{10,... | collective-permute-start | bytes 786440 | tf_op jit(solution)/shard_map/ppermute | solution.py:525
  39.0 0.4 project0.1.own
  39.4 5.0 %collective-permute-done.8.a = bf16[256,512]{1,0:T(8,128)(2,1)S(1)} collective-permute-done((bf16[256,512]{1,0:T(8,128)(2,1)S(1)}, bf16[256,512]{1,0:T(8,128)(2,1)S(1)}, u32[]{:S(2)}, u32[]{:S(2)}) %collective-permute-start.8) | collective-permute-done | bytes 262176 | tf_op jit(solution)/shard_map/ppermute | solution.py:525
  44.4 4.9 %collective-permute-done.9.b = bf16[256,512]{1,0:T(8,128)(2,1)S(1)} collective-permute-done((bf16[256,512]{1,0:T(8,128)(2,1)S(1)}, bf16[256,512]{1,0:T(8,128)(2,1)S(1)}, u32[]{:S(2)}, u32[]{:S(2)}) %collective-permute-start.9) | collective-permute-done | bytes 262176 | tf_op jit(solution)/shard_map/ppermute | solution.py:525
  49.3 0.0 collective-permute-done.10.c
  49.3 1.1 %finish.1 = bf16[512,256]{1,0:T(8,128)(2,1)} custom-call(f32[256,512]{1,0:T(8,128)S(1)} %project0.1.own, bf16[256,512]{1,0:T(8,128)(2,1)S(1)} %collective-permute-done.8.a, bf16[256,512]{1,0:T(8,128)(2,1)S(1)} %collective-permute-done.9.b, bf16[256,512]{1,0:T(8,128)(2,1)S(1)} %collective-permute-done.10.c), custom_call_target="tpu_custom_call" | custom-call | tf_op jit(solution)/shard_map/finish/pallas_call | solution.py:36
  (4 shorter events, 0.1 us)
Async XLA Ops:
  0.0 33.2 %collective-permute-start.7 = (bf16[512,4096]{1,0:T(8,128)(2,1)}, bf16[512,4096]{1,0:T(8,128)(2,1)S(1)}, u32[]{:S(2)}, u32[]{:S(2)}) collective-permute-start(bf16[512,4096]{1,0:T(8,128)(2,1)} %weight_hbm.1), channel_id=1, source_target_pairs={{0,1},{1,0},{2,3},{3,2},{4,5},{5,4},{6,7},{7,6},{8,9},{9,8},{10,11... | collective-permute-start | bytes 12582920 | tf_op jit(solution)/shard_map/ppermute | solution.py:494
  2.6 4.6 %collective-permute-start = (bf16[48,512]{1,0:T(8,128)(2,1)S(1)}, bf16[48,512]{1,0:T(8,128)(2,1)S(1)}, u32[]{:S(2)}, u32[]{:S(2)}) collective-permute-start(bf16[48,512]{1,0:T(8,128)(2,1)S(1)} %get-tuple-element.22.after.mine), channel_id=1, source_target_pairs={{0,8},{8,0},{16,24},{24,16},{32,40},{40,32},{48,56},{56,48},{64,72... | collective-permute-start | bytes 147464 | tf_op jit(solution)/shard_map/ppermute | solution.py:508
  7.2 5.2 %collective-permute-start.1 = (bf16[48,512]{1,0:T(8,128)(2,1)S(1)}, bf16[48,512]{1,0:T(8,128)(2,1)S(1)}, u32[]{:S(2)}, u32[]{:S(2)}) collective-permute-start(bf16[48,512]{1,0:T(8,128)(2,1)S(1)} %get-tuple-element.27.after.mine), channel_id=1, source_target_pairs={{0,16},{8,24},{16,0},{24,8},{32,48},{40,56},{48,32},{56,40},{64,80... | collective-permute-start | bytes 147464 | tf_op jit(solution)/shard_map/ppermute | solution.py:508
  12.5 7.6 %collective-permute-start.2 = (bf16[48,512]{1,0:T(8,128)(2,1)S(1)}, bf16[48,512]{1,0:T(8,128)(2,1)S(1)}, u32[]{:S(2)}, u32[]{:S(2)}) collective-permute-start(bf16[48,512]{1,0:T(8,128)(2,1)S(1)} %get-tuple-element.30.mine), channel_id=1, source_target_pairs={{0,56},{8,48},{16,40},{24,32},{32,24},{40,16},{48,8},{56,0},{64,12... | collective-permute-start | bytes 147464 | tf_op jit(solution)/shard_map/ppermute | solution.py:508
  20.1 9.0 %collective-permute-start.5 = (bf16[48,512]{1,0:T(8,128)(2,1)S(1)}, bf16[48,512]{1,0:T(8,128)(2,1)S(1)}, u32[]{:S(2)}, u32[]{:S(2)}) collective-permute-start(bf16[48,512]{1,0:T(8,128)(2,1)S(1)} %get-tuple-element.33.mine), channel_id=1, source_target_pairs={{0,192},{8,200},{16,208},{24,216},{32,224},{40,232},{48,240},{56,2... | collective-permute-start | bytes 147464 | tf_op jit(solution)/shard_map/ppermute | solution.py:518
  25.0 4.1 %collective-permute-start.4 = (bf16[48,512]{1,0:T(8,128)(2,1)S(1)}, bf16[48,512]{1,0:T(8,128)(2,1)S(1)}, u32[]{:S(2)}, u32[]{:S(2)}) collective-permute-start(bf16[48,512]{1,0:T(8,128)(2,1)S(1)} %get-tuple-element.33.mine), channel_id=1, source_target_pairs={{0,128},{8,136},{16,144},{24,152},{32,160},{40,168},{48,176},{56,1... | collective-permute-start | bytes 147464 | tf_op jit(solution)/shard_map/ppermute | solution.py:518
  26.3 4.5 %collective-permute-start.3 = (bf16[48,512]{1,0:T(8,128)(2,1)S(1)}, bf16[48,512]{1,0:T(8,128)(2,1)S(1)}, u32[]{:S(2)}, u32[]{:S(2)}) collective-permute-start(bf16[48,512]{1,0:T(8,128)(2,1)S(1)} %get-tuple-element.33.mine), channel_id=1, source_target_pairs={{0,64},{8,72},{16,80},{24,88},{32,96},{40,104},{48,112},{56,120},{... | collective-permute-start | bytes 147464 | tf_op jit(solution)/shard_map/ppermute | solution.py:518
  31.6 1.6 %collective-permute-start.6 = (bf16[256,512]{1,0:T(8,128)(2,1)S(1)}, bf16[256,512]{1,0:T(8,128)(2,1)S(1)}, u32[]{:S(2)}, u32[]{:S(2)}) collective-permute-start(bf16[256,512]{1,0:T(8,128)(2,1)S(1)} %gated.1.mine_ref), channel_id=1, source_target_pairs={{0,1},{1,0},{2,3},{3,2},{4,5},{5,4},{6,7},{7,6},{8,9},{9,8},{10,11... | collective-permute-start | bytes 786440 | tf_op jit(solution)/shard_map/ppermute | solution.py:521
  33.6 10.7 %collective-permute-start.8 = (bf16[256,512]{1,0:T(8,128)(2,1)S(1)}, bf16[256,512]{1,0:T(8,128)(2,1)S(1)}, u32[]{:S(2)}, u32[]{:S(2)}) collective-permute-start(bf16[256,512]{1,0:T(8,128)(2,1)S(1)} %project2.1), channel_id=1, source_target_pairs={{0,4},{1,5},{2,6},{3,7},{4,0},{5,1},{6,2},{7,3},{8,12},{9,13},{10,... | collective-permute-start | bytes 786440 | tf_op jit(solution)/shard_map/ppermute | solution.py:525
  37.2 12.1 %collective-permute-start.9 = (bf16[256,512]{1,0:T(8,128)(2,1)S(1)}, bf16[256,512]{1,0:T(8,128)(2,1)S(1)}, u32[]{:S(2)}, u32[]{:S(2)}) collective-permute-start(bf16[256,512]{1,0:T(8,128)(2,1)S(1)} %project1.1), channel_id=1, source_target_pairs={{0,2},{1,3},{2,0},{3,1},{4,6},{5,7},{6,4},{7,5},{8,10},{9,11},{10,... | collective-permute-start | bytes 786440 | tf_op jit(solution)/shard_map/ppermute | solution.py:525
  38.3 11.0 %collective-permute-start.10 = (bf16[256,512]{1,0:T(8,128)(2,1)S(1)}, bf16[256,512]{1,0:T(8,128)(2,1)S(1)}, u32[]{:S(2)}, u32[]{:S(2)}) collective-permute-start(bf16[256,512]{1,0:T(8,128)(2,1)S(1)} %project3.1), channel_id=1, source_target_pairs={{0,6},{1,7},{2,4},{3,5},{4,2},{5,3},{6,0},{7,1},{8,14},{9,15},{10,... | collective-permute-start | bytes 786440 | tf_op jit(solution)/shard_map/ppermute | solution.py:525
where the time goes:
time: 51.4 us; the launch traced here: 50.4 us
  starting transfers between devices  23.9 us (46%)
  waiting for transfers between devices  15.9 us (31%)
  Pallas kernels  10.4 us (20%)
    pallas_call x12, Pallas kernels, run(): pl.pallas_call(kernel, in_specs=[pl.BlockSpec(memory_space=space) for spa...  10.4 us
    ppermute x3, starting transfers between devices, per_device(): theirs = lax.ppermute(message, 'ctx', [(i, i ^ by) for i in range(n_ctx)])  10.4 us
    ppermute x3, waiting for transfers between devices, per_device(): lax.ppermute(part, 'ch', [(i, i ^ 2 * k) for i in range(n_ch)])  9.92 us
    ppermute x3, starting transfers between devices, per_device(): messages.append(lax.ppermute(message, 'ctx', pairs))  8.98 us
    ppermute x3, starting transfers between devices, per_device(): lax.ppermute(part, 'ch', [(i, i ^ 2 * k) for i in range(n_ch)])  4.45 us
    ppermute x3, waiting for transfers between devices, per_device(): theirs = lax.ppermute(message, 'ctx', [(i, i ^ by) for i in range(n_ctx)])  2.74 us
    ppermute x3, waiting for transfers between devices, per_device(): messages.append(lax.ppermute(message, 'ctx', pairs))  1.72 us
    ppermute x1, waiting for transfers between devices, per_device(): other = lax.ppermute(own, 'ch', sibling)  1.52 us
  transfers between devices with their start and end apart: 11, of which 6 were waited for; matrix products, arithmetic and copies ran while one was open for 0% of the time, Pallas kernels for 18%

commit v1 on v0

--- a/solution.py
+++ b/solution.py
@@ -1,5 +1,3 @@
-import functools
-
 import jax
 import jax.numpy as jnp
 from jax import lax
@@ -17,11 +15,12 @@
 NT = (((1,), (1,)), ((), ()))
 TN = (((0,), (0,)), ((), ()))
 
-STEPS = ((1, 1), (2, 2), (4, 7))
-DECAY, FADE, WEIGHT, GROWTH, OVER_Z, OVER_Y = 0, 1, 4, 5, 7, 22
-TABLES = 28
+FOUR, PAIR = 4, 7
+DECAY, FADE, WEIGHT, GROWTH = 0, 1, 4, 5
+ALL, ALL_SEAM, AHEAD, AHEAD_SEAM, OVER_PAIR, OVER_Y = 7, 10, 13, 16, 18, 23
+TABLES = 29
 SKIP, GROWN, FIRST = 9, 10, 11
-EDGES = 32
+EDGES = 16
 
 
 def call(kernel, name, out, scratch=(), held=True, outside=(), unread=()):
@@ -85,17 +84,24 @@
     tables[WEIGHT] = residue * jnp.sqrt(damping)
     tables[GROWTH] = fade(-1.0)
     tables[GROWTH + 1] = fade(-2.0)
-    for j, (size, _) in enumerate(STEPS):
-        at = OVER_Z + 5 * j
-        older = (z & size) != 0
-        ahead = (z & (size - 1)) * span
-        whole = fade(float(size * span))
-        tables[at] = only(older, fade(ahead.astype(F32)))
-        seen = jnp.maximum(ahead - 2, 0).astype(F32)
-        tables[at + 1] = only(older & (ahead > 0), fade(seen))
-        tables[at + 2] = jnp.where(older, whole, 1.0)
-        tables[at + 3] = jnp.where(older, 1.0, whole)
-        tables[at + 4] = fade(float(size * span - 2))
+    place = z & (FOUR - 1)
+    for q in range(3):
+        tables[ALL + q] = fade(float((3 - q) * span))
+        tables[ALL_SEAM + q] = fade(float((3 - q) * span - 2))
+        ahead = jnp.maximum(place - 1 - q, 0) * span
+        tables[AHEAD + q] = only(q < place, fade(ahead.astype(F32)))
+    for q in range(2):
+        seen = jnp.maximum((place - 1 - q) * span - 2, 0)
+        tables[AHEAD_SEAM + q] = only(q + 1 < place, fade(seen.astype(F32)))
+    older = (z & FOUR) != 0
+    ahead = place * span
+    whole = fade(float(FOUR * span))
+    tables[OVER_PAIR] = only(older, fade(ahead.astype(F32)))
+    seen = jnp.maximum(ahead - 2, 0).astype(F32)
+    tables[OVER_PAIR + 1] = only(older & (ahead > 0), fade(seen))
+    tables[OVER_PAIR + 2] = jnp.where(older, whole, 1.0)
+    tables[OVER_PAIR + 3] = jnp.where(older, 1.0, whole)
+    tables[OVER_PAIR + 4] = fade(float(FOUR * span - 2))
     for s in range(3):
         ahead = (ROW * s + z) * span
         tables[OVER_Y + s] = only(y >= s + 1, fade(ahead.astype(F32)))
@@ -195,9 +201,11 @@
             state[r : r + 1, lanes] = total[SEGMENTS - 1 :]
 
     by_group(channels, group)
-    high = state[...].astype(BF16)
-    message[0:ORDER, :] = high
-    message[ORDER:EDGES, :] = (state[...] - high.astype(F32)).astype(BF16)
+    at = lambda i: params[FIRST + i : FIRST + i + 1, :]
+    start_fade = jnp.exp(-damping[...] * float(span - 2))
+    start = start_fade * (tables[DECAY] * (at(0) * at(2)) + at(1) * at(3))
+    total = state[...] + jnp.where(lax.axis_index("ctx") == 0, start, 0.0)
+    message[0:ORDER, :] = total.astype(BF16)
     edges[...] = jnp.zeros_like(edges)
     for s in range(2):
         edges[2 * s : 2 * s + 1, :] = streams[s, 0:1, :]
@@ -309,8 +317,7 @@
 
 
 def unpack(message):
-    state = message[0:ORDER, :].astype(F32) + message[ORDER:EDGES, :].astype(F32)
-    return state, message[EDGES:, :].astype(F32)
+    return message[0:ORDER, :].astype(F32), message[EDGES:, :].astype(F32)
 
 
 def gated_start(params, new, old):
@@ -326,14 +333,59 @@
     return k0 * v0, k1 * v1
 
 
-def merge_kernel(
-    j, mine, theirs, before, border, params, tables, after, message, before_out, border_out
+def in_order(place, mine, swapped):
+    one, two, three = swapped
+    pick = lambda q, m, a, b, c: jnp.where(
+        place == q, m, jnp.where((place ^ 1) == q, a, jnp.where((place ^ 2) == q, b, c))
+    )
+    return [
+        tuple(pick(q, m, a, b, c) for m, a, b, c in zip(mine, one, two, three)) for q in range(4)
+    ]
+
+
+def send(message, state, first, last):
+    message[0:ORDER, :] = state.astype(BF16)
+    row = lax.broadcasted_iota(jnp.int32, first.shape, 0)
+    message[EDGES:, :] = jnp.where(row < 4, first, last).astype(BF16)
+
+
+def merge_four_kernel(mine, three, two, one, params, tables, after, message, before, border):
+    _, z = place_of()
+    place = z & (FOUR - 1)
+    blocks = in_order(place, unpack(mine), [unpack(m) for m in (one, two, three)])
+    total, ahead = blocks[3][0], jnp.zeros_like(before)
+    for q in range(3):
+        total = total + tables[ALL + q] * blocks[q][0]
+        ahead = ahead + tables[AHEAD + q] * blocks[q][0]
+        u0, u1 = gated_start(params, blocks[q + 1][1], blocks[q][1])
+        seam = tables[DECAY] * u0 + u1
+        total = total + tables[ALL_SEAM + q] * seam
+        if q < 2:
+            ahead = ahead + tables[AHEAD_SEAM + q] * seam
+    send(message, total, blocks[0][1], blocks[3][1])
+    before[...] = ahead
+    last = jnp.zeros_like(border)
+    for q in range(3):
+        last = jnp.where(place == q + 1, blocks[q][1], last)
+    border[...] = last
+
+
+def merge_four(mine, swapped, params, tables, after):
+    channels = mine.shape[1]
+    shape = jax.ShapeDtypeStruct
+    out = [shape(mine.shape, BF16), shape((ORDER, channels), F32), shape((16, channels), F32)]
+    return call(merge_four_kernel, "merge_four", out, unread=(6,))(
+        mine, *swapped, params, tables, after
+    )
+
+
+def merge_pair_kernel(
+    mine, theirs, before, border, params, tables, after, message, before_out, border_out
 ):
-    size = STEPS[j][0]
-    at = OVER_Z + 5 * j
+    at = OVER_PAIR
     _, z = place_of()
-    older = (z & size) != 0
-    first = (z & (size - 1)) == 0
+    older = (z & FOUR) != 0
+    first = (z & (FOUR - 1)) == 0
     my_state, my_edges = unpack(mine)
     state, edges = unpack(theirs)
     new = jnp.where(older, my_edges, edges)
@@ -341,28 +393,24 @@
     u0, u1 = gated_start(params, new, old)
     seam = tables[DECAY] * u0 + u1
     total = tables[at + 2] * state + tables[at + 3] * my_state + tables[at + 4] * seam
-    high = total.astype(BF16)
-    message[0:ORDER, :] = high
-    message[ORDER:EDGES, :] = (total - high.astype(F32)).astype(BF16)
-    row = lax.broadcasted_iota(jnp.int32, my_edges.shape, 0)
-    message[EDGES:, :] = jnp.where(row < 4, old, new).astype(BF16)
+    send(message, total, old, new)
     before_out[...] = before[...] + tables[at] * state + tables[at + 1] * seam
     border_out[...] = jnp.where(older & first, edges, border[...])
 
 
-def merge(j, mine, theirs, before, border, params, tables, after):
+def merge_pair(mine, theirs, before, border, params, tables, after):
     shape = jax.ShapeDtypeStruct
     out = [shape(mine.shape, BF16), shape(before.shape, F32), shape(border.shape, F32)]
-    return call(functools.partial(merge_kernel, j), f"merge{j}", out, unread=(6,))(
+    return call(merge_pair_kernel, "merge_pair", out, unread=(6,))(
         mine, theirs, before, border, params, tables, after
     )
 
 
 def gate_kernel(
     mine,
+    row3,
+    row2,
     row1,
-    row2,
-    row3,
     before_in,
     border_in,
     local,
@@ -378,7 +426,11 @@
     span, channels = local.shape
     steps = span // SEGMENTS
     y, z = place_of()
-    rows = [unpack(m) for m in (mine, row1, row2, row3)]
+    lying = in_order(y, unpack(mine), [unpack(m) for m in (row1, row2, row3)])
+    rows = [unpack(mine)]
+    for s in range(1, 4):
+        pick = lambda a, b, c: jnp.where(y - s == 0, a, jnp.where(y - s == 1, b, c))
+        rows.append(tuple(pick(a, b, c) for a, b, c in zip(*lying[:3])))
     total = before_in[...]
     for s in range(3):
         u0, u1 = gated_start(params, rows[s][1], rows[s + 1][1])
@@ -456,30 +508,50 @@
     return call(blocks_kernel, "weight_blocks", out, scratch, outside=(0,), unread=(1,))(weight, after)
 
 
-def project(mine, other, weight, far, k, dtype):
+def project(mine, other, weight, far, name, wanted, dtype):
+    span = mine.shape[0]
     columns = far.shape[1] // lax.axis_size("ch")
 
-    def kernel(mine_ref, other_ref, weight_ref, far_ref, out_ref):
-        block = lax.axis_index("ch") ^ (2 * k)
-        at = pl.ds(pl.multiple_of(block * columns, columns), columns)
-        near = weight_ref[:, k * columns : (k + 1) * columns]
-        total = jnp.dot(mine_ref[...], near, preferred_element_type=F32)
-        total = total + jnp.dot(other_ref[...], far_ref[:, at], preferred_element_type=F32)
-        out_ref[...] = total.astype(out_ref.dtype)
-
-    out = jax.ShapeDtypeStruct((mine.shape[0], columns), dtype)
-    return call(kernel, f"project{k}", out)(mine, other, weight, far)
-
-
-def finish_kernel(own, a, b, c, out):
-    total = own[...] + a[...].astype(F32)
-    total = total + (b[...].astype(F32) + c[...].astype(F32))
+    def kernel(mine_ref, other_ref, weight_ref, far_ref, *out_refs):
+        for out_ref, (k, part) in zip(out_refs, wanted):
+            block = lax.axis_index("ch") ^ (2 * k)
+            there = pl.ds(pl.multiple_of(block * columns, columns), columns)
+            here = slice(k * columns, (k + 1) * columns)
+            rows = slice(None)
+            if part is not None:
+                rows = slice(part * (span // 2), (part + 1) * (span // 2))
+            total = jnp.dot(mine_ref[rows, :], weight_ref[:, here], preferred_element_type=F32)
+            total = total + jnp.dot(
+                other_ref[rows, :], far_ref[:, there], preferred_element_type=F32
+            )
+            out_ref[...] = total.astype(out_ref.dtype)
+
+    out = [
+        jax.ShapeDtypeStruct((span if part is None else span // 2, columns), dtype)
+        for _, part in wanted
+    ]
+    return call(kernel, name, out)(mine, other, weight, far)
+
+
+def relay_kernel(passing, own, out):
+    out[...] = (passing[...].astype(F32) + own[...]).astype(BF16)
+
+
+def relay(passing, own):
+    return call(relay_kernel, "relay", jax.ShapeDtypeStruct(own.shape, BF16))(passing, own)
+
+
+def finish_kernel(own, direct1, joined3, direct3, joined1, out):
+    half = direct1.shape[0]
+    top = own[0:half, :] + (direct1[...].astype(F32) + joined3[...].astype(F32))
+    low = own[half:, :] + (direct3[...].astype(F32) + joined1[...].astype(F32))
+    total = jnp.concatenate([top.astype(BF16), low.astype(BF16)], axis=0)
     out[...] = lax.dot_general(
-        total.astype(BF16), order_matrix(total.shape[0]), TN, preferred_element_type=F32
+        total, order_matrix(total.shape[0]), TN, preferred_element_type=F32
     ).astype(BF16)
 
 
-def finish(own, received):
+def finish(own, *received):
     span, columns = own.shape
     out = jax.ShapeDtypeStruct((columns, span), BF16)
     return call(finish_kernel, "finish", out, held=False)(own, *received)
@@ -502,29 +574,33 @@
         modal_residue.T,
         skip_gain[None, :],
     )
-    before = jnp.zeros((ORDER, channels), F32)
-    border = jnp.zeros((16, channels), F32)
-    for j, (_, by) in enumerate(STEPS):
-        theirs = lax.ppermute(message, "ctx", [(i, i ^ by) for i in range(n_ctx)])
-        if j == 0:
-            local, gate, carry, reach = local_scan(gated, query_in, params, tables, message)
-            done = local
-        if j == 1:
-            done = weight = weight_blocks(out_weight, message)
-        message, before, border = merge(j, message, theirs, before, border, params, tables, done)
-    messages = [message]
-    for s in range(1, n_ctx // ROW):
-        pairs = [(i, i + s * ROW) for i in range(n_ctx - s * ROW)]
-        messages.append(lax.ppermute(message, "ctx", pairs))
+    def across(value, by):
+        return lax.ppermute(value, "ctx", [(i, i ^ by) for i in range(n_ctx)])
+
+    swapped = [across(message, k) for k in (3, 2, 1)]
+    local, gate, carry, reach = local_scan(gated, query_in, params, tables, message)
+    message, before, border = merge_four(message, swapped, params, tables, local)
+    theirs = across(message, PAIR)
+    weight = weight_blocks(out_weight, message)
+    message, before, border = merge_pair(message, theirs, before, border, params, tables, weight)
+    messages = [message] + [across(message, k * ROW) for k in (3, 2, 1)]
 
     own = gate_all(messages, before, border, local, gate, carry, reach, params, tables)
     other = lax.ppermute(own, "ch", sibling)
-    received = []
-    for k in (2, 1, 3):
-        part = project(own, other, weight, far, k, BF16)
-        received.append(lax.ppermute(part, "ch", [(i, i ^ (2 * k)) for i in range(n_ch)]))
-    kept = project(own, other, weight, far, 0, F32)
-    return finish(kept, received)
+
+    def swap(value, k):
+        return lax.ppermute(value, "ch", [(i, i ^ (2 * k)) for i in range(n_ch)])
+
+    operands = (own, other, weight, far)
+    over3, over1 = project(*operands, "opposite", [(2, 1), (2, 0)], BF16)
+    over3, over1 = swap(over3, 3), swap(over1, 1)
+    direct3, direct1 = project(*operands, "neighbours", [(3, 1), (1, 0)], BF16)
+    direct3, direct1 = swap(direct3, 3), swap(direct1, 1)
+    mine3, mine1 = project(*operands, "joining", [(3, 0), (1, 1)], F32)
+    (kept,) = project(*operands, "kept", [(0, None)], F32)
+    joined1 = swap(relay(over3, mine1), 1)
+    joined3 = swap(relay(over1, mine3), 3)
+    return finish(kept, direct1, joined3, direct3, joined1)
 
 
 def solution(mesh):

time: 51.4 us -> 46.1 us (0.90); the launches traced: 50.4 us -> 45.9 us
  starting transfers between devices: 23.9 us -> 21.2 us
  waiting for transfers between devices: 15.9 us -> 14 us
    ppermute x9 -> x13, starting transfers between devices: 23.8 us -> 21.1 us  [the longest x7 14.1 us: across(): return lax.ppermute(value, 'ctx', [(i, i ^ by) for i in range(n_ctx)])]
    ppermute x9 -> x13, waiting for transfers between devices: 14.4 us -> 12.5 us  [the longest x6 7.15 us: swap(): return lax.ppermute(value, 'ch', [(i, i ^ 2 * k) for i in range(n_ch)])]
    pallas_call x12 -> x13, Pallas kernels: 10.4 us -> 10.5 us  [run(): pl.pallas_call(kernel, in_specs=[pl.BlockSpec(memory_space=space) for spa...]
  transfers between devices with their start and end apart: 11 -> 15, of which waited for: 6 -> 10; matrix products, arithmetic and copies ran while one was open for 0% -> 0% of each run, Pallas kernels for 18% -> 20%
where the time goes in v1:
time: 46.1 us; the launch traced here: 45.9 us
  starting transfers between devices  21.2 us (46%)
  waiting for transfers between devices  14 us (30%)
  Pallas kernels  10.5 us (23%)
    ppermute x7, starting transfers between devices, across(): return lax.ppermute(value, 'ctx', [(i, i ^ by) for i in range(n_ctx)])  14.1 us
    pallas_call x13, Pallas kernels, run(): pl.pallas_call(kernel, in_specs=[pl.BlockSpec(memory_space=space) for spa...  10.5 us
    ppermute x6, waiting for transfers between devices, swap(): return lax.ppermute(value, 'ch', [(i, i ^ 2 * k) for i in range(n_ch)])  7.15 us
    ppermute x6, starting transfers between devices, swap(): return lax.ppermute(value, 'ch', [(i, i ^ 2 * k) for i in range(n_ch)])  6.96 us
    ppermute x7, waiting for transfers between devices, across(): return lax.ppermute(value, 'ctx', [(i, i ^ by) for i in range(n_ctx)])  5.36 us
    ppermute x1, waiting for transfers between devices, per_device(): other = lax.ppermute(own, 'ch', sibling)  1.52 us
  transfers between devices with their start and end apart: 15, of which 10 were waited for; matrix products, arithmetic and copies ran while one was open for 0% of the time, Pallas kernels for 20%

profile of v1, /device:TPU:32, one launch (start us, length us, event | category | flops | bytes accessed | tf_op | source)
XLA Modules:
  0.0 45.9 jit_solution(9885863230153575874)
XLA Ops:
  0.0 0.0 collective-permute-start.8
  0.0 2.6 %states.1 = (bf16[32,512]{1,0:T(8,128)(2,1)S(1)}, f32[256,512]{1,0:T(8,128)S(1)}, f32[16,512]{1,0:T(8,128)S(1)}, f32[29,16,512]{2,1,0:T(8,128)S(1)}) custom-call(bf16[512,256]{1,0:T(8,128)(2,1)} %key_hbm.1, bf16[512,256]{1,0:T(8,128)(2,1)} %value_hbm.1, bf16[512,256]{1,0:T(8,128)(2,1)} %query_hbm.3, f32[3,3,512]{2,1,0:T(4,128)} %bitcast.6, ...), custom_call_target="tpu_custom_call" | custom-call | tf_op jit(solution)/shard_map/states/pallas_call | solution.py:35
  2.6 2.0 %collective-permute-start = (bf16[32,512]{1,0:T(8,128)(2,1)S(1)}, bf16[32,512]{1,0:T(8,128)(2,1)S(1)}, u32[]{:S(2)}, u32[]{:S(2)}) collective-permute-start(bf16[32,512]{1,0:T(8,128)(2,1)S(1)} %get-tuple-element.25.after.mine), channel_id=1, source_target_pairs={{0,24},{8,16},{16,8},{24,0},{32,56},{40,48},{48,40},{56,32},{64,88... | collective-permute-start | bytes 98312 | tf_op jit(solution)/shard_map/ppermute | solution.py:578
  4.6 2.3 %collective-permute-start.1 = (bf16[32,512]{1,0:T(8,128)(2,1)S(1)}, bf16[32,512]{1,0:T(8,128)(2,1)S(1)}, u32[]{:S(2)}, u32[]{:S(2)}) collective-permute-start(bf16[32,512]{1,0:T(8,128)(2,1)S(1)} %get-tuple-element.25.after.mine), channel_id=1, source_target_pairs={{0,16},{8,24},{16,0},{24,8},{32,48},{40,56},{48,32},{56,40},{64,80... | collective-permute-start | bytes 98312 | tf_op jit(solution)/shard_map/ppermute | solution.py:578
  6.9 0.5 %collective-permute-start.2 = (bf16[32,512]{1,0:T(8,128)(2,1)S(1)}, bf16[32,512]{1,0:T(8,128)(2,1)S(1)}, u32[]{:S(2)}, u32[]{:S(2)}) collective-permute-start(bf16[32,512]{1,0:T(8,128)(2,1)S(1)} %get-tuple-element.25.after.mine), channel_id=1, source_target_pairs={{0,8},{8,0},{16,24},{24,16},{32,40},{40,32},{48,56},{56,48},{64,72... | collective-permute-start | bytes 98312 | tf_op jit(solution)/shard_map/ppermute | solution.py:578
  7.4 2.7 %local_scan.1 = (f32[256,512]{1,0:T(8,128)S(1)}, f32[256,512]{1,0:T(8,128)S(1)}, f32[128,512]{1,0:T(8,128)S(1)}, f32[128,512]{1,0:T(8,128)S(1)}) custom-call(f32[256,512]{1,0:T(8,128)S(1)} %get-tuple-element.28.gated, bf16[512,256]{1,0:T(8,128)(2,1)} %query_hbm.3, f32[16,512]{1,0:T(8,128)S(1)} %get-tuple-element.26.params, ...), custom_call_target="tpu_custom_call" | custom-call | tf_op jit(solution)/shard_map/local_scan/pallas_call | solution.py:35
  10.1 0.0 collective-permute-done.three
  10.1 0.0 collective-permute-done.1.two
  10.1 0.7 %collective-permute-done.2.one = bf16[32,512]{1,0:T(8,128)(2,1)S(1)} collective-permute-done((bf16[32,512]{1,0:T(8,128)(2,1)S(1)}, bf16[32,512]{1,0:T(8,128)(2,1)S(1)}, u32[]{:S(2)}, u32[]{:S(2)}) %collective-permute-start.2) | collective-permute-done | bytes 32800 | tf_op jit(solution)/shard_map/ppermute | solution.py:578
  10.8 0.1 merge_four.1
  10.9 5.1 %collective-permute-start.3 = (bf16[32,512]{1,0:T(8,128)(2,1)S(1)}, bf16[32,512]{1,0:T(8,128)(2,1)S(1)}, u32[]{:S(2)}, u32[]{:S(2)}) collective-permute-start(bf16[32,512]{1,0:T(8,128)(2,1)S(1)} %get-tuple-element.30.after.mine), channel_id=1, source_target_pairs={{0,56},{8,48},{16,40},{24,32},{32,24},{40,16},{48,8},{56,0},{64,12... | collective-permute-start | bytes 98312 | tf_op jit(solution)/shard_map/ppermute | solution.py:578
  16.0 1.6 %weight_blocks.1.after.weight_ref = bf16[512,2048]{1,0:T(8,128)(2,1)S(1)} custom-call(bf16[512,4096]{1,0:T(8,128)(2,1)} %weight_hbm.1, bf16[32,512]{1,0:T(8,128)(2,1)S(1)} %get-tuple-element.30.after.mine), custom_call_target="tpu_custom_call" | custom-call | tf_op jit(solution)/shard_map/weight_blocks/pallas_call | solution.py:35
  17.6 0.3 collective-permute-done.3.theirs
  17.9 3.1 %collective-permute-start.4 = (bf16[32,512]{1,0:T(8,128)(2,1)S(1)}, bf16[32,512]{1,0:T(8,128)(2,1)S(1)}, u32[]{:S(2)}, u32[]{:S(2)}) collective-permute-start(bf16[32,512]{1,0:T(8,128)(2,1)S(1)} %get-tuple-element.33.mine), channel_id=1, source_target_pairs={{0,192},{8,200},{16,208},{24,216},{32,224},{40,232},{48,240},{56,2... | collective-permute-start | bytes 98312 | tf_op jit(solution)/shard_map/ppermute | solution.py:578
  21.0 0.6 %collective-permute-start.5 = (bf16[32,512]{1,0:T(8,128)(2,1)S(1)}, bf16[32,512]{1,0:T(8,128)(2,1)S(1)}, u32[]{:S(2)}, u32[]{:S(2)}) collective-permute-start(bf16[32,512]{1,0:T(8,128)(2,1)S(1)} %get-tuple-element.33.mine), channel_id=1, source_target_pairs={{0,128},{8,136},{16,144},{24,152},{32,160},{40,168},{48,176},{56,1... | collective-permute-start | bytes 98312 | tf_op jit(solution)/shard_map/ppermute | solution.py:578
  21.7 0.5 %collective-permute-start.6 = (bf16[32,512]{1,0:T(8,128)(2,1)S(1)}, bf16[32,512]{1,0:T(8,128)(2,1)S(1)}, u32[]{:S(2)}, u32[]{:S(2)}) collective-permute-start(bf16[32,512]{1,0:T(8,128)(2,1)S(1)} %get-tuple-element.33.mine), channel_id=1, source_target_pairs={{0,64},{8,72},{16,80},{24,88},{32,96},{40,104},{48,112},{56,120},{... | collective-permute-start | bytes 98312 | tf_op jit(solution)/shard_map/ppermute | solution.py:578
  22.1 1.0 %collective-permute-done.4.row3 = bf16[32,512]{1,0:T(8,128)(2,1)S(1)} collective-permute-done((bf16[32,512]{1,0:T(8,128)(2,1)S(1)}, bf16[32,512]{1,0:T(8,128)(2,1)S(1)}, u32[]{:S(2)}, u32[]{:S(2)}) %collective-permute-start.4) | collective-permute-done | bytes 32800 | tf_op jit(solution)/shard_map/ppermute | solution.py:578
  23.2 3.3 %collective-permute-done.5.row2 = bf16[32,512]{1,0:T(8,128)(2,1)S(1)} collective-permute-done((bf16[32,512]{1,0:T(8,128)(2,1)S(1)}, bf16[32,512]{1,0:T(8,128)(2,1)S(1)}, u32[]{:S(2)}, u32[]{:S(2)}) %collective-permute-start.5) | collective-permute-done | bytes 32800 | tf_op jit(solution)/shard_map/ppermute | solution.py:578
  26.4 0.0 collective-permute-done.6.row1
  26.4 0.8 %gated.1.mine_ref = bf16[256,512]{1,0:T(8,128)(2,1)S(1)} custom-call(bf16[32,512]{1,0:T(8,128)(2,1)S(1)} %get-tuple-element.33.mine, bf16[32,512]{1,0:T(8,128)(2,1)S(1)} %collective-permute-done.4.row3, bf16[32,512]{1,0:T(8,128)(2,1)S(1)} %collective-permute-done.5.row2, bf16[32,512]{1,0:T(8,128)(2,1)S(1)} %collective-permute-done.6.row1, ...), custom_call_target="tpu_custom_call" | custom-call | tf_op jit(solution)/shard_map/gated/pallas_call | solution.py:35
  27.2 0.1 collective-permute-start.7
  27.3 1.5 %collective-permute-done.7.other_ref = bf16[256,512]{1,0:T(8,128)(2,1)S(1)} collective-permute-done((bf16[256,512]{1,0:T(8,128)(2,1)S(1)}, bf16[256,512]{1,0:T(8,128)(2,1)S(1)}, u32[]{:S(2)}, u32[]{:S(2)}) %collective-permute-start.7) | collective-permute-done | bytes 262176 | tf_op jit(solution)/shard_map/ppermute | solution.py:589
  28.9 0.0 collective-permute-done.8.far_ref
  28.9 0.4 opposite.1
  29.3 2.9 %collective-permute-start.13 = (bf16[128,512]{1,0:T(8,128)(2,1)S(1)}, bf16[128,512]{1,0:T(8,128)(2,1)S(1)}, u32[]{:S(2)}, u32[]{:S(2)}) collective-permute-start(bf16[128,512]{1,0:T(8,128)(2,1)S(1)} %get-tuple-element.43), channel_id=1, source_target_pairs={{0,6},{1,7},{2,4},{3,5},{4,2},{5,3},{6,0},{7,1},{8,14},{9,15},{10,... | collective-permute-start | bytes 393224 | tf_op jit(solution)/shard_map/ppermute | solution.py:592
  32.2 0.2 collective-permute-start.10
  32.4 0.4 neighbours.1
  32.8 1.2 %collective-permute-start.12 = (bf16[128,512]{1,0:T(8,128)(2,1)S(1)}, bf16[128,512]{1,0:T(8,128)(2,1)S(1)}, u32[]{:S(2)}, u32[]{:S(2)}) collective-permute-start(bf16[128,512]{1,0:T(8,128)(2,1)S(1)} %get-tuple-element.42), channel_id=1, source_target_pairs={{0,6},{1,7},{2,4},{3,5},{4,2},{5,3},{6,0},{7,1},{8,14},{9,15},{10,... | collective-permute-start | bytes 393224 | tf_op jit(solution)/shard_map/ppermute | solution.py:592
  34.1 0.8 %collective-permute-start.9 = (bf16[128,512]{1,0:T(8,128)(2,1)S(1)}, bf16[128,512]{1,0:T(8,128)(2,1)S(1)}, u32[]{:S(2)}, u32[]{:S(2)}) collective-permute-start(bf16[128,512]{1,0:T(8,128)(2,1)S(1)} %get-tuple-element.39), channel_id=1, source_target_pairs={{0,2},{1,3},{2,0},{3,1},{4,6},{5,7},{6,4},{7,5},{8,10},{9,11},{10,... | collective-permute-start | bytes 393224 | tf_op jit(solution)/shard_map/ppermute | solution.py:592
  34.8 0.4 joining.1
  35.3 0.9 %collective-permute-done.13.passing = bf16[128,512]{1,0:T(8,128)(2,1)S(1)} collective-permute-done((bf16[128,512]{1,0:T(8,128)(2,1)S(1)}, bf16[128,512]{1,0:T(8,128)(2,1)S(1)}, u32[]{:S(2)}, u32[]{:S(2)}) %collective-permute-start.13) | collective-permute-done | bytes 131104 | tf_op jit(solution)/shard_map/ppermute | solution.py:592
  36.2 0.5 %collective-permute-start.14 = (bf16[128,512]{1,0:T(8,128)(2,1)S(1)}, bf16[128,512]{1,0:T(8,128)(2,1)S(1)}, u32[]{:S(2)}, u32[]{:S(2)}) collective-permute-start(bf16[128,512]{1,0:T(8,128)(2,1)S(1)} %relay.3), channel_id=1, source_target_pairs={{0,2},{1,3},{2,0},{3,1},{4,6},{5,7},{6,4},{7,5},{8,10},{9,11},{10,... | collective-permute-start | bytes 393224 | tf_op jit(solution)/shard_map/ppermute | solution.py:592
  36.7 1.9 %collective-permute-done.10.passing = bf16[128,512]{1,0:T(8,128)(2,1)S(1)} collective-permute-done((bf16[128,512]{1,0:T(8,128)(2,1)S(1)}, bf16[128,512]{1,0:T(8,128)(2,1)S(1)}, u32[]{:S(2)}, u32[]{:S(2)}) %collective-permute-start.10) | collective-permute-done | bytes 131104 | tf_op jit(solution)/shard_map/ppermute | solution.py:592
  38.6 1.4 %collective-permute-start.11 = (bf16[128,512]{1,0:T(8,128)(2,1)S(1)}, bf16[128,512]{1,0:T(8,128)(2,1)S(1)}, u32[]{:S(2)}, u32[]{:S(2)}) collective-permute-start(bf16[128,512]{1,0:T(8,128)(2,1)S(1)} %relay.2), channel_id=1, source_target_pairs={{0,6},{1,7},{2,4},{3,5},{4,2},{5,3},{6,0},{7,1},{8,14},{9,15},{10,... | collective-permute-start | bytes 393224 | tf_op jit(solution)/shard_map/ppermute | solution.py:592
  40.0 0.4 kept.1.own
  40.4 0.0 collective-permute-done.12.direct3
  40.4 0.9 %collective-permute-done.9.direct1 = bf16[128,512]{1,0:T(8,128)(2,1)S(1)} collective-permute-done((bf16[128,512]{1,0:T(8,128)(2,1)S(1)}, bf16[128,512]{1,0:T(8,128)(2,1)S(1)}, u32[]{:S(2)}, u32[]{:S(2)}) %collective-permute-start.9) | collective-permute-done | bytes 131104 | tf_op jit(solution)/shard_map/ppermute | solution.py:592
  41.4 1.7 %collective-permute-done.14.joined1 = bf16[128,512]{1,0:T(8,128)(2,1)S(1)} collective-permute-done((bf16[128,512]{1,0:T(8,128)(2,1)S(1)}, bf16[128,512]{1,0:T(8,128)(2,1)S(1)}, u32[]{:S(2)}, u32[]{:S(2)}) %collective-permute-start.14) | collective-permute-done | bytes 131104 | tf_op jit(solution)/shard_map/ppermute | solution.py:592
  43.0 1.8 %collective-permute-done.11.joined3 = bf16[128,512]{1,0:T(8,128)(2,1)S(1)} collective-permute-done((bf16[128,512]{1,0:T(8,128)(2,1)S(1)}, bf16[128,512]{1,0:T(8,128)(2,1)S(1)}, u32[]{:S(2)}, u32[]{:S(2)}) %collective-permute-start.11) | collective-permute-done | bytes 131104 | tf_op jit(solution)/shard_map/ppermute | solution.py:592
  44.8 1.0 %finish.1 = bf16[512,256]{1,0:T(8,128)(2,1)} custom-call(f32[256,512]{1,0:T(8,128)S(1)} %kept.1.own, bf16[128,512]{1,0:T(8,128)(2,1)S(1)} %collective-permute-done.9.direct1, bf16[128,512]{1,0:T(8,128)(2,1)S(1)} %collective-permute-done.11.joined3, bf16[128,512]{1,0:T(8,128)(2,1)S(1)} %collective-permute-done.12.direct3, ...), custom_call_target="tpu_custom_call" | custom-call | tf_op jit(solution)/shard_map/finish/pallas_call | solution.py:35
  (3 shorter events, 0.1 us)
Async XLA Ops:
  0.0 28.9 %collective-permute-start.8 = (bf16[512,4096]{1,0:T(8,128)(2,1)}, bf16[512,4096]{1,0:T(8,128)(2,1)S(1)}, u32[]{:S(2)}, u32[]{:S(2)}) collective-permute-start(bf16[512,4096]{1,0:T(8,128)(2,1)} %weight_hbm.1), channel_id=1, source_target_pairs={{0,1},{1,0},{2,3},{3,2},{4,5},{5,4},{6,7},{7,6},{8,9},{9,8},{10,11... | collective-permute-start | bytes 12582920 | tf_op jit(solution)/shard_map/ppermute | solution.py:566
  2.6 7.5 %collective-permute-start = (bf16[32,512]{1,0:T(8,128)(2,1)S(1)}, bf16[32,512]{1,0:T(8,128)(2,1)S(1)}, u32[]{:S(2)}, u32[]{:S(2)}) collective-permute-start(bf16[32,512]{1,0:T(8,128)(2,1)S(1)} %get-tuple-element.25.after.mine), channel_id=1, source_target_pairs={{0,24},{8,16},{16,8},{24,0},{32,56},{40,48},{48,40},{56,32},{64,88... | collective-permute-start | bytes 98312 | tf_op jit(solution)/shard_map/ppermute | solution.py:578
  4.6 5.5 %collective-permute-start.1 = (bf16[32,512]{1,0:T(8,128)(2,1)S(1)}, bf16[32,512]{1,0:T(8,128)(2,1)S(1)}, u32[]{:S(2)}, u32[]{:S(2)}) collective-permute-start(bf16[32,512]{1,0:T(8,128)(2,1)S(1)} %get-tuple-element.25.after.mine), channel_id=1, source_target_pairs={{0,16},{8,24},{16,0},{24,8},{32,48},{40,56},{48,32},{56,40},{64,80... | collective-permute-start | bytes 98312 | tf_op jit(solution)/shard_map/ppermute | solution.py:578
  6.9 3.9 %collective-permute-start.2 = (bf16[32,512]{1,0:T(8,128)(2,1)S(1)}, bf16[32,512]{1,0:T(8,128)(2,1)S(1)}, u32[]{:S(2)}, u32[]{:S(2)}) collective-permute-start(bf16[32,512]{1,0:T(8,128)(2,1)S(1)} %get-tuple-element.25.after.mine), channel_id=1, source_target_pairs={{0,8},{8,0},{16,24},{24,16},{32,40},{40,32},{48,56},{56,48},{64,72... | collective-permute-start | bytes 98312 | tf_op jit(solution)/shard_map/ppermute | solution.py:578
  10.9 7.0 %collective-permute-start.3 = (bf16[32,512]{1,0:T(8,128)(2,1)S(1)}, bf16[32,512]{1,0:T(8,128)(2,1)S(1)}, u32[]{:S(2)}, u32[]{:S(2)}) collective-permute-start(bf16[32,512]{1,0:T(8,128)(2,1)S(1)} %get-tuple-element.30.after.mine), channel_id=1, source_target_pairs={{0,56},{8,48},{16,40},{24,32},{32,24},{40,16},{48,8},{56,0},{64,12... | collective-permute-start | bytes 98312 | tf_op jit(solution)/shard_map/ppermute | solution.py:578
  17.9 5.2 %collective-permute-start.4 = (bf16[32,512]{1,0:T(8,128)(2,1)S(1)}, bf16[32,512]{1,0:T(8,128)(2,1)S(1)}, u32[]{:S(2)}, u32[]{:S(2)}) collective-permute-start(bf16[32,512]{1,0:T(8,128)(2,1)S(1)} %get-tuple-element.33.mine), channel_id=1, source_target_pairs={{0,192},{8,200},{16,208},{24,216},{32,224},{40,232},{48,240},{56,2... | collective-permute-start | bytes 98312 | tf_op jit(solution)/shard_map/ppermute | solution.py:578
  21.0 5.4 %collective-permute-start.5 = (bf16[32,512]{1,0:T(8,128)(2,1)S(1)}, bf16[32,512]{1,0:T(8,128)(2,1)S(1)}, u32[]{:S(2)}, u32[]{:S(2)}) collective-permute-start(bf16[32,512]{1,0:T(8,128)(2,1)S(1)} %get-tuple-element.33.mine), channel_id=1, source_target_pairs={{0,128},{8,136},{16,144},{24,152},{32,160},{40,168},{48,176},{56,1... | collective-permute-start | bytes 98312 | tf_op jit(solution)/shard_map/ppermute | solution.py:578
  21.7 4.8 %collective-permute-start.6 = (bf16[32,512]{1,0:T(8,128)(2,1)S(1)}, bf16[32,512]{1,0:T(8,128)(2,1)S(1)}, u32[]{:S(2)}, u32[]{:S(2)}) collective-permute-start(bf16[32,512]{1,0:T(8,128)(2,1)S(1)} %get-tuple-element.33.mine), channel_id=1, source_target_pairs={{0,64},{8,72},{16,80},{24,88},{32,96},{40,104},{48,112},{56,120},{... | collective-permute-start | bytes 98312 | tf_op jit(solution)/shard_map/ppermute | solution.py:578
  27.2 1.6 %collective-permute-start.7 = (bf16[256,512]{1,0:T(8,128)(2,1)S(1)}, bf16[256,512]{1,0:T(8,128)(2,1)S(1)}, u32[]{:S(2)}, u32[]{:S(2)}) collective-permute-start(bf16[256,512]{1,0:T(8,128)(2,1)S(1)} %gated.1.mine_ref), channel_id=1, source_target_pairs={{0,1},{1,0},{2,3},{3,2},{4,5},{5,4},{6,7},{7,6},{8,9},{9,8},{10,11... | collective-permute-start | bytes 786440 | tf_op jit(solution)/shard_map/ppermute | solution.py:589
  29.3 6.8 %collective-permute-start.13 = (bf16[128,512]{1,0:T(8,128)(2,1)S(1)}, bf16[128,512]{1,0:T(8,128)(2,1)S(1)}, u32[]{:S(2)}, u32[]{:S(2)}) collective-permute-start(bf16[128,512]{1,0:T(8,128)(2,1)S(1)} %get-tuple-element.43), channel_id=1, source_target_pairs={{0,6},{1,7},{2,4},{3,5},{4,2},{5,3},{6,0},{7,1},{8,14},{9,15},{10,... | collective-permute-start | bytes 393224 | tf_op jit(solution)/shard_map/ppermute | solution.py:592
  32.2 6.4 %collective-permute-start.10 = (bf16[128,512]{1,0:T(8,128)(2,1)S(1)}, bf16[128,512]{1,0:T(8,128)(2,1)S(1)}, u32[]{:S(2)}, u32[]{:S(2)}) collective-permute-start(bf16[128,512]{1,0:T(8,128)(2,1)S(1)} %get-tuple-element.40), channel_id=1, source_target_pairs={{0,2},{1,3},{2,0},{3,1},{4,6},{5,7},{6,4},{7,5},{8,10},{9,11},{10,... | collective-permute-start | bytes 393224 | tf_op jit(solution)/shard_map/ppermute | solution.py:592
  32.8 7.6 %collective-permute-start.12 = (bf16[128,512]{1,0:T(8,128)(2,1)S(1)}, bf16[128,512]{1,0:T(8,128)(2,1)S(1)}, u32[]{:S(2)}, u32[]{:S(2)}) collective-permute-start(bf16[128,512]{1,0:T(8,128)(2,1)S(1)} %get-tuple-element.42), channel_id=1, source_target_pairs={{0,6},{1,7},{2,4},{3,5},{4,2},{5,3},{6,0},{7,1},{8,14},{9,15},{10,... | collective-permute-start | bytes 393224 | tf_op jit(solution)/shard_map/ppermute | solution.py:592
  34.1 7.3 %collective-permute-start.9 = (bf16[128,512]{1,0:T(8,128)(2,1)S(1)}, bf16[128,512]{1,0:T(8,128)(2,1)S(1)}, u32[]{:S(2)}, u32[]{:S(2)}) collective-permute-start(bf16[128,512]{1,0:T(8,128)(2,1)S(1)} %get-tuple-element.39), channel_id=1, source_target_pairs={{0,2},{1,3},{2,0},{3,1},{4,6},{5,7},{6,4},{7,5},{8,10},{9,11},{10,... | collective-permute-start | bytes 393224 | tf_op jit(solution)/shard_map/ppermute | solution.py:592
  36.2 6.9 %collective-permute-start.14 = (bf16[128,512]{1,0:T(8,128)(2,1)S(1)}, bf16[128,512]{1,0:T(8,128)(2,1)S(1)}, u32[]{:S(2)}, u32[]{:S(2)}) collective-permute-start(bf16[128,512]{1,0:T(8,128)(2,1)S(1)} %relay.3), channel_id=1, source_target_pairs={{0,2},{1,3},{2,0},{3,1},{4,6},{5,7},{6,4},{7,5},{8,10},{9,11},{10,... | collective-permute-start | bytes 393224 | tf_op jit(solution)/shard_map/ppermute | solution.py:592
  38.6 6.3 %collective-permute-start.11 = (bf16[128,512]{1,0:T(8,128)(2,1)S(1)}, bf16[128,512]{1,0:T(8,128)(2,1)S(1)}, u32[]{:S(2)}, u32[]{:S(2)}) collective-permute-start(bf16[128,512]{1,0:T(8,128)(2,1)S(1)} %relay.2), channel_id=1, source_target_pairs={{0,6},{1,7},{2,4},{3,5},{4,2},{5,3},{6,0},{7,1},{8,14},{9,15},{10,... | collective-permute-start | bytes 393224 | tf_op jit(solution)/shard_map/ppermute | solution.py:592

commit v2 on v1

--- a/solution.py
+++ b/solution.py
@@ -19,12 +19,14 @@
 DECAY, FADE, WEIGHT, GROWTH = 0, 1, 4, 5
 ALL, ALL_SEAM, AHEAD, AHEAD_SEAM, OVER_PAIR, OVER_Y = 7, 10, 13, 16, 18, 23
 TABLES = 29
-SKIP, GROWN, FIRST = 9, 10, 11
+SKIP, FIRST = 9, 10
 EDGES = 16
 
 
 def call(kernel, name, out, scratch=(), held=True, outside=(), unread=()):
     whole = pl.BlockSpec(memory_space=pltpu.VMEM)
+    if not held:
+        whole = pl.BlockSpec(memory_space=pl.ANY)
     place = (lambda o: pltpu.VMEM(o.shape, o.dtype)) if held else (lambda o: o)
 
     def run(*args):
@@ -69,8 +71,9 @@
     return here // ROW, lax.rem(here, ROW)
 
 
-def fill_tables(damping, residue, span, tables):
+def fill_tables(basis, modes, span, tables):
     y, z = place_of()
+    damping, residue = modes[0], modes[1]
 
     def fade(by):
         return jnp.exp(-damping * by)
@@ -78,9 +81,8 @@
     def only(flag, value):
         return jnp.where(flag, value, 0.0)
 
-    tables[DECAY] = fade(1.0)
-    for i in range(3):
-        tables[FADE + i] = fade(float((span // SEGMENTS) << i))
+    for i in range(4):
+        tables[DECAY + i] = basis[i]
     tables[WEIGHT] = residue * jnp.sqrt(damping)
     tables[GROWTH] = fade(-1.0)
     tables[GROWTH + 1] = fade(-2.0)
@@ -120,12 +122,12 @@
     message,
     gated,
     params,
-    tables,
+    basis,
+    modes,
+    order,
     raw,
     tail,
     taps_in,
-    damping,
-    residue,
     skip,
     streams,
     state,
@@ -134,42 +136,47 @@
 ):
     channels, span = key_hbm.shape
     steps = span // SEGMENTS
-    copies = [
+    fixed = [
         pltpu.make_async_copy(src, dst, sems.at[i])
         for i, (src, dst) in enumerate(
             (
-                (damping_hbm, damping),
-                (residue_hbm, residue),
-                (key_hbm, raw.at[0]),
-                (value_hbm, raw.at[1]),
+                (damping_hbm, modes.at[0]),
                 (taps_hbm, taps_in),
+                (residue_hbm, modes.at[1]),
                 (skip_hbm, skip),
                 (query_hbm.at[:, span - LANES :], tail),
             )
         )
     ]
-    for c in copies:
+
+    big = [
+        pltpu.make_async_copy(src, raw.at[s], sems.at[len(fixed) + s])
+        for s, src in enumerate((key_hbm, value_hbm))
+    ]
+    for c in fixed[:2]:
         c.start()
-    order = order_matrix(span)
-    for c in copies[:2]:
-        c.wait()
-    fill_tables(damping[...], residue[...], span, tables)
-    for c in copies[2:]:
-        c.wait()
-    for s in range(2):
-        streams[s] = lax.dot_general(order, raw[s], NT, preferred_element_type=F32)
+    for c in big:
+        c.start()
+    for c in fixed[2:]:
+        c.start()
+    order[...] = order_matrix(span)
     segment = segment_index()
     params[...] = jnp.zeros_like(params)
+    edges[...] = jnp.zeros_like(edges)
+    for c in fixed[:2]:
+        c.wait()
+    basis[DECAY] = jnp.exp(-modes[0])
+    for i in range(3):
+        basis[FADE + i] = jnp.exp(-modes[0] * float(steps << i))
     for i in range(9):
         params[i : i + 1, :] = taps_in[(1 + i // 3) % 3, i % 3, :][None, :]
-    params[SKIP : SKIP + 1, :] = skip[...]
-    params[GROWN : GROWN + 1, :] = jnp.sum(
-        tables[WEIGHT] * tables[GROWTH], axis=0, keepdims=True
-    )
+    for s in range(2):
+        big[s].wait()
+        streams[s] = lax.dot_general(order[...], raw[s], NT, preferred_element_type=F32)
 
     def group(lanes):
         taps = [params[i : i + 1, lanes] for i in range(6)]
-        decay = [tables[DECAY, r : r + 1, lanes] for r in range(ORDER)]
+        decay = [basis[DECAY, r : r + 1, lanes] for r in range(ORDER)]
 
         def at(s, a):
             if a >= 0:
@@ -196,17 +203,19 @@
         for r in range(ORDER):
             total = held[r]
             for i in range(3):
-                fade = tables[FADE + i, r : r + 1, lanes]
+                fade = basis[FADE + i, r : r + 1, lanes]
                 total = total + fade * pltpu.roll(total, 1 << i, 0)
             state[r : r + 1, lanes] = total[SEGMENTS - 1 :]
 
     by_group(channels, group)
     at = lambda i: params[FIRST + i : FIRST + i + 1, :]
-    start_fade = jnp.exp(-damping[...] * float(span - 2))
-    start = start_fade * (tables[DECAY] * (at(0) * at(2)) + at(1) * at(3))
+    start_fade = jnp.exp(-modes[0] * float(span - 2))
+    start = start_fade * (basis[DECAY] * (at(0) * at(2)) + at(1) * at(3))
     total = state[...] + jnp.where(lax.axis_index("ctx") == 0, start, 0.0)
     message[0:ORDER, :] = total.astype(BF16)
-    edges[...] = jnp.zeros_like(edges)
+    for c in fixed[2:]:
+        c.wait()
+    params[SKIP : SKIP + 1, :] = skip[...]
     for s in range(2):
         edges[2 * s : 2 * s + 1, :] = streams[s, 0:1, :]
         edges[2 * s + 1 : 2 * s + 2, :] = streams[s, SEGMENTS : SEGMENTS + 1, :]
@@ -226,14 +235,14 @@
         shape((EDGES + 16, channels), BF16),
         shape((span, channels), F32),
         shape((16, channels), F32),
-        shape((TABLES, ORDER, channels), F32),
+        shape((4, ORDER, channels), F32),
+        shape((2, ORDER, channels), F32),
+        shape((span, span), BF16),
     ]
     scratch = [
         pltpu.VMEM((2, channels, span), BF16),
         pltpu.VMEM((channels, LANES), BF16),
         pltpu.VMEM(taps.shape, F32),
-        pltpu.VMEM(damping.shape, F32),
-        pltpu.VMEM(residue.shape, F32),
         pltpu.VMEM(skip.shape, F32),
         pltpu.VMEM((2, span, channels), F32),
         pltpu.VMEM((ORDER, channels), F32),
@@ -246,15 +255,29 @@
 
 
 def local_kernel(
-    gated, query_hbm, params, tables, after, local, gate, carry, reach, raw, stream, sem
+    gated,
+    query_hbm,
+    params,
+    basis,
+    modes,
+    order,
+    after,
+    local,
+    gate,
+    carry,
+    reach,
+    tables,
+    raw,
+    stream,
+    sem,
 ):
     channels, span = query_hbm.shape
     steps = span // SEGMENTS
     copy = pltpu.make_async_copy(query_hbm, raw, sem)
     copy.start()
-    order = order_matrix(span)
+    fill_tables(basis, modes, span, tables)
     copy.wait()
-    stream[...] = lax.dot_general(order, raw[...], NT, preferred_element_type=F32)
+    stream[...] = lax.dot_general(order[...], raw[...], NT, preferred_element_type=F32)
     segment = segment_index()
 
     def group(lanes):
@@ -297,7 +320,7 @@
     by_group(channels, group)
 
 
-def local_scan(gated, query_in, params, tables, after):
+def local_scan(gated, query_in, params, basis, modes, order, after):
     channels, span = query_in.shape
     shape = jax.ShapeDtypeStruct
     out = [
@@ -305,14 +328,15 @@
         shape((span, channels), F32),
         shape((ORDER * SEGMENTS, channels), F32),
         shape((ORDER * SEGMENTS, channels), F32),
+        shape((TABLES, ORDER, channels), F32),
     ]
     scratch = [
         pltpu.VMEM((channels, span), BF16),
         pltpu.VMEM((span, channels), F32),
         pltpu.SemaphoreType.DMA,
     ]
-    return call(local_kernel, "local_scan", out, scratch, outside=(1,), unread=(4,))(
-        gated, query_in, params, tables, after
+    return call(local_kernel, "local_scan", out, scratch, outside=(1,), unread=(6,))(
+        gated, query_in, params, basis, modes, order, after
     )
 
 
@@ -443,7 +467,8 @@
     u[0] = (p(FIRST) + p(1) * e(1) + p(2) * e(0)) * (p(FIRST + 2) + p(4) * e(3) + p(5) * e(2))
     u[1] = (p(FIRST + 1) + p(2) * e(1)) * (p(FIRST + 3) + p(5) * e(3))
     before[...] = total + tables[GROWTH] * u[0] + tables[GROWTH + 1] * u[1]
-    starts[0:1, :] = p(SKIP) * u[0] - p(GROWN) * u[1]
+    grown = jnp.sum(tables[WEIGHT] * tables[GROWTH], axis=0, keepdims=True)
+    starts[0:1, :] = p(SKIP) * u[0] - grown * u[1]
     starts[1:2, :] = p(SKIP) * u[1]
     starts[2:3, :] = p(7) * e(5) + p(8) * e(4)
     starts[3:4, :] = p(8) * e(5)
@@ -508,29 +533,33 @@
     return call(blocks_kernel, "weight_blocks", out, scratch, outside=(0,), unread=(1,))(weight, after)
 
 
-def project(mine, other, weight, far, name, wanted, dtype):
-    span = mine.shape[0]
+def near_kernel(mine, weight, out):
+    out[...] = jnp.dot(mine[...], weight[...], preferred_element_type=F32)
+
+
+def near_sums(mine, weight):
+    out = jax.ShapeDtypeStruct((mine.shape[0], weight.shape[1]), F32)
+    return call(near_kernel, "near_sums", out)(mine, weight)
+
+
+def project(near, other, far, name, wanted, dtype):
+    span = near.shape[0]
+    half = span // 2
     columns = far.shape[1] // lax.axis_size("ch")
 
-    def kernel(mine_ref, other_ref, weight_ref, far_ref, *out_refs):
-        for out_ref, (k, part) in zip(out_refs, wanted):
-            block = lax.axis_index("ch") ^ (2 * k)
-            there = pl.ds(pl.multiple_of(block * columns, columns), columns)
-            here = slice(k * columns, (k + 1) * columns)
-            rows = slice(None)
-            if part is not None:
-                rows = slice(part * (span // 2), (part + 1) * (span // 2))
-            total = jnp.dot(mine_ref[rows, :], weight_ref[:, here], preferred_element_type=F32)
-            total = total + jnp.dot(
-                other_ref[rows, :], far_ref[:, there], preferred_element_type=F32
-            )
-            out_ref[...] = total.astype(out_ref.dtype)
-
-    out = [
-        jax.ShapeDtypeStruct((span if part is None else span // 2, columns), dtype)
-        for _, part in wanted
-    ]
-    return call(kernel, name, out)(mine, other, weight, far)
+    def kernel(near_ref, other_ref, far_ref, *out_refs):
+        for out_ref, parts in zip(out_refs, wanted):
+            for i, (k, part) in enumerate(parts):
+                block = lax.axis_index("ch") ^ (2 * k)
+                there = pl.ds(pl.multiple_of(block * columns, columns), columns)
+                rows = slice(part * half, (part + 1) * half)
+                total = near_ref[rows, k * columns : (k + 1) * columns] + jnp.dot(
+                    other_ref[rows, :], far_ref[:, there], preferred_element_type=F32
+                )
+                out_ref[i * half : (i + 1) * half, :] = total.astype(dtype)
+
+    out = [jax.ShapeDtypeStruct((half * len(parts), columns), dtype) for parts in wanted]
+    return call(kernel, name, out)(near, other, far)
 
 
 def relay_kernel(passing, own, out):
@@ -541,20 +570,29 @@
     return call(relay_kernel, "relay", jax.ShapeDtypeStruct(own.shape, BF16))(passing, own)
 
 
-def finish_kernel(own, direct1, joined3, direct3, joined1, out):
-    half = direct1.shape[0]
-    top = own[0:half, :] + (direct1[...].astype(F32) + joined3[...].astype(F32))
-    low = own[half:, :] + (direct3[...].astype(F32) + joined1[...].astype(F32))
-    total = jnp.concatenate([top.astype(BF16), low.astype(BF16)], axis=0)
-    out[...] = lax.dot_general(
-        total, order_matrix(total.shape[0]), TN, preferred_element_type=F32
-    ).astype(BF16)
+def finish_kernel(own, direct1, direct3, joined1, joined3, order, out, result, sems):
+    half = joined1.shape[0]
+    columns = own.shape[1]
+    copies = []
+    for i in range(2):
+        here = slice(i * columns // 2, (i + 1) * columns // 2)
+        top = own[0:half, here] + (direct1[:, here].astype(F32) + joined3[:, here].astype(F32))
+        low = own[half:, here] + (direct3[:, here].astype(F32) + joined1[:, here].astype(F32))
+        total = jnp.concatenate([top.astype(BF16), low.astype(BF16)], axis=0)
+        result[here, :] = lax.dot_general(
+            total, order[...], TN, preferred_element_type=F32
+        ).astype(BF16)
+        copies.append(pltpu.make_async_copy(result.at[here, :], out.at[here, :], sems.at[i]))
+        copies[-1].start()
+    for c in copies:
+        c.wait()
 
 
 def finish(own, *received):
     span, columns = own.shape
     out = jax.ShapeDtypeStruct((columns, span), BF16)
-    return call(finish_kernel, "finish", out, held=False)(own, *received)
+    scratch = [pltpu.VMEM(out.shape, BF16), pltpu.SemaphoreType.DMA((2,))]
+    return call(finish_kernel, "finish", out, scratch, held=False)(own, *received)
 
 
 def per_device(
@@ -563,9 +601,7 @@
     channels = query_in.shape[0]
     n_ctx, n_ch = lax.axis_size("ctx"), lax.axis_size("ch")
     sibling = [(i, i ^ 1) for i in range(n_ch)]
-    far = lax.ppermute(out_weight, "ch", sibling)
-
-    message, gated, params, tables = states(
+    message, gated, params, basis, modes, order = states(
         key_in,
         value_in,
         query_in,
@@ -578,8 +614,12 @@
         return lax.ppermute(value, "ctx", [(i, i ^ by) for i in range(n_ctx)])
 
     swapped = [across(message, k) for k in (3, 2, 1)]
-    local, gate, carry, reach = local_scan(gated, query_in, params, tables, message)
+    local, gate, carry, reach, tables = local_scan(
+        gated, query_in, params, basis, modes, order, message
+    )
     message, before, border = merge_four(message, swapped, params, tables, local)
+    later, _ = lax.optimization_barrier((out_weight, message))
+    far = lax.ppermute(later, "ch", sibling)
     theirs = across(message, PAIR)
     weight = weight_blocks(out_weight, message)
     message, before, border = merge_pair(message, theirs, before, border, params, tables, weight)
@@ -591,16 +631,16 @@
     def swap(value, k):
         return lax.ppermute(value, "ch", [(i, i ^ (2 * k)) for i in range(n_ch)])
 
-    operands = (own, other, weight, far)
-    over3, over1 = project(*operands, "opposite", [(2, 1), (2, 0)], BF16)
+    operands = (near_sums(own, weight), other, far)
+    over3, over1 = project(*operands, "opposite", [[(2, 1)], [(2, 0)]], BF16)
     over3, over1 = swap(over3, 3), swap(over1, 1)
-    direct3, direct1 = project(*operands, "neighbours", [(3, 1), (1, 0)], BF16)
+    direct3, direct1 = project(*operands, "neighbours", [[(3, 1)], [(1, 0)]], BF16)
     direct3, direct1 = swap(direct3, 3), swap(direct1, 1)
-    mine3, mine1 = project(*operands, "joining", [(3, 0), (1, 1)], F32)
-    (kept,) = project(*operands, "kept", [(0, None)], F32)
+    mine3, mine1 = project(*operands, "joining", [[(3, 0)], [(1, 1)]], F32)
+    (kept,) = project(*operands, "kept", [[(0, 0), (0, 1)]], F32)
     joined1 = swap(relay(over3, mine1), 1)
     joined3 = swap(relay(over1, mine3), 3)
-    return finish(kept, direct1, joined3, direct3, joined1)
+    return finish(kept, direct1, direct3, joined1, joined3, order)
 
 
 def solution(mesh):

time: 46.1 us -> 44.3 us (0.961)
  waiting for transfers between devices: 14 us -> 10.6 us
  starting transfers between devices: 21.2 us -> 22.7 us
    ppermute x6, waiting for transfers between devices: 7.15 us -> 4.27 us  [swap(): return lax.ppermute(value, 'ch', [(i, i ^ 2 * k) for i in range(n_ch)])]
    ppermute x6, starting transfers between devices: 6.96 us -> 8.42 us  [swap(): return lax.ppermute(value, 'ch', [(i, i ^ 2 * k) for i in range(n_ch)])]
    ppermute x1, waiting for transfers between devices: 1.52 us -> 0.81 us  [per_device(): other = lax.ppermute(own, 'ch', sibling)]
    pallas_call x13 -> x14, Pallas kernels: 10.5 us -> 10.7 us  [run(): pl.pallas_call(kernel, in_specs=[pl.BlockSpec(memory_space=space) for spa...]
  transfers between devices with their start and end apart: 15 -> 15, of which waited for: 10 -> 9; matrix products, arithmetic and copies ran while one was open for 0% -> 0% of each run, Pallas kernels for 20% -> 15%
where the time goes in v2:
time: 44.3 us; the launch traced here: 44.2 us
  starting transfers between devices  22.7 us (51%)
  Pallas kernels  10.7 us (24%)
  waiting for transfers between devices  10.6 us (24%)
    ppermute x7, starting transfers between devices, across(): return lax.ppermute(value, 'ctx', [(i, i ^ by) for i in range(n_ctx)])  14.1 us
    pallas_call x14, Pallas kernels, run(): pl.pallas_call(kernel, in_specs=[pl.BlockSpec(memory_space=space) for spa...  10.7 us
    ppermute x6, starting transfers between devices, swap(): return lax.ppermute(value, 'ch', [(i, i ^ 2 * k) for i in range(n_ch)])  8.42 us
    ppermute x7, waiting for transfers between devices, across(): return lax.ppermute(value, 'ctx', [(i, i ^ by) for i in range(n_ctx)])  5.5 us
    ppermute x6, waiting for transfers between devices, swap(): return lax.ppermute(value, 'ch', [(i, i ^ 2 * k) for i in range(n_ch)])  4.27 us
  transfers between devices with their start and end apart: 15, of which 9 were waited for; matrix products, arithmetic and copies ran while one was open for 0% of the time, Pallas kernels for 15%

profile of v2, /device:TPU:32, one launch (start us, length us, event | category | flops | bytes accessed | tf_op | source)
XLA Modules:
  0.0 44.2 jit_solution(13734063703940394600)
XLA Ops:
  0.0 2.6 %states.1 = (bf16[32,512]{1,0:T(8,128)(2,1)S(1)}, f32[256,512]{1,0:T(8,128)S(1)}, f32[16,512]{1,0:T(8,128)S(1)}, f32[4,16,512]{2,1,0:T(8,128)S(1)}, f32[2,16,512...) custom-call(bf16[512,256]{1,0:T(8,128)(2,1)} %key_hbm.1, bf16[512,256]{1,0:T(8,128)(2,1)} %value_hbm.1, ...), custom_call_target="tpu_custom_call" | custom-call | tf_op jit(solution)/shard_map/states/pallas_call | solution.py:37
  2.6 2.0 %collective-permute-start = (bf16[32,512]{1,0:T(8,128)(2,1)S(1)}, bf16[32,512]{1,0:T(8,128)(2,1)S(1)}, u32[]{:S(2)}, u32[]{:S(2)}) collective-permute-start(bf16[32,512]{1,0:T(8,128)(2,1)S(1)} %get-tuple-element.29.after.mine), channel_id=1, source_target_pairs={{0,24},{8,16},{16,8},{24,0},{32,56},{40,48},{48,40},{56,32},{64,88... | collective-permute-start | bytes 98312 | tf_op jit(solution)/shard_map/ppermute | solution.py:614
  4.6 2.3 %collective-permute-start.1 = (bf16[32,512]{1,0:T(8,128)(2,1)S(1)}, bf16[32,512]{1,0:T(8,128)(2,1)S(1)}, u32[]{:S(2)}, u32[]{:S(2)}) collective-permute-start(bf16[32,512]{1,0:T(8,128)(2,1)S(1)} %get-tuple-element.29.after.mine), channel_id=1, source_target_pairs={{0,16},{8,24},{16,0},{24,8},{32,48},{40,56},{48,32},{56,40},{64,80... | collective-permute-start | bytes 98312 | tf_op jit(solution)/shard_map/ppermute | solution.py:614
  6.9 0.5 %collective-permute-start.2 = (bf16[32,512]{1,0:T(8,128)(2,1)S(1)}, bf16[32,512]{1,0:T(8,128)(2,1)S(1)}, u32[]{:S(2)}, u32[]{:S(2)}) collective-permute-start(bf16[32,512]{1,0:T(8,128)(2,1)S(1)} %get-tuple-element.29.after.mine), channel_id=1, source_target_pairs={{0,8},{8,0},{16,24},{24,16},{32,40},{40,32},{48,56},{56,48},{64,72... | collective-permute-start | bytes 98312 | tf_op jit(solution)/shard_map/ppermute | solution.py:614
  7.4 2.7 %local_scan.1 = (f32[256,512]{1,0:T(8,128)S(1)}, f32[256,512]{1,0:T(8,128)S(1)}, f32[128,512]{1,0:T(8,128)S(1)}, f32[128,512]{1,0:T(8,128)S(1)}, f32[29,16,512]{2,1,0:T(8,128)S(1)}) custom-call(f32[256,512]{1,0:T(8,128)S(1)} %get-tuple-element.31.gated, bf16[512,256]{1,0:T(8,128)(2,1)} %query_hbm.3, f32[16,512]{1,0:T(8,128)S(1)} %get-tuple-element.30.params, ...), custom_call_target="tpu_custom_call" | custom-call | tf_op jit(solution)/shard_map/local_scan/pallas_call | solution.py:37
  10.1 0.0 collective-permute-done.three
  10.1 0.0 collective-permute-done.1.two
  10.1 0.7 %collective-permute-done.2.one = bf16[32,512]{1,0:T(8,128)(2,1)S(1)} collective-permute-done((bf16[32,512]{1,0:T(8,128)(2,1)S(1)}, bf16[32,512]{1,0:T(8,128)(2,1)S(1)}, u32[]{:S(2)}, u32[]{:S(2)}) %collective-permute-start.2) | collective-permute-done | bytes 32800 | tf_op jit(solution)/shard_map/ppermute | solution.py:614
  10.8 0.1 merge_four.1
  10.9 0.1 collective-permute-start.8
  11.0 5.1 %collective-permute-start.3 = (bf16[32,512]{1,0:T(8,128)(2,1)S(1)}, bf16[32,512]{1,0:T(8,128)(2,1)S(1)}, u32[]{:S(2)}, u32[]{:S(2)}) collective-permute-start(bf16[32,512]{1,0:T(8,128)(2,1)S(1)} %get-tuple-element.37.after.mine), channel_id=1, source_target_pairs={{0,56},{8,48},{16,40},{24,32},{32,24},{40,16},{48,8},{56,0},{64,12... | collective-permute-start | bytes 98312 | tf_op jit(solution)/shard_map/ppermute | solution.py:614
  16.1 1.6 %weight_blocks.1.after.weight = bf16[512,2048]{1,0:T(8,128)(2,1)S(1)} custom-call(bf16[512,4096]{1,0:T(8,128)(2,1)} %weight_hbm.1, bf16[32,512]{1,0:T(8,128)(2,1)S(1)} %get-tuple-element.37.after.mine), custom_call_target="tpu_custom_call" | custom-call | tf_op jit(solution)/shard_map/weight_blocks/pallas_call | solution.py:37
  17.7 0.5 %collective-permute-done.3.theirs = bf16[32,512]{1,0:T(8,128)(2,1)S(1)} collective-permute-done((bf16[32,512]{1,0:T(8,128)(2,1)S(1)}, bf16[32,512]{1,0:T(8,128)(2,1)S(1)}, u32[]{:S(2)}, u32[]{:S(2)}) %collective-permute-start.3) | collective-permute-done | bytes 32800 | tf_op jit(solution)/shard_map/ppermute | solution.py:614
  18.2 3.1 %collective-permute-start.4 = (bf16[32,512]{1,0:T(8,128)(2,1)S(1)}, bf16[32,512]{1,0:T(8,128)(2,1)S(1)}, u32[]{:S(2)}, u32[]{:S(2)}) collective-permute-start(bf16[32,512]{1,0:T(8,128)(2,1)S(1)} %get-tuple-element.40.mine), channel_id=1, source_target_pairs={{0,192},{8,200},{16,208},{24,216},{32,224},{40,232},{48,240},{56,2... | collective-permute-start | bytes 98312 | tf_op jit(solution)/shard_map/ppermute | solution.py:614
  21.3 0.6 %collective-permute-start.5 = (bf16[32,512]{1,0:T(8,128)(2,1)S(1)}, bf16[32,512]{1,0:T(8,128)(2,1)S(1)}, u32[]{:S(2)}, u32[]{:S(2)}) collective-permute-start(bf16[32,512]{1,0:T(8,128)(2,1)S(1)} %get-tuple-element.40.mine), channel_id=1, source_target_pairs={{0,128},{8,136},{16,144},{24,152},{32,160},{40,168},{48,176},{56,1... | collective-permute-start | bytes 98312 | tf_op jit(solution)/shard_map/ppermute | solution.py:614
  21.9 0.4 %collective-permute-start.6 = (bf16[32,512]{1,0:T(8,128)(2,1)S(1)}, bf16[32,512]{1,0:T(8,128)(2,1)S(1)}, u32[]{:S(2)}, u32[]{:S(2)}) collective-permute-start(bf16[32,512]{1,0:T(8,128)(2,1)S(1)} %get-tuple-element.40.mine), channel_id=1, source_target_pairs={{0,64},{8,72},{16,80},{24,88},{32,96},{40,104},{48,112},{56,120},{... | collective-permute-start | bytes 98312 | tf_op jit(solution)/shard_map/ppermute | solution.py:614
  22.4 1.0 %collective-permute-done.4.row3 = bf16[32,512]{1,0:T(8,128)(2,1)S(1)} collective-permute-done((bf16[32,512]{1,0:T(8,128)(2,1)S(1)}, bf16[32,512]{1,0:T(8,128)(2,1)S(1)}, u32[]{:S(2)}, u32[]{:S(2)}) %collective-permute-start.4) | collective-permute-done | bytes 32800 | tf_op jit(solution)/shard_map/ppermute | solution.py:614
  23.4 3.3 %collective-permute-done.5.row2 = bf16[32,512]{1,0:T(8,128)(2,1)S(1)} collective-permute-done((bf16[32,512]{1,0:T(8,128)(2,1)S(1)}, bf16[32,512]{1,0:T(8,128)(2,1)S(1)}, u32[]{:S(2)}, u32[]{:S(2)}) %collective-permute-start.5) | collective-permute-done | bytes 32800 | tf_op jit(solution)/shard_map/ppermute | solution.py:614
  26.7 0.0 collective-permute-done.6.row1
  26.7 0.8 %gated.1.mine = bf16[256,512]{1,0:T(8,128)(2,1)S(1)} custom-call(bf16[32,512]{1,0:T(8,128)(2,1)S(1)} %get-tuple-element.40.mine, bf16[32,512]{1,0:T(8,128)(2,1)S(1)} %collective-permute-done.4.row3, bf16[32,512]{1,0:T(8,128)(2,1)S(1)} %collective-permute-done.5.row2, bf16[32,512]{1,0:T(8,128)(2,1)S(1)} %collective-permute-done.6.row1, ...), custom_call_target="tpu_custom_call" | custom-call | tf_op jit(solution)/shard_map/gated/pallas_call | solution.py:37
  27.5 0.1 collective-permute-start.7
  27.6 0.7 %near_sums.1.near_ref = f32[256,2048]{1,0:T(8,128)S(1)} custom-call(bf16[256,512]{1,0:T(8,128)(2,1)S(1)} %gated.1.mine, bf16[512,2048]{1,0:T(8,128)(2,1)S(1)} %weight_blocks.1.after.weight), custom_call_target="tpu_custom_call" | custom-call | tf_op jit(solution)/shard_map/near_sums/pallas_call | solution.py:37
  28.3 0.8 %collective-permute-done.7.other_ref = bf16[256,512]{1,0:T(8,128)(2,1)S(1)} collective-permute-done((bf16[256,512]{1,0:T(8,128)(2,1)S(1)}, bf16[256,512]{1,0:T(8,128)(2,1)S(1)}, u32[]{:S(2)}, u32[]{:S(2)}) %collective-permute-start.7) | collective-permute-done | bytes 262176 | tf_op jit(solution)/shard_map/ppermute | solution.py:629
  29.1 0.0 collective-permute-done.8.far_ref
  29.1 0.3 opposite.1
  29.5 1.6 %collective-permute-start.13 = (bf16[128,512]{1,0:T(8,128)(2,1)S(1)}, bf16[128,512]{1,0:T(8,128)(2,1)S(1)}, u32[]{:S(2)}, u32[]{:S(2)}) collective-permute-start(bf16[128,512]{1,0:T(8,128)(2,1)S(1)} %get-tuple-element.51), channel_id=1, source_target_pairs={{0,2},{1,3},{2,0},{3,1},{4,6},{5,7},{6,4},{7,5},{8,10},{9,11},{10,... | collective-permute-start | bytes 393224 | tf_op jit(solution)/shard_map/ppermute | solution.py:632
  31.0 2.1 %collective-permute-start.11 = (bf16[128,512]{1,0:T(8,128)(2,1)S(1)}, bf16[128,512]{1,0:T(8,128)(2,1)S(1)}, u32[]{:S(2)}, u32[]{:S(2)}) collective-permute-start(bf16[128,512]{1,0:T(8,128)(2,1)S(1)} %get-tuple-element.49), channel_id=1, source_target_pairs={{0,6},{1,7},{2,4},{3,5},{4,2},{5,3},{6,0},{7,1},{8,14},{9,15},{10,... | collective-permute-start | bytes 393224 | tf_op jit(solution)/shard_map/ppermute | solution.py:632
  33.1 0.3 neighbours.1
  33.5 1.2 %collective-permute-start.10 = (bf16[128,512]{1,0:T(8,128)(2,1)S(1)}, bf16[128,512]{1,0:T(8,128)(2,1)S(1)}, u32[]{:S(2)}, u32[]{:S(2)}) collective-permute-start(bf16[128,512]{1,0:T(8,128)(2,1)S(1)} %get-tuple-element.48), channel_id=1, source_target_pairs={{0,6},{1,7},{2,4},{3,5},{4,2},{5,3},{6,0},{7,1},{8,14},{9,15},{10,... | collective-permute-start | bytes 393224 | tf_op jit(solution)/shard_map/ppermute | solution.py:632
  34.7 0.0 collective-permute-start.9
  34.7 0.3 joining.1
  35.0 0.1 collective-permute-done.13.passing
  35.1 2.8 %collective-permute-start.14 = (bf16[128,512]{1,0:T(8,128)(2,1)S(1)}, bf16[128,512]{1,0:T(8,128)(2,1)S(1)}, u32[]{:S(2)}, u32[]{:S(2)}) collective-permute-start(bf16[128,512]{1,0:T(8,128)(2,1)S(1)} %relay.3), channel_id=1, source_target_pairs={{0,6},{1,7},{2,4},{3,5},{4,2},{5,3},{6,0},{7,1},{8,14},{9,15},{10,... | collective-permute-start | bytes 393224 | tf_op jit(solution)/shard_map/ppermute | solution.py:632
  38.0 0.1 collective-permute-done.11.passing
  38.1 0.7 %collective-permute-start.12 = (bf16[128,512]{1,0:T(8,128)(2,1)S(1)}, bf16[128,512]{1,0:T(8,128)(2,1)S(1)}, u32[]{:S(2)}, u32[]{:S(2)}) collective-permute-start(bf16[128,512]{1,0:T(8,128)(2,1)S(1)} %relay.2), channel_id=1, source_target_pairs={{0,2},{1,3},{2,0},{3,1},{4,6},{5,7},{6,4},{7,5},{8,10},{9,11},{10,... | collective-permute-start | bytes 393224 | tf_op jit(solution)/shard_map/ppermute | solution.py:632
  38.8 0.3 kept.1.own
  39.1 2.1 %collective-permute-done.10.direct3 = bf16[128,512]{1,0:T(8,128)(2,1)S(1)} collective-permute-done((bf16[128,512]{1,0:T(8,128)(2,1)S(1)}, bf16[128,512]{1,0:T(8,128)(2,1)S(1)}, u32[]{:S(2)}, u32[]{:S(2)}) %collective-permute-start.10) | collective-permute-done | bytes 131104 | tf_op jit(solution)/shard_map/ppermute | solution.py:632
  41.2 0.0 collective-permute-done.9.direct1
  41.2 1.9 %collective-permute-done.14.joined3 = bf16[128,512]{1,0:T(8,128)(2,1)S(1)} collective-permute-done((bf16[128,512]{1,0:T(8,128)(2,1)S(1)}, bf16[128,512]{1,0:T(8,128)(2,1)S(1)}, u32[]{:S(2)}, u32[]{:S(2)}) %collective-permute-start.14) | collective-permute-done | bytes 131104 | tf_op jit(solution)/shard_map/ppermute | solution.py:632
  43.1 0.0 collective-permute-done.12.joined1
  43.2 1.0 %finish.1 = bf16[512,256]{1,0:T(8,128)(2,1)} custom-call(f32[256,512]{1,0:T(8,128)S(1)} %kept.1.own, bf16[128,512]{1,0:T(8,128)(2,1)S(1)} %collective-permute-done.9.direct1, bf16[128,512]{1,0:T(8,128)(2,1)S(1)} %collective-permute-done.10.direct3, bf16[128,512]{1,0:T(8,128)(2,1)S(1)} %collective-permute-done.12.joined1, ...), custom_call_target="tpu_custom_call" | custom-call | tf_op jit(solution)/shard_map/finish/pallas_call | solution.py:37
  (3 shorter events, 0.1 us)
Async XLA Ops:
  2.6 7.5 %collective-permute-start = (bf16[32,512]{1,0:T(8,128)(2,1)S(1)}, bf16[32,512]{1,0:T(8,128)(2,1)S(1)}, u32[]{:S(2)}, u32[]{:S(2)}) collective-permute-start(bf16[32,512]{1,0:T(8,128)(2,1)S(1)} %get-tuple-element.29.after.mine), channel_id=1, source_target_pairs={{0,24},{8,16},{16,8},{24,0},{32,56},{40,48},{48,40},{56,32},{64,88... | collective-permute-start | bytes 98312 | tf_op jit(solution)/shard_map/ppermute | solution.py:614
  4.6 5.5 %collective-permute-start.1 = (bf16[32,512]{1,0:T(8,128)(2,1)S(1)}, bf16[32,512]{1,0:T(8,128)(2,1)S(1)}, u32[]{:S(2)}, u32[]{:S(2)}) collective-permute-start(bf16[32,512]{1,0:T(8,128)(2,1)S(1)} %get-tuple-element.29.after.mine), channel_id=1, source_target_pairs={{0,16},{8,24},{16,0},{24,8},{32,48},{40,56},{48,32},{56,40},{64,80... | collective-permute-start | bytes 98312 | tf_op jit(solution)/shard_map/ppermute | solution.py:614
  6.9 3.9 %collective-permute-start.2 = (bf16[32,512]{1,0:T(8,128)(2,1)S(1)}, bf16[32,512]{1,0:T(8,128)(2,1)S(1)}, u32[]{:S(2)}, u32[]{:S(2)}) collective-permute-start(bf16[32,512]{1,0:T(8,128)(2,1)S(1)} %get-tuple-element.29.after.mine), channel_id=1, source_target_pairs={{0,8},{8,0},{16,24},{24,16},{32,40},{40,32},{48,56},{56,48},{64,72... | collective-permute-start | bytes 98312 | tf_op jit(solution)/shard_map/ppermute | solution.py:614
  10.9 18.2 %collective-permute-start.8 = (bf16[512,4096]{1,0:T(8,128)(2,1)}, bf16[512,4096]{1,0:T(8,128)(2,1)S(1)}, u32[]{:S(2)}, u32[]{:S(2)}) collective-permute-start(bf16[512,4096]{1,0:T(8,128)(2,1)} %weight_hbm.1), channel_id=1, source_target_pairs={{0,1},{1,0},{2,3},{3,2},{4,5},{5,4},{6,7},{7,6},{8,9},{9,8},{10,11... | collective-permute-start | bytes 12582920 | tf_op jit(solution)/shard_map/ppermute | solution.py:622
  11.0 7.1 %collective-permute-start.3 = (bf16[32,512]{1,0:T(8,128)(2,1)S(1)}, bf16[32,512]{1,0:T(8,128)(2,1)S(1)}, u32[]{:S(2)}, u32[]{:S(2)}) collective-permute-start(bf16[32,512]{1,0:T(8,128)(2,1)S(1)} %get-tuple-element.37.after.mine), channel_id=1, source_target_pairs={{0,56},{8,48},{16,40},{24,32},{32,24},{40,16},{48,8},{56,0},{64,12... | collective-permute-start | bytes 98312 | tf_op jit(solution)/shard_map/ppermute | solution.py:614
  18.2 5.2 %collective-permute-start.4 = (bf16[32,512]{1,0:T(8,128)(2,1)S(1)}, bf16[32,512]{1,0:T(8,128)(2,1)S(1)}, u32[]{:S(2)}, u32[]{:S(2)}) collective-permute-start(bf16[32,512]{1,0:T(8,128)(2,1)S(1)} %get-tuple-element.40.mine), channel_id=1, source_target_pairs={{0,192},{8,200},{16,208},{24,216},{32,224},{40,232},{48,240},{56,2... | collective-permute-start | bytes 98312 | tf_op jit(solution)/shard_map/ppermute | solution.py:614
  21.3 5.4 %collective-permute-start.5 = (bf16[32,512]{1,0:T(8,128)(2,1)S(1)}, bf16[32,512]{1,0:T(8,128)(2,1)S(1)}, u32[]{:S(2)}, u32[]{:S(2)}) collective-permute-start(bf16[32,512]{1,0:T(8,128)(2,1)S(1)} %get-tuple-element.40.mine), channel_id=1, source_target_pairs={{0,128},{8,136},{16,144},{24,152},{32,160},{40,168},{48,176},{56,1... | collective-permute-start | bytes 98312 | tf_op jit(solution)/shard_map/ppermute | solution.py:614
  21.9 4.8 %collective-permute-start.6 = (bf16[32,512]{1,0:T(8,128)(2,1)S(1)}, bf16[32,512]{1,0:T(8,128)(2,1)S(1)}, u32[]{:S(2)}, u32[]{:S(2)}) collective-permute-start(bf16[32,512]{1,0:T(8,128)(2,1)S(1)} %get-tuple-element.40.mine), channel_id=1, source_target_pairs={{0,64},{8,72},{16,80},{24,88},{32,96},{40,104},{48,112},{56,120},{... | collective-permute-start | bytes 98312 | tf_op jit(solution)/shard_map/ppermute | solution.py:614
  27.5 1.6 %collective-permute-start.7 = (bf16[256,512]{1,0:T(8,128)(2,1)S(1)}, bf16[256,512]{1,0:T(8,128)(2,1)S(1)}, u32[]{:S(2)}, u32[]{:S(2)}) collective-permute-start(bf16[256,512]{1,0:T(8,128)(2,1)S(1)} %gated.1.mine), channel_id=1, source_target_pairs={{0,1},{1,0},{2,3},{3,2},{4,5},{5,4},{6,7},{7,6},{8,9},{9,8},{10,11... | collective-permute-start | bytes 786440 | tf_op jit(solution)/shard_map/ppermute | solution.py:629
  29.5 5.6 %collective-permute-start.13 = (bf16[128,512]{1,0:T(8,128)(2,1)S(1)}, bf16[128,512]{1,0:T(8,128)(2,1)S(1)}, u32[]{:S(2)}, u32[]{:S(2)}) collective-permute-start(bf16[128,512]{1,0:T(8,128)(2,1)S(1)} %get-tuple-element.51), channel_id=1, source_target_pairs={{0,2},{1,3},{2,0},{3,1},{4,6},{5,7},{6,4},{7,5},{8,10},{9,11},{10,... | collective-permute-start | bytes 393224 | tf_op jit(solution)/shard_map/ppermute | solution.py:632
  31.0 7.0 %collective-permute-start.11 = (bf16[128,512]{1,0:T(8,128)(2,1)S(1)}, bf16[128,512]{1,0:T(8,128)(2,1)S(1)}, u32[]{:S(2)}, u32[]{:S(2)}) collective-permute-start(bf16[128,512]{1,0:T(8,128)(2,1)S(1)} %get-tuple-element.49), channel_id=1, source_target_pairs={{0,6},{1,7},{2,4},{3,5},{4,2},{5,3},{6,0},{7,1},{8,14},{9,15},{10,... | collective-permute-start | bytes 393224 | tf_op jit(solution)/shard_map/ppermute | solution.py:632
  33.5 7.7 %collective-permute-start.10 = (bf16[128,512]{1,0:T(8,128)(2,1)S(1)}, bf16[128,512]{1,0:T(8,128)(2,1)S(1)}, u32[]{:S(2)}, u32[]{:S(2)}) collective-permute-start(bf16[128,512]{1,0:T(8,128)(2,1)S(1)} %get-tuple-element.48), channel_id=1, source_target_pairs={{0,6},{1,7},{2,4},{3,5},{4,2},{5,3},{6,0},{7,1},{8,14},{9,15},{10,... | collective-permute-start | bytes 393224 | tf_op jit(solution)/shard_map/ppermute | solution.py:632
  34.7 6.5 %collective-permute-start.9 = (bf16[128,512]{1,0:T(8,128)(2,1)S(1)}, bf16[128,512]{1,0:T(8,128)(2,1)S(1)}, u32[]{:S(2)}, u32[]{:S(2)}) collective-permute-start(bf16[128,512]{1,0:T(8,128)(2,1)S(1)} %get-tuple-element.47), channel_id=1, source_target_pairs={{0,2},{1,3},{2,0},{3,1},{4,6},{5,7},{6,4},{7,5},{8,10},{9,11},{10,... | collective-permute-start | bytes 393224 | tf_op jit(solution)/shard_map/ppermute | solution.py:632
  35.1 8.0 %collective-permute-start.14 = (bf16[128,512]{1,0:T(8,128)(2,1)S(1)}, bf16[128,512]{1,0:T(8,128)(2,1)S(1)}, u32[]{:S(2)}, u32[]{:S(2)}) collective-permute-start(bf16[128,512]{1,0:T(8,128)(2,1)S(1)} %relay.3), channel_id=1, source_target_pairs={{0,6},{1,7},{2,4},{3,5},{4,2},{5,3},{6,0},{7,1},{8,14},{9,15},{10,... | collective-permute-start | bytes 393224 | tf_op jit(solution)/shard_map/ppermute | solution.py:632
  38.1 5.1 %collective-permute-start.12 = (bf16[128,512]{1,0:T(8,128)(2,1)S(1)}, bf16[128,512]{1,0:T(8,128)(2,1)S(1)}, u32[]{:S(2)}, u32[]{:S(2)}) collective-permute-start(bf16[128,512]{1,0:T(8,128)(2,1)S(1)} %relay.2), channel_id=1, source_target_pairs={{0,2},{1,3},{2,0},{3,1},{4,6},{5,7},{6,4},{7,5},{8,10},{9,11},{10,... | collective-permute-start | bytes 393224 | tf_op jit(solution)/shard_map/ppermute | solution.py:632

commit v3 on v2

--- a/solution.py
+++ b/solution.py
@@ -71,7 +71,7 @@
     return here // ROW, lax.rem(here, ROW)
 
 
-def fill_tables(basis, modes, span, tables):
+def tables_kernel(span, basis, modes, tables):
     y, z = place_of()
     damping, residue = modes[0], modes[1]
 
@@ -111,6 +111,11 @@
         tables[OVER_Y + 3 + s] = only((y >= s + 1) & (ahead > 0), fade(seen))
 
 
+def make_tables(span, basis, modes):
+    out = jax.ShapeDtypeStruct((TABLES, *basis.shape[1:]), F32)
+    return call(lambda *refs: tables_kernel(span, *refs), "tables", out)(basis, modes)
+
+
 def states_kernel(
     key_hbm,
     value_hbm,
@@ -132,6 +137,7 @@
     streams,
     state,
     edges,
+    start_fade,
     sems,
 ):
     channels, span = key_hbm.shape
@@ -163,16 +169,27 @@
     segment = segment_index()
     params[...] = jnp.zeros_like(params)
     edges[...] = jnp.zeros_like(edges)
-    for c in fixed[:2]:
+    for c in big + fixed:
         c.wait()
+    for s in range(2):
+        streams[s] = lax.dot_general(order[...], raw[s], NT, preferred_element_type=F32)
     basis[DECAY] = jnp.exp(-modes[0])
     for i in range(3):
         basis[FADE + i] = jnp.exp(-modes[0] * float(steps << i))
+    start_fade[...] = jnp.exp(-modes[0] * float(span - 2))
     for i in range(9):
         params[i : i + 1, :] = taps_in[(1 + i // 3) % 3, i % 3, :][None, :]
+    params[SKIP : SKIP + 1, :] = skip[...]
     for s in range(2):
-        big[s].wait()
-        streams[s] = lax.dot_general(order[...], raw[s], NT, preferred_element_type=F32)
+        edges[2 * s : 2 * s + 1, :] = streams[s, 0:1, :]
+        edges[2 * s + 1 : 2 * s + 2, :] = streams[s, SEGMENTS : SEGMENTS + 1, :]
+        edges[4 + 2 * s : 5 + 2 * s, :] = streams[s, span - SEGMENTS - 1 : span - SEGMENTS, :]
+        edges[5 + 2 * s : 6 + 2 * s, :] = streams[s, span - 1 : span, :]
+    row = lax.broadcasted_iota(jnp.int32, (8, LANES), 0)
+    col = lax.broadcasted_iota(jnp.int32, (8, LANES), 1)
+    pick = jnp.where(col == LANES - 2 + row, 1.0, 0.0).astype(BF16)
+    edges[8:16, :] = lax.dot_general(pick, tail[...], NT, preferred_element_type=F32)
+    message[EDGES:, :] = edges[...].astype(BF16)
 
     def group(lanes):
         taps = [params[i : i + 1, lanes] for i in range(6)]
@@ -209,23 +226,9 @@
 
     by_group(channels, group)
     at = lambda i: params[FIRST + i : FIRST + i + 1, :]
-    start_fade = jnp.exp(-modes[0] * float(span - 2))
-    start = start_fade * (basis[DECAY] * (at(0) * at(2)) + at(1) * at(3))
+    start = start_fade[...] * (basis[DECAY] * (at(0) * at(2)) + at(1) * at(3))
     total = state[...] + jnp.where(lax.axis_index("ctx") == 0, start, 0.0)
     message[0:ORDER, :] = total.astype(BF16)
-    for c in fixed[2:]:
-        c.wait()
-    params[SKIP : SKIP + 1, :] = skip[...]
-    for s in range(2):
-        edges[2 * s : 2 * s + 1, :] = streams[s, 0:1, :]
-        edges[2 * s + 1 : 2 * s + 2, :] = streams[s, SEGMENTS : SEGMENTS + 1, :]
-        edges[4 + 2 * s : 5 + 2 * s, :] = streams[s, span - SEGMENTS - 1 : span - SEGMENTS, :]
-        edges[5 + 2 * s : 6 + 2 * s, :] = streams[s, span - 1 : span, :]
-    row = lax.broadcasted_iota(jnp.int32, (8, LANES), 0)
-    col = lax.broadcasted_iota(jnp.int32, (8, LANES), 1)
-    pick = jnp.where(col == LANES - 2 + row, 1.0, 0.0).astype(BF16)
-    edges[8:16, :] = lax.dot_general(pick, tail[...], NT, preferred_element_type=F32)
-    message[EDGES:, :] = edges[...].astype(BF16)
 
 
 def states(key_in, value_in, query_in, taps, damping, residue, skip):
@@ -247,6 +250,7 @@
         pltpu.VMEM((2, span, channels), F32),
         pltpu.VMEM((ORDER, channels), F32),
         pltpu.VMEM((16, channels), F32),
+        pltpu.VMEM((ORDER, channels), F32),
         pltpu.SemaphoreType.DMA((7,)),
     ]
     return call(states_kernel, "states", out, scratch, outside=range(7))(
@@ -258,15 +262,13 @@
     gated,
     query_hbm,
     params,
-    basis,
-    modes,
+    tables,
     order,
     after,
     local,
     gate,
     carry,
     reach,
-    tables,
     raw,
     stream,
     sem,
@@ -275,7 +277,6 @@
     steps = span // SEGMENTS
     copy = pltpu.make_async_copy(query_hbm, raw, sem)
     copy.start()
-    fill_tables(basis, modes, span, tables)
     copy.wait()
     stream[...] = lax.dot_general(order[...], raw[...], NT, preferred_element_type=F32)
     segment = segment_index()
@@ -320,7 +321,7 @@
     by_group(channels, group)
 
 
-def local_scan(gated, query_in, params, basis, modes, order, after):
+def local_scan(gated, query_in, params, tables, order, after):
     channels, span = query_in.shape
     shape = jax.ShapeDtypeStruct
     out = [
@@ -328,15 +329,14 @@
         shape((span, channels), F32),
         shape((ORDER * SEGMENTS, channels), F32),
         shape((ORDER * SEGMENTS, channels), F32),
-        shape((TABLES, ORDER, channels), F32),
     ]
     scratch = [
         pltpu.VMEM((channels, span), BF16),
         pltpu.VMEM((span, channels), F32),
         pltpu.SemaphoreType.DMA,
     ]
-    return call(local_kernel, "local_scan", out, scratch, outside=(1,), unread=(6,))(
-        gated, query_in, params, basis, modes, order, after
+    return call(local_kernel, "local_scan", out, scratch, outside=(1,), unread=(5,))(
+        gated, query_in, params, tables, order, after
     )
 
 
@@ -373,7 +373,7 @@
     message[EDGES:, :] = jnp.where(row < 4, first, last).astype(BF16)
 
 
-def merge_four_kernel(mine, three, two, one, params, tables, after, message, before, border):
+def merge_four_kernel(mine, three, two, one, params, tables, message, before, border):
     _, z = place_of()
     place = z & (FOUR - 1)
     blocks = in_order(place, unpack(mine), [unpack(m) for m in (one, two, three)])
@@ -394,13 +394,11 @@
     border[...] = last
 
 
-def merge_four(mine, swapped, params, tables, after):
+def merge_four(mine, swapped, params, tables):
     channels = mine.shape[1]
     shape = jax.ShapeDtypeStruct
     out = [shape(mine.shape, BF16), shape((ORDER, channels), F32), shape((16, channels), F32)]
-    return call(merge_four_kernel, "merge_four", out, unread=(6,))(
-        mine, *swapped, params, tables, after
-    )
+    return call(merge_four_kernel, "merge_four", out)(mine, *swapped, params, tables)
 
 
 def merge_pair_kernel(
@@ -432,8 +430,8 @@
 
 def gate_kernel(
     mine,
+    row2,
     row3,
-    row2,
     row1,
     before_in,
     border_in,
@@ -614,16 +612,15 @@
         return lax.ppermute(value, "ctx", [(i, i ^ by) for i in range(n_ctx)])
 
     swapped = [across(message, k) for k in (3, 2, 1)]
-    local, gate, carry, reach, tables = local_scan(
-        gated, query_in, params, basis, modes, order, message
-    )
-    message, before, border = merge_four(message, swapped, params, tables, local)
+    tables = make_tables(query_in.shape[1], basis, modes)
+    message, before, border = merge_four(message, swapped, params, tables)
     later, _ = lax.optimization_barrier((out_weight, message))
     far = lax.ppermute(later, "ch", sibling)
     theirs = across(message, PAIR)
     weight = weight_blocks(out_weight, message)
     message, before, border = merge_pair(message, theirs, before, border, params, tables, weight)
-    messages = [message] + [across(message, k * ROW) for k in (3, 2, 1)]
+    local, gate, carry, reach = local_scan(gated, query_in, params, tables, order, message)
+    messages = [message] + [across(message, k * ROW) for k in (2, 3, 1)]
 
     own = gate_all(messages, before, border, local, gate, carry, reach, params, tables)
     other = lax.ppermute(own, "ch", sibling)

time: 44.3 us -> 44 us (level)
  waiting for transfers between devices: 10.6 us -> 10.1 us
    ppermute x7, waiting for transfers between devices: 5.5 us -> 5.03 us  [across(): return lax.ppermute(value, 'ctx', [(i, i ^ by) for i in range(n_ctx)])]
    pallas_call x14 -> x15, Pallas kernels: 10.7 us -> 10.7 us  [run(): pl.pallas_call(kernel, in_specs=[pl.BlockSpec(memory_space=space) for spa...]
  transfers between devices with their start and end apart: 15 -> 15, of which waited for: 9 -> 9; matrix products, arithmetic and copies ran while one was open for 0% -> 0% of each run, Pallas kernels for 15% -> 16%
where the time goes in v3:
time: 44 us; the launch traced here: 43.8 us
  starting transfers between devices  22.9 us (52%)
  Pallas kernels  10.7 us (24%)
  waiting for transfers between devices  10.1 us (23%)
    ppermute x7, starting transfers between devices, across(): return lax.ppermute(value, 'ctx', [(i, i ^ by) for i in range(n_ctx)])  14.3 us
    pallas_call x15, Pallas kernels, run(): pl.pallas_call(kernel, in_specs=[pl.BlockSpec(memory_space=space) for spa...  10.7 us
    ppermute x6, starting transfers between devices, swap(): return lax.ppermute(value, 'ch', [(i, i ^ 2 * k) for i in range(n_ch)])  8.4 us
    ppermute x7, waiting for transfers between devices, across(): return lax.ppermute(value, 'ctx', [(i, i ^ by) for i in range(n_ctx)])  5.03 us
    ppermute x6, waiting for transfers between devices, swap(): return lax.ppermute(value, 'ch', [(i, i ^ 2 * k) for i in range(n_ch)])  4.29 us
  transfers between devices with their start and end apart: 15, of which 9 were waited for; matrix products, arithmetic and copies ran while one was open for 0% of the time, Pallas kernels for 16%

profile of v3, /device:TPU:32, one launch (start us, length us, event | category | flops | bytes accessed | tf_op | source)
XLA Modules:
  0.0 43.8 jit_solution(16929515187482594451)
XLA Ops:
  0.0 2.4 %states.1 = (bf16[32,512]{1,0:T(8,128)(2,1)S(1)}, f32[256,512]{1,0:T(8,128)S(1)}, f32[16,512]{1,0:T(8,128)S(1)}, f32[4,16,512]{2,1,0:T(8,128)S(1)}, f32[2,16,512...) custom-call(bf16[512,256]{1,0:T(8,128)(2,1)} %key_hbm.1, bf16[512,256]{1,0:T(8,128)(2,1)} %value_hbm.1, ...), custom_call_target="tpu_custom_call" | custom-call | tf_op jit(solution)/shard_map/states/pallas_call | solution.py:37
  2.4 2.0 %collective-permute-start = (bf16[32,512]{1,0:T(8,128)(2,1)S(1)}, bf16[32,512]{1,0:T(8,128)(2,1)S(1)}, u32[]{:S(2)}, u32[]{:S(2)}) collective-permute-start(bf16[32,512]{1,0:T(8,128)(2,1)S(1)} %get-tuple-element.28.mine), channel_id=1, source_target_pairs={{0,24},{8,16},{16,8},{24,0},{32,56},{40,48},{48,40},{56,32},{64,88... | collective-permute-start | bytes 98312 | tf_op jit(solution)/shard_map/ppermute | solution.py:612
  4.4 2.3 %collective-permute-start.1 = (bf16[32,512]{1,0:T(8,128)(2,1)S(1)}, bf16[32,512]{1,0:T(8,128)(2,1)S(1)}, u32[]{:S(2)}, u32[]{:S(2)}) collective-permute-start(bf16[32,512]{1,0:T(8,128)(2,1)S(1)} %get-tuple-element.28.mine), channel_id=1, source_target_pairs={{0,16},{8,24},{16,0},{24,8},{32,48},{40,56},{48,32},{56,40},{64,80... | collective-permute-start | bytes 98312 | tf_op jit(solution)/shard_map/ppermute | solution.py:612
  6.7 0.5 %collective-permute-start.2 = (bf16[32,512]{1,0:T(8,128)(2,1)S(1)}, bf16[32,512]{1,0:T(8,128)(2,1)S(1)}, u32[]{:S(2)}, u32[]{:S(2)}) collective-permute-start(bf16[32,512]{1,0:T(8,128)(2,1)S(1)} %get-tuple-element.28.mine), channel_id=1, source_target_pairs={{0,8},{8,0},{16,24},{24,16},{32,40},{40,32},{48,56},{56,48},{64,72... | collective-permute-start | bytes 98312 | tf_op jit(solution)/shard_map/ppermute | solution.py:612
  7.2 0.1 tables.1
  7.4 0.0 collective-permute-done.three
  7.4 2.0 %collective-permute-done.1.two = bf16[32,512]{1,0:T(8,128)(2,1)S(1)} collective-permute-done((bf16[32,512]{1,0:T(8,128)(2,1)S(1)}, bf16[32,512]{1,0:T(8,128)(2,1)S(1)}, u32[]{:S(2)}, u32[]{:S(2)}) %collective-permute-start.1) | collective-permute-done | bytes 32800 | tf_op jit(solution)/shard_map/ppermute | solution.py:612
  9.3 1.3 %collective-permute-done.2.one = bf16[32,512]{1,0:T(8,128)(2,1)S(1)} collective-permute-done((bf16[32,512]{1,0:T(8,128)(2,1)S(1)}, bf16[32,512]{1,0:T(8,128)(2,1)S(1)}, u32[]{:S(2)}, u32[]{:S(2)}) %collective-permute-start.2) | collective-permute-done | bytes 32800 | tf_op jit(solution)/shard_map/ppermute | solution.py:612
  10.6 0.1 merge_four.1
  10.7 0.1 collective-permute-start.8
  10.8 5.1 %collective-permute-start.3 = (bf16[32,512]{1,0:T(8,128)(2,1)S(1)}, bf16[32,512]{1,0:T(8,128)(2,1)S(1)}, u32[]{:S(2)}, u32[]{:S(2)}) collective-permute-start(bf16[32,512]{1,0:T(8,128)(2,1)S(1)} %get-tuple-element.32.after.mine), channel_id=1, source_target_pairs={{0,56},{8,48},{16,40},{24,32},{32,24},{40,16},{48,8},{56,0},{64,12... | collective-permute-start | bytes 98312 | tf_op jit(solution)/shard_map/ppermute | solution.py:612
  15.9 1.6 %weight_blocks.1.after.weight = bf16[512,2048]{1,0:T(8,128)(2,1)S(1)} custom-call(bf16[512,4096]{1,0:T(8,128)(2,1)} %weight_hbm.1, bf16[32,512]{1,0:T(8,128)(2,1)S(1)} %get-tuple-element.32.after.mine), custom_call_target="tpu_custom_call" | custom-call | tf_op jit(solution)/shard_map/weight_blocks/pallas_call | solution.py:37
  17.5 0.4 collective-permute-done.3.theirs
  17.9 3.3 %collective-permute-start.4 = (bf16[32,512]{1,0:T(8,128)(2,1)S(1)}, bf16[32,512]{1,0:T(8,128)(2,1)S(1)}, u32[]{:S(2)}, u32[]{:S(2)}) collective-permute-start(bf16[32,512]{1,0:T(8,128)(2,1)S(1)} %get-tuple-element.35.after.mine), channel_id=1, source_target_pairs={{0,128},{8,136},{16,144},{24,152},{32,160},{40,168},{48,176},{56,1... | collective-permute-start | bytes 98312 | tf_op jit(solution)/shard_map/ppermute | solution.py:612
  21.2 1.1 %collective-permute-start.5 = (bf16[32,512]{1,0:T(8,128)(2,1)S(1)}, bf16[32,512]{1,0:T(8,128)(2,1)S(1)}, u32[]{:S(2)}, u32[]{:S(2)}) collective-permute-start(bf16[32,512]{1,0:T(8,128)(2,1)S(1)} %get-tuple-element.35.after.mine), channel_id=1, source_target_pairs={{0,192},{8,200},{16,208},{24,216},{32,224},{40,232},{48,240},{56,2... | collective-permute-start | bytes 98312 | tf_op jit(solution)/shard_map/ppermute | solution.py:612
  22.3 0.0 collective-permute-start.6
  22.3 2.7 %local_scan.1 = (f32[256,512]{1,0:T(8,128)S(1)}, f32[256,512]{1,0:T(8,128)S(1)}, f32[128,512]{1,0:T(8,128)S(1)}, f32[128,512]{1,0:T(8,128)S(1)}) custom-call(f32[256,512]{1,0:T(8,128)S(1)} %get-tuple-element.38.gated, bf16[512,256]{1,0:T(8,128)(2,1)} %query_hbm.3, f32[16,512]{1,0:T(8,128)S(1)} %get-tuple-element.29.params, f32[29,16,512]{2,1,0:T(8,128)S(1)} %tables.1, ...), custom_call_target="tpu_custom_call" | custom-call | tf_op jit(solution)/shard_map/local_scan/pallas_call | solution.py:37
  25.0 0.0 collective-permute-done.4.row2
  25.0 1.4 %collective-permute-done.5.row3 = bf16[32,512]{1,0:T(8,128)(2,1)S(1)} collective-permute-done((bf16[32,512]{1,0:T(8,128)(2,1)S(1)}, bf16[32,512]{1,0:T(8,128)(2,1)S(1)}, u32[]{:S(2)}, u32[]{:S(2)}) %collective-permute-start.5) | collective-permute-done | bytes 32800 | tf_op jit(solution)/shard_map/ppermute | solution.py:612
  26.4 0.0 collective-permute-done.6.row1
  26.4 0.8 %gated.1.mine = bf16[256,512]{1,0:T(8,128)(2,1)S(1)} custom-call(bf16[32,512]{1,0:T(8,128)(2,1)S(1)} %get-tuple-element.35.after.mine, bf16[32,512]{1,0:T(8,128)(2,1)S(1)} %collective-permute-done.4.row2, bf16[32,512]{1,0:T(8,128)(2,1)S(1)} %collective-permute-done.5.row3, bf16[32,512]{1,0:T(8,128)(2,1)S(1)} %collective-permute-done.6.row1, ...), custom_call_target="tpu_custom_call" | custom-call | tf_op jit(solution)/shard_map/gated/pallas_call | solution.py:37
  27.1 0.1 collective-permute-start.7
  27.2 0.7 %near_sums.1.near_ref = f32[256,2048]{1,0:T(8,128)S(1)} custom-call(bf16[256,512]{1,0:T(8,128)(2,1)S(1)} %gated.1.mine, bf16[512,2048]{1,0:T(8,128)(2,1)S(1)} %weight_blocks.1.after.weight), custom_call_target="tpu_custom_call" | custom-call | tf_op jit(solution)/shard_map/near_sums/pallas_call | solution.py:37
  28.0 0.8 %collective-permute-done.7.other_ref = bf16[256,512]{1,0:T(8,128)(2,1)S(1)} collective-permute-done((bf16[256,512]{1,0:T(8,128)(2,1)S(1)}, bf16[256,512]{1,0:T(8,128)(2,1)S(1)}, u32[]{:S(2)}, u32[]{:S(2)}) %collective-permute-start.7) | collective-permute-done | bytes 262176 | tf_op jit(solution)/shard_map/ppermute | solution.py:626
  28.8 0.0 collective-permute-done.8.far_ref
  28.8 0.3 opposite.1
  29.1 1.6 %collective-permute-start.13 = (bf16[128,512]{1,0:T(8,128)(2,1)S(1)}, bf16[128,512]{1,0:T(8,128)(2,1)S(1)}, u32[]{:S(2)}, u32[]{:S(2)}) collective-permute-start(bf16[128,512]{1,0:T(8,128)(2,1)S(1)} %get-tuple-element.49), channel_id=1, source_target_pairs={{0,2},{1,3},{2,0},{3,1},{4,6},{5,7},{6,4},{7,5},{8,10},{9,11},{10,... | collective-permute-start | bytes 393224 | tf_op jit(solution)/shard_map/ppermute | solution.py:629
  30.7 2.1 %collective-permute-start.11 = (bf16[128,512]{1,0:T(8,128)(2,1)S(1)}, bf16[128,512]{1,0:T(8,128)(2,1)S(1)}, u32[]{:S(2)}, u32[]{:S(2)}) collective-permute-start(bf16[128,512]{1,0:T(8,128)(2,1)S(1)} %get-tuple-element.47), channel_id=1, source_target_pairs={{0,6},{1,7},{2,4},{3,5},{4,2},{5,3},{6,0},{7,1},{8,14},{9,15},{10,... | collective-permute-start | bytes 393224 | tf_op jit(solution)/shard_map/ppermute | solution.py:629
  32.8 0.3 neighbours.1
  33.1 1.2 %collective-permute-start.10 = (bf16[128,512]{1,0:T(8,128)(2,1)S(1)}, bf16[128,512]{1,0:T(8,128)(2,1)S(1)}, u32[]{:S(2)}, u32[]{:S(2)}) collective-permute-start(bf16[128,512]{1,0:T(8,128)(2,1)S(1)} %get-tuple-element.46), channel_id=1, source_target_pairs={{0,6},{1,7},{2,4},{3,5},{4,2},{5,3},{6,0},{7,1},{8,14},{9,15},{10,... | collective-permute-start | bytes 393224 | tf_op jit(solution)/shard_map/ppermute | solution.py:629
  34.3 0.0 collective-permute-start.9
  34.3 0.3 joining.1
  34.6 0.1 collective-permute-done.13.passing
  34.7 2.8 %collective-permute-start.14 = (bf16[128,512]{1,0:T(8,128)(2,1)S(1)}, bf16[128,512]{1,0:T(8,128)(2,1)S(1)}, u32[]{:S(2)}, u32[]{:S(2)}) collective-permute-start(bf16[128,512]{1,0:T(8,128)(2,1)S(1)} %relay.3), channel_id=1, source_target_pairs={{0,6},{1,7},{2,4},{3,5},{4,2},{5,3},{6,0},{7,1},{8,14},{9,15},{10,... | collective-permute-start | bytes 393224 | tf_op jit(solution)/shard_map/ppermute | solution.py:629
  37.6 0.1 collective-permute-done.11.passing
  37.7 0.7 %collective-permute-start.12 = (bf16[128,512]{1,0:T(8,128)(2,1)S(1)}, bf16[128,512]{1,0:T(8,128)(2,1)S(1)}, u32[]{:S(2)}, u32[]{:S(2)}) collective-permute-start(bf16[128,512]{1,0:T(8,128)(2,1)S(1)} %relay.2), channel_id=1, source_target_pairs={{0,2},{1,3},{2,0},{3,1},{4,6},{5,7},{6,4},{7,5},{8,10},{9,11},{10,... | collective-permute-start | bytes 393224 | tf_op jit(solution)/shard_map/ppermute | solution.py:629
  38.4 0.3 kept.1.own
  38.7 2.1 %collective-permute-done.10.direct3 = bf16[128,512]{1,0:T(8,128)(2,1)S(1)} collective-permute-done((bf16[128,512]{1,0:T(8,128)(2,1)S(1)}, bf16[128,512]{1,0:T(8,128)(2,1)S(1)}, u32[]{:S(2)}, u32[]{:S(2)}) %collective-permute-start.10) | collective-permute-done | bytes 131104 | tf_op jit(solution)/shard_map/ppermute | solution.py:629
  40.8 0.0 collective-permute-done.9.direct1
  40.8 1.9 %collective-permute-done.14.joined3 = bf16[128,512]{1,0:T(8,128)(2,1)S(1)} collective-permute-done((bf16[128,512]{1,0:T(8,128)(2,1)S(1)}, bf16[128,512]{1,0:T(8,128)(2,1)S(1)}, u32[]{:S(2)}, u32[]{:S(2)}) %collective-permute-start.14) | collective-permute-done | bytes 131104 | tf_op jit(solution)/shard_map/ppermute | solution.py:629
  42.8 0.0 collective-permute-done.12.joined1
  42.8 1.0 %finish.1 = bf16[512,256]{1,0:T(8,128)(2,1)} custom-call(f32[256,512]{1,0:T(8,128)S(1)} %kept.1.own, bf16[128,512]{1,0:T(8,128)(2,1)S(1)} %collective-permute-done.9.direct1, bf16[128,512]{1,0:T(8,128)(2,1)S(1)} %collective-permute-done.10.direct3, bf16[128,512]{1,0:T(8,128)(2,1)S(1)} %collective-permute-done.12.joined1, ...), custom_call_target="tpu_custom_call" | custom-call | tf_op jit(solution)/shard_map/finish/pallas_call | solution.py:37
  (3 shorter events, 0.1 us)
Async XLA Ops:
  2.4 5.0 %collective-permute-start = (bf16[32,512]{1,0:T(8,128)(2,1)S(1)}, bf16[32,512]{1,0:T(8,128)(2,1)S(1)}, u32[]{:S(2)}, u32[]{:S(2)}) collective-permute-start(bf16[32,512]{1,0:T(8,128)(2,1)S(1)} %get-tuple-element.28.mine), channel_id=1, source_target_pairs={{0,24},{8,16},{16,8},{24,0},{32,56},{40,48},{48,40},{56,32},{64,88... | collective-permute-start | bytes 98312 | tf_op jit(solution)/shard_map/ppermute | solution.py:612
  4.4 4.9 %collective-permute-start.1 = (bf16[32,512]{1,0:T(8,128)(2,1)S(1)}, bf16[32,512]{1,0:T(8,128)(2,1)S(1)}, u32[]{:S(2)}, u32[]{:S(2)}) collective-permute-start(bf16[32,512]{1,0:T(8,128)(2,1)S(1)} %get-tuple-element.28.mine), channel_id=1, source_target_pairs={{0,16},{8,24},{16,0},{24,8},{32,48},{40,56},{48,32},{56,40},{64,80... | collective-permute-start | bytes 98312 | tf_op jit(solution)/shard_map/ppermute | solution.py:612
  6.7 3.9 %collective-permute-start.2 = (bf16[32,512]{1,0:T(8,128)(2,1)S(1)}, bf16[32,512]{1,0:T(8,128)(2,1)S(1)}, u32[]{:S(2)}, u32[]{:S(2)}) collective-permute-start(bf16[32,512]{1,0:T(8,128)(2,1)S(1)} %get-tuple-element.28.mine), channel_id=1, source_target_pairs={{0,8},{8,0},{16,24},{24,16},{32,40},{40,32},{48,56},{56,48},{64,72... | collective-permute-start | bytes 98312 | tf_op jit(solution)/shard_map/ppermute | solution.py:612
  10.7 18.0 %collective-permute-start.8 = (bf16[512,4096]{1,0:T(8,128)(2,1)}, bf16[512,4096]{1,0:T(8,128)(2,1)S(1)}, u32[]{:S(2)}, u32[]{:S(2)}) collective-permute-start(bf16[512,4096]{1,0:T(8,128)(2,1)} %weight_hbm.1), channel_id=1, source_target_pairs={{0,1},{1,0},{2,3},{3,2},{4,5},{5,4},{6,7},{7,6},{8,9},{9,8},{10,11... | collective-permute-start | bytes 12582920 | tf_op jit(solution)/shard_map/ppermute | solution.py:618
  10.8 7.1 %collective-permute-start.3 = (bf16[32,512]{1,0:T(8,128)(2,1)S(1)}, bf16[32,512]{1,0:T(8,128)(2,1)S(1)}, u32[]{:S(2)}, u32[]{:S(2)}) collective-permute-start(bf16[32,512]{1,0:T(8,128)(2,1)S(1)} %get-tuple-element.32.after.mine), channel_id=1, source_target_pairs={{0,56},{8,48},{16,40},{24,32},{32,24},{40,16},{48,8},{56,0},{64,12... | collective-permute-start | bytes 98312 | tf_op jit(solution)/shard_map/ppermute | solution.py:612
  17.9 7.0 %collective-permute-start.4 = (bf16[32,512]{1,0:T(8,128)(2,1)S(1)}, bf16[32,512]{1,0:T(8,128)(2,1)S(1)}, u32[]{:S(2)}, u32[]{:S(2)}) collective-permute-start(bf16[32,512]{1,0:T(8,128)(2,1)S(1)} %get-tuple-element.35.after.mine), channel_id=1, source_target_pairs={{0,128},{8,136},{16,144},{24,152},{32,160},{40,168},{48,176},{56,1... | collective-permute-start | bytes 98312 | tf_op jit(solution)/shard_map/ppermute | solution.py:612
  21.2 5.1 %collective-permute-start.5 = (bf16[32,512]{1,0:T(8,128)(2,1)S(1)}, bf16[32,512]{1,0:T(8,128)(2,1)S(1)}, u32[]{:S(2)}, u32[]{:S(2)}) collective-permute-start(bf16[32,512]{1,0:T(8,128)(2,1)S(1)} %get-tuple-element.35.after.mine), channel_id=1, source_target_pairs={{0,192},{8,200},{16,208},{24,216},{32,224},{40,232},{48,240},{56,2... | collective-permute-start | bytes 98312 | tf_op jit(solution)/shard_map/ppermute | solution.py:612
  22.3 4.1 %collective-permute-start.6 = (bf16[32,512]{1,0:T(8,128)(2,1)S(1)}, bf16[32,512]{1,0:T(8,128)(2,1)S(1)}, u32[]{:S(2)}, u32[]{:S(2)}) collective-permute-start(bf16[32,512]{1,0:T(8,128)(2,1)S(1)} %get-tuple-element.35.after.mine), channel_id=1, source_target_pairs={{0,64},{8,72},{16,80},{24,88},{32,96},{40,104},{48,112},{56,120},{... | collective-permute-start | bytes 98312 | tf_op jit(solution)/shard_map/ppermute | solution.py:612
  27.1 1.6 %collective-permute-start.7 = (bf16[256,512]{1,0:T(8,128)(2,1)S(1)}, bf16[256,512]{1,0:T(8,128)(2,1)S(1)}, u32[]{:S(2)}, u32[]{:S(2)}) collective-permute-start(bf16[256,512]{1,0:T(8,128)(2,1)S(1)} %gated.1.mine), channel_id=1, source_target_pairs={{0,1},{1,0},{2,3},{3,2},{4,5},{5,4},{6,7},{7,6},{8,9},{9,8},{10,11... | collective-permute-start | bytes 786440 | tf_op jit(solution)/shard_map/ppermute | solution.py:626
  29.1 5.6 %collective-permute-start.13 = (bf16[128,512]{1,0:T(8,128)(2,1)S(1)}, bf16[128,512]{1,0:T(8,128)(2,1)S(1)}, u32[]{:S(2)}, u32[]{:S(2)}) collective-permute-start(bf16[128,512]{1,0:T(8,128)(2,1)S(1)} %get-tuple-element.49), channel_id=1, source_target_pairs={{0,2},{1,3},{2,0},{3,1},{4,6},{5,7},{6,4},{7,5},{8,10},{9,11},{10,... | collective-permute-start | bytes 393224 | tf_op jit(solution)/shard_map/ppermute | solution.py:629
  30.7 7.0 %collective-permute-start.11 = (bf16[128,512]{1,0:T(8,128)(2,1)S(1)}, bf16[128,512]{1,0:T(8,128)(2,1)S(1)}, u32[]{:S(2)}, u32[]{:S(2)}) collective-permute-start(bf16[128,512]{1,0:T(8,128)(2,1)S(1)} %get-tuple-element.47), channel_id=1, source_target_pairs={{0,6},{1,7},{2,4},{3,5},{4,2},{5,3},{6,0},{7,1},{8,14},{9,15},{10,... | collective-permute-start | bytes 393224 | tf_op jit(solution)/shard_map/ppermute | solution.py:629
  33.1 7.7 %collective-permute-start.10 = (bf16[128,512]{1,0:T(8,128)(2,1)S(1)}, bf16[128,512]{1,0:T(8,128)(2,1)S(1)}, u32[]{:S(2)}, u32[]{:S(2)}) collective-permute-start(bf16[128,512]{1,0:T(8,128)(2,1)S(1)} %get-tuple-element.46), channel_id=1, source_target_pairs={{0,6},{1,7},{2,4},{3,5},{4,2},{5,3},{6,0},{7,1},{8,14},{9,15},{10,... | collective-permute-start | bytes 393224 | tf_op jit(solution)/shard_map/ppermute | solution.py:629
  34.3 6.5 %collective-permute-start.9 = (bf16[128,512]{1,0:T(8,128)(2,1)S(1)}, bf16[128,512]{1,0:T(8,128)(2,1)S(1)}, u32[]{:S(2)}, u32[]{:S(2)}) collective-permute-start(bf16[128,512]{1,0:T(8,128)(2,1)S(1)} %get-tuple-element.45), channel_id=1, source_target_pairs={{0,2},{1,3},{2,0},{3,1},{4,6},{5,7},{6,4},{7,5},{8,10},{9,11},{10,... | collective-permute-start | bytes 393224 | tf_op jit(solution)/shard_map/ppermute | solution.py:629
  34.7 8.0 %collective-permute-start.14 = (bf16[128,512]{1,0:T(8,128)(2,1)S(1)}, bf16[128,512]{1,0:T(8,128)(2,1)S(1)}, u32[]{:S(2)}, u32[]{:S(2)}) collective-permute-start(bf16[128,512]{1,0:T(8,128)(2,1)S(1)} %relay.3), channel_id=1, source_target_pairs={{0,6},{1,7},{2,4},{3,5},{4,2},{5,3},{6,0},{7,1},{8,14},{9,15},{10,... | collective-permute-start | bytes 393224 | tf_op jit(solution)/shard_map/ppermute | solution.py:629
  37.7 5.1 %collective-permute-start.12 = (bf16[128,512]{1,0:T(8,128)(2,1)S(1)}, bf16[128,512]{1,0:T(8,128)(2,1)S(1)}, u32[]{:S(2)}, u32[]{:S(2)}) collective-permute-start(bf16[128,512]{1,0:T(8,128)(2,1)S(1)} %relay.2), channel_id=1, source_target_pairs={{0,2},{1,3},{2,0},{3,1},{4,6},{5,7},{6,4},{7,5},{8,10},{9,11},{10,... | collective-permute-start | bytes 393224 | tf_op jit(solution)/shard_map/ppermute | solution.py:629

commit v4 on v3

--- a/solution.py
+++ b/solution.py
@@ -560,6 +560,26 @@
     return call(kernel, name, out)(near, other, far)
 
 
+def sides(near, other, far):
+    span = near.shape[0]
+    half = span // 2
+    columns = far.shape[1] // lax.axis_size("ch")
+
+    def kernel(near_ref, other_ref, far_ref, direct3, direct1, mine3, mine1):
+        for k, direct, mine in ((3, direct3, mine3), (1, direct1, mine1)):
+            block = lax.axis_index("ch") ^ (2 * k)
+            there = pl.ds(pl.multiple_of(block * columns, columns), columns)
+            total = near_ref[:, k * columns : (k + 1) * columns] + jnp.dot(
+                other_ref[...], far_ref[:, there], preferred_element_type=F32
+            )
+            top, low = total[:half], total[half:]
+            direct[...] = (low if k == 3 else top).astype(BF16)
+            mine[...] = top if k == 3 else low
+
+    out = [jax.ShapeDtypeStruct((half, columns), d) for d in (BF16, BF16, F32, F32)]
+    return call(kernel, "sides", out)(near, other, far)
+
+
 def relay_kernel(passing, own, out):
     out[...] = (passing[...].astype(F32) + own[...]).astype(BF16)
 
@@ -631,9 +651,8 @@
     operands = (near_sums(own, weight), other, far)
     over3, over1 = project(*operands, "opposite", [[(2, 1)], [(2, 0)]], BF16)
     over3, over1 = swap(over3, 3), swap(over1, 1)
-    direct3, direct1 = project(*operands, "neighbours", [[(3, 1)], [(1, 0)]], BF16)
+    direct3, direct1, mine3, mine1 = sides(*operands)
     direct3, direct1 = swap(direct3, 3), swap(direct1, 1)
-    mine3, mine1 = project(*operands, "joining", [[(3, 0)], [(1, 1)]], F32)
     (kept,) = project(*operands, "kept", [[(0, 0), (0, 1)]], F32)
     joined1 = swap(relay(over3, mine1), 1)
     joined3 = swap(relay(over1, mine3), 3)

time: 44 us -> 43.9 us (level)
    pallas_call x15 -> x14, Pallas kernels: 10.7 us -> 10.5 us  [run(): pl.pallas_call(kernel, in_specs=[pl.BlockSpec(memory_space=space) for spa...]
  transfers between devices with their start and end apart: 15 -> 15, of which waited for: 9 -> 8; matrix products, arithmetic and copies ran while one was open for 0% -> 0% of each run, Pallas kernels for 16% -> 15%
where the time goes in v4:
time: 43.9 us; the launch traced here: 43.8 us
  starting transfers between devices  22.8 us (52%)
  Pallas kernels  10.5 us (24%)
  waiting for transfers between devices  10.4 us (24%)
    ppermute x7, starting transfers between devices, across(): return lax.ppermute(value, 'ctx', [(i, i ^ by) for i in range(n_ctx)])  14.3 us
    pallas_call x14, Pallas kernels, run(): pl.pallas_call(kernel, in_specs=[pl.BlockSpec(memory_space=space) for spa...  10.5 us
    ppermute x6, starting transfers between devices, swap(): return lax.ppermute(value, 'ch', [(i, i ^ 2 * k) for i in range(n_ch)])  8.32 us
    ppermute x7, waiting for transfers between devices, across(): return lax.ppermute(value, 'ctx', [(i, i ^ by) for i in range(n_ctx)])  5.03 us
    ppermute x6, waiting for transfers between devices, swap(): return lax.ppermute(value, 'ch', [(i, i ^ 2 * k) for i in range(n_ch)])  4.52 us
  transfers between devices with their start and end apart: 15, of which 8 were waited for; matrix products, arithmetic and copies ran while one was open for 0% of the time, Pallas kernels for 15%

profile of v4, /device:TPU:32, one launch (start us, length us, event | category | flops | bytes accessed | tf_op | source)
XLA Modules:
  0.0 43.8 jit_solution(11704287578820316862)
XLA Ops:
  0.0 2.4 %states.1 = (bf16[32,512]{1,0:T(8,128)(2,1)S(1)}, f32[256,512]{1,0:T(8,128)S(1)}, f32[16,512]{1,0:T(8,128)S(1)}, f32[4,16,512]{2,1,0:T(8,128)S(1)}, f32[2,16,512...) custom-call(bf16[512,256]{1,0:T(8,128)(2,1)} %key_hbm.1, bf16[512,256]{1,0:T(8,128)(2,1)} %value_hbm.1, ...), custom_call_target="tpu_custom_call" | custom-call | tf_op jit(solution)/shard_map/states/pallas_call | solution.py:37
  2.4 2.0 %collective-permute-start = (bf16[32,512]{1,0:T(8,128)(2,1)S(1)}, bf16[32,512]{1,0:T(8,128)(2,1)S(1)}, u32[]{:S(2)}, u32[]{:S(2)}) collective-permute-start(bf16[32,512]{1,0:T(8,128)(2,1)S(1)} %get-tuple-element.28.mine), channel_id=1, source_target_pairs={{0,24},{8,16},{16,8},{24,0},{32,56},{40,48},{48,40},{56,32},{64,88... | collective-permute-start | bytes 98312 | tf_op jit(solution)/shard_map/ppermute | solution.py:632
  4.4 2.3 %collective-permute-start.1 = (bf16[32,512]{1,0:T(8,128)(2,1)S(1)}, bf16[32,512]{1,0:T(8,128)(2,1)S(1)}, u32[]{:S(2)}, u32[]{:S(2)}) collective-permute-start(bf16[32,512]{1,0:T(8,128)(2,1)S(1)} %get-tuple-element.28.mine), channel_id=1, source_target_pairs={{0,16},{8,24},{16,0},{24,8},{32,48},{40,56},{48,32},{56,40},{64,80... | collective-permute-start | bytes 98312 | tf_op jit(solution)/shard_map/ppermute | solution.py:632
  6.7 0.5 %collective-permute-start.2 = (bf16[32,512]{1,0:T(8,128)(2,1)S(1)}, bf16[32,512]{1,0:T(8,128)(2,1)S(1)}, u32[]{:S(2)}, u32[]{:S(2)}) collective-permute-start(bf16[32,512]{1,0:T(8,128)(2,1)S(1)} %get-tuple-element.28.mine), channel_id=1, source_target_pairs={{0,8},{8,0},{16,24},{24,16},{32,40},{40,32},{48,56},{56,48},{64,72... | collective-permute-start | bytes 98312 | tf_op jit(solution)/shard_map/ppermute | solution.py:632
  7.2 0.1 tables.1
  7.4 0.0 collective-permute-done.three
  7.4 2.0 %collective-permute-done.1.two = bf16[32,512]{1,0:T(8,128)(2,1)S(1)} collective-permute-done((bf16[32,512]{1,0:T(8,128)(2,1)S(1)}, bf16[32,512]{1,0:T(8,128)(2,1)S(1)}, u32[]{:S(2)}, u32[]{:S(2)}) %collective-permute-start.1) | collective-permute-done | bytes 32800 | tf_op jit(solution)/shard_map/ppermute | solution.py:632
  9.3 1.3 %collective-permute-done.2.one = bf16[32,512]{1,0:T(8,128)(2,1)S(1)} collective-permute-done((bf16[32,512]{1,0:T(8,128)(2,1)S(1)}, bf16[32,512]{1,0:T(8,128)(2,1)S(1)}, u32[]{:S(2)}, u32[]{:S(2)}) %collective-permute-start.2) | collective-permute-done | bytes 32800 | tf_op jit(solution)/shard_map/ppermute | solution.py:632
  10.6 0.1 merge_four.1
  10.7 0.1 collective-permute-start.8
  10.8 5.1 %collective-permute-start.3 = (bf16[32,512]{1,0:T(8,128)(2,1)S(1)}, bf16[32,512]{1,0:T(8,128)(2,1)S(1)}, u32[]{:S(2)}, u32[]{:S(2)}) collective-permute-start(bf16[32,512]{1,0:T(8,128)(2,1)S(1)} %get-tuple-element.32.after.mine), channel_id=1, source_target_pairs={{0,56},{8,48},{16,40},{24,32},{32,24},{40,16},{48,8},{56,0},{64,12... | collective-permute-start | bytes 98312 | tf_op jit(solution)/shard_map/ppermute | solution.py:632
  15.9 1.6 %weight_blocks.1.after.weight = bf16[512,2048]{1,0:T(8,128)(2,1)S(1)} custom-call(bf16[512,4096]{1,0:T(8,128)(2,1)} %weight_hbm.1, bf16[32,512]{1,0:T(8,128)(2,1)S(1)} %get-tuple-element.32.after.mine), custom_call_target="tpu_custom_call" | custom-call | tf_op jit(solution)/shard_map/weight_blocks/pallas_call | solution.py:37
  17.5 0.4 collective-permute-done.3.theirs
  17.9 3.3 %collective-permute-start.4 = (bf16[32,512]{1,0:T(8,128)(2,1)S(1)}, bf16[32,512]{1,0:T(8,128)(2,1)S(1)}, u32[]{:S(2)}, u32[]{:S(2)}) collective-permute-start(bf16[32,512]{1,0:T(8,128)(2,1)S(1)} %get-tuple-element.35.after.mine), channel_id=1, source_target_pairs={{0,128},{8,136},{16,144},{24,152},{32,160},{40,168},{48,176},{56,1... | collective-permute-start | bytes 98312 | tf_op jit(solution)/shard_map/ppermute | solution.py:632
  21.2 1.1 %collective-permute-start.5 = (bf16[32,512]{1,0:T(8,128)(2,1)S(1)}, bf16[32,512]{1,0:T(8,128)(2,1)S(1)}, u32[]{:S(2)}, u32[]{:S(2)}) collective-permute-start(bf16[32,512]{1,0:T(8,128)(2,1)S(1)} %get-tuple-element.35.after.mine), channel_id=1, source_target_pairs={{0,192},{8,200},{16,208},{24,216},{32,224},{40,232},{48,240},{56,2... | collective-permute-start | bytes 98312 | tf_op jit(solution)/shard_map/ppermute | solution.py:632
  22.3 0.0 collective-permute-start.6
  22.3 2.7 %local_scan.1 = (f32[256,512]{1,0:T(8,128)S(1)}, f32[256,512]{1,0:T(8,128)S(1)}, f32[128,512]{1,0:T(8,128)S(1)}, f32[128,512]{1,0:T(8,128)S(1)}) custom-call(f32[256,512]{1,0:T(8,128)S(1)} %get-tuple-element.38.gated, bf16[512,256]{1,0:T(8,128)(2,1)} %query_hbm.3, f32[16,512]{1,0:T(8,128)S(1)} %get-tuple-element.29.params, f32[29,16,512]{2,1,0:T(8,128)S(1)} %tables.1, ...), custom_call_target="tpu_custom_call" | custom-call | tf_op jit(solution)/shard_map/local_scan/pallas_call | solution.py:37
  25.0 0.0 collective-permute-done.4.row2
  25.0 1.4 %collective-permute-done.5.row3 = bf16[32,512]{1,0:T(8,128)(2,1)S(1)} collective-permute-done((bf16[32,512]{1,0:T(8,128)(2,1)S(1)}, bf16[32,512]{1,0:T(8,128)(2,1)S(1)}, u32[]{:S(2)}, u32[]{:S(2)}) %collective-permute-start.5) | collective-permute-done | bytes 32800 | tf_op jit(solution)/shard_map/ppermute | solution.py:632
  26.4 0.0 collective-permute-done.6.row1
  26.4 0.8 %gated.1.mine = bf16[256,512]{1,0:T(8,128)(2,1)S(1)} custom-call(bf16[32,512]{1,0:T(8,128)(2,1)S(1)} %get-tuple-element.35.after.mine, bf16[32,512]{1,0:T(8,128)(2,1)S(1)} %collective-permute-done.4.row2, bf16[32,512]{1,0:T(8,128)(2,1)S(1)} %collective-permute-done.5.row3, bf16[32,512]{1,0:T(8,128)(2,1)S(1)} %collective-permute-done.6.row1, ...), custom_call_target="tpu_custom_call" | custom-call | tf_op jit(solution)/shard_map/gated/pallas_call | solution.py:37
  27.1 0.1 collective-permute-start.7
  27.2 0.7 %near_sums.1.near_ref = f32[256,2048]{1,0:T(8,128)S(1)} custom-call(bf16[256,512]{1,0:T(8,128)(2,1)S(1)} %gated.1.mine, bf16[512,2048]{1,0:T(8,128)(2,1)S(1)} %weight_blocks.1.after.weight), custom_call_target="tpu_custom_call" | custom-call | tf_op jit(solution)/shard_map/near_sums/pallas_call | solution.py:37
  28.0 0.8 %collective-permute-done.7.other_ref = bf16[256,512]{1,0:T(8,128)(2,1)S(1)} collective-permute-done((bf16[256,512]{1,0:T(8,128)(2,1)S(1)}, bf16[256,512]{1,0:T(8,128)(2,1)S(1)}, u32[]{:S(2)}, u32[]{:S(2)}) %collective-permute-start.7) | collective-permute-done | bytes 262176 | tf_op jit(solution)/shard_map/ppermute | solution.py:646
  28.8 0.0 collective-permute-done.8.far_ref
  28.8 0.3 opposite.1
  29.1 1.6 %collective-permute-start.13 = (bf16[128,512]{1,0:T(8,128)(2,1)S(1)}, bf16[128,512]{1,0:T(8,128)(2,1)S(1)}, u32[]{:S(2)}, u32[]{:S(2)}) collective-permute-start(bf16[128,512]{1,0:T(8,128)(2,1)S(1)} %get-tuple-element.49), channel_id=1, source_target_pairs={{0,2},{1,3},{2,0},{3,1},{4,6},{5,7},{6,4},{7,5},{8,10},{9,11},{10,... | collective-permute-start | bytes 393224 | tf_op jit(solution)/shard_map/ppermute | solution.py:649
  30.7 2.1 %collective-permute-start.11 = (bf16[128,512]{1,0:T(8,128)(2,1)S(1)}, bf16[128,512]{1,0:T(8,128)(2,1)S(1)}, u32[]{:S(2)}, u32[]{:S(2)}) collective-permute-start(bf16[128,512]{1,0:T(8,128)(2,1)S(1)} %get-tuple-element.47), channel_id=1, source_target_pairs={{0,6},{1,7},{2,4},{3,5},{4,2},{5,3},{6,0},{7,1},{8,14},{9,15},{10,... | collective-permute-start | bytes 393224 | tf_op jit(solution)/shard_map/ppermute | solution.py:649
  32.8 0.4 sides.1
  33.2 1.2 %collective-permute-start.10 = (bf16[128,512]{1,0:T(8,128)(2,1)S(1)}, bf16[128,512]{1,0:T(8,128)(2,1)S(1)}, u32[]{:S(2)}, u32[]{:S(2)}) collective-permute-start(bf16[128,512]{1,0:T(8,128)(2,1)S(1)} %get-tuple-element.46), channel_id=1, source_target_pairs={{0,6},{1,7},{2,4},{3,5},{4,2},{5,3},{6,0},{7,1},{8,14},{9,15},{10,... | collective-permute-start | bytes 393224 | tf_op jit(solution)/shard_map/ppermute | solution.py:649
  34.4 0.0 collective-permute-start.9
  34.4 0.3 collective-permute-done.13.passing
  34.7 2.8 %collective-permute-start.14 = (bf16[128,512]{1,0:T(8,128)(2,1)S(1)}, bf16[128,512]{1,0:T(8,128)(2,1)S(1)}, u32[]{:S(2)}, u32[]{:S(2)}) collective-permute-start(bf16[128,512]{1,0:T(8,128)(2,1)S(1)} %relay.3), channel_id=1, source_target_pairs={{0,6},{1,7},{2,4},{3,5},{4,2},{5,3},{6,0},{7,1},{8,14},{9,15},{10,... | collective-permute-start | bytes 393224 | tf_op jit(solution)/shard_map/ppermute | solution.py:649
  37.6 0.0 collective-permute-done.11.passing
  37.6 0.6 %collective-permute-start.12 = (bf16[128,512]{1,0:T(8,128)(2,1)S(1)}, bf16[128,512]{1,0:T(8,128)(2,1)S(1)}, u32[]{:S(2)}, u32[]{:S(2)}) collective-permute-start(bf16[128,512]{1,0:T(8,128)(2,1)S(1)} %relay.2), channel_id=1, source_target_pairs={{0,2},{1,3},{2,0},{3,1},{4,6},{5,7},{6,4},{7,5},{8,10},{9,11},{10,... | collective-permute-start | bytes 393224 | tf_op jit(solution)/shard_map/ppermute | solution.py:649
  38.2 0.3 kept.1.own
  38.5 2.4 %collective-permute-done.10.direct3 = bf16[128,512]{1,0:T(8,128)(2,1)S(1)} collective-permute-done((bf16[128,512]{1,0:T(8,128)(2,1)S(1)}, bf16[128,512]{1,0:T(8,128)(2,1)S(1)}, u32[]{:S(2)}, u32[]{:S(2)}) %collective-permute-start.10) | collective-permute-done | bytes 131104 | tf_op jit(solution)/shard_map/ppermute | solution.py:649
  40.9 0.0 collective-permute-done.9.direct1
  40.9 1.8 %collective-permute-done.14.joined3 = bf16[128,512]{1,0:T(8,128)(2,1)S(1)} collective-permute-done((bf16[128,512]{1,0:T(8,128)(2,1)S(1)}, bf16[128,512]{1,0:T(8,128)(2,1)S(1)}, u32[]{:S(2)}, u32[]{:S(2)}) %collective-permute-start.14) | collective-permute-done | bytes 131104 | tf_op jit(solution)/shard_map/ppermute | solution.py:649
  42.8 0.0 collective-permute-done.12.joined1
  42.8 1.0 %finish.1 = bf16[512,256]{1,0:T(8,128)(2,1)} custom-call(f32[256,512]{1,0:T(8,128)S(1)} %kept.1.own, bf16[128,512]{1,0:T(8,128)(2,1)S(1)} %collective-permute-done.9.direct1, bf16[128,512]{1,0:T(8,128)(2,1)S(1)} %collective-permute-done.10.direct3, bf16[128,512]{1,0:T(8,128)(2,1)S(1)} %collective-permute-done.12.joined1, ...), custom_call_target="tpu_custom_call" | custom-call | tf_op jit(solution)/shard_map/finish/pallas_call | solution.py:37
  (3 shorter events, 0.1 us)
Async XLA Ops:
  2.4 5.0 %collective-permute-start = (bf16[32,512]{1,0:T(8,128)(2,1)S(1)}, bf16[32,512]{1,0:T(8,128)(2,1)S(1)}, u32[]{:S(2)}, u32[]{:S(2)}) collective-permute-start(bf16[32,512]{1,0:T(8,128)(2,1)S(1)} %get-tuple-element.28.mine), channel_id=1, source_target_pairs={{0,24},{8,16},{16,8},{24,0},{32,56},{40,48},{48,40},{56,32},{64,88... | collective-permute-start | bytes 98312 | tf_op jit(solution)/shard_map/ppermute | solution.py:632
  4.4 4.9 %collective-permute-start.1 = (bf16[32,512]{1,0:T(8,128)(2,1)S(1)}, bf16[32,512]{1,0:T(8,128)(2,1)S(1)}, u32[]{:S(2)}, u32[]{:S(2)}) collective-permute-start(bf16[32,512]{1,0:T(8,128)(2,1)S(1)} %get-tuple-element.28.mine), channel_id=1, source_target_pairs={{0,16},{8,24},{16,0},{24,8},{32,48},{40,56},{48,32},{56,40},{64,80... | collective-permute-start | bytes 98312 | tf_op jit(solution)/shard_map/ppermute | solution.py:632
  6.7 3.9 %collective-permute-start.2 = (bf16[32,512]{1,0:T(8,128)(2,1)S(1)}, bf16[32,512]{1,0:T(8,128)(2,1)S(1)}, u32[]{:S(2)}, u32[]{:S(2)}) collective-permute-start(bf16[32,512]{1,0:T(8,128)(2,1)S(1)} %get-tuple-element.28.mine), channel_id=1, source_target_pairs={{0,8},{8,0},{16,24},{24,16},{32,40},{40,32},{48,56},{56,48},{64,72... | collective-permute-start | bytes 98312 | tf_op jit(solution)/shard_map/ppermute | solution.py:632
  10.7 18.0 %collective-permute-start.8 = (bf16[512,4096]{1,0:T(8,128)(2,1)}, bf16[512,4096]{1,0:T(8,128)(2,1)S(1)}, u32[]{:S(2)}, u32[]{:S(2)}) collective-permute-start(bf16[512,4096]{1,0:T(8,128)(2,1)} %weight_hbm.1), channel_id=1, source_target_pairs={{0,1},{1,0},{2,3},{3,2},{4,5},{5,4},{6,7},{7,6},{8,9},{9,8},{10,11... | collective-permute-start | bytes 12582920 | tf_op jit(solution)/shard_map/ppermute | solution.py:638
  10.8 7.1 %collective-permute-start.3 = (bf16[32,512]{1,0:T(8,128)(2,1)S(1)}, bf16[32,512]{1,0:T(8,128)(2,1)S(1)}, u32[]{:S(2)}, u32[]{:S(2)}) collective-permute-start(bf16[32,512]{1,0:T(8,128)(2,1)S(1)} %get-tuple-element.32.after.mine), channel_id=1, source_target_pairs={{0,56},{8,48},{16,40},{24,32},{32,24},{40,16},{48,8},{56,0},{64,12... | collective-permute-start | bytes 98312 | tf_op jit(solution)/shard_map/ppermute | solution.py:632
  17.9 7.0 %collective-permute-start.4 = (bf16[32,512]{1,0:T(8,128)(2,1)S(1)}, bf16[32,512]{1,0:T(8,128)(2,1)S(1)}, u32[]{:S(2)}, u32[]{:S(2)}) collective-permute-start(bf16[32,512]{1,0:T(8,128)(2,1)S(1)} %get-tuple-element.35.after.mine), channel_id=1, source_target_pairs={{0,128},{8,136},{16,144},{24,152},{32,160},{40,168},{48,176},{56,1... | collective-permute-start | bytes 98312 | tf_op jit(solution)/shard_map/ppermute | solution.py:632
  21.2 5.1 %collective-permute-start.5 = (bf16[32,512]{1,0:T(8,128)(2,1)S(1)}, bf16[32,512]{1,0:T(8,128)(2,1)S(1)}, u32[]{:S(2)}, u32[]{:S(2)}) collective-permute-start(bf16[32,512]{1,0:T(8,128)(2,1)S(1)} %get-tuple-element.35.after.mine), channel_id=1, source_target_pairs={{0,192},{8,200},{16,208},{24,216},{32,224},{40,232},{48,240},{56,2... | collective-permute-start | bytes 98312 | tf_op jit(solution)/shard_map/ppermute | solution.py:632
  22.3 4.1 %collective-permute-start.6 = (bf16[32,512]{1,0:T(8,128)(2,1)S(1)}, bf16[32,512]{1,0:T(8,128)(2,1)S(1)}, u32[]{:S(2)}, u32[]{:S(2)}) collective-permute-start(bf16[32,512]{1,0:T(8,128)(2,1)S(1)} %get-tuple-element.35.after.mine), channel_id=1, source_target_pairs={{0,64},{8,72},{16,80},{24,88},{32,96},{40,104},{48,112},{56,120},{... | collective-permute-start | bytes 98312 | tf_op jit(solution)/shard_map/ppermute | solution.py:632
  27.1 1.6 %collective-permute-start.7 = (bf16[256,512]{1,0:T(8,128)(2,1)S(1)}, bf16[256,512]{1,0:T(8,128)(2,1)S(1)}, u32[]{:S(2)}, u32[]{:S(2)}) collective-permute-start(bf16[256,512]{1,0:T(8,128)(2,1)S(1)} %gated.1.mine), channel_id=1, source_target_pairs={{0,1},{1,0},{2,3},{3,2},{4,5},{5,4},{6,7},{7,6},{8,9},{9,8},{10,11... | collective-permute-start | bytes 786440 | tf_op jit(solution)/shard_map/ppermute | solution.py:646
  29.1 5.6 %collective-permute-start.13 = (bf16[128,512]{1,0:T(8,128)(2,1)S(1)}, bf16[128,512]{1,0:T(8,128)(2,1)S(1)}, u32[]{:S(2)}, u32[]{:S(2)}) collective-permute-start(bf16[128,512]{1,0:T(8,128)(2,1)S(1)} %get-tuple-element.49), channel_id=1, source_target_pairs={{0,2},{1,3},{2,0},{3,1},{4,6},{5,7},{6,4},{7,5},{8,10},{9,11},{10,... | collective-permute-start | bytes 393224 | tf_op jit(solution)/shard_map/ppermute | solution.py:649
  30.7 6.9 %collective-permute-start.11 = (bf16[128,512]{1,0:T(8,128)(2,1)S(1)}, bf16[128,512]{1,0:T(8,128)(2,1)S(1)}, u32[]{:S(2)}, u32[]{:S(2)}) collective-permute-start(bf16[128,512]{1,0:T(8,128)(2,1)S(1)} %get-tuple-element.47), channel_id=1, source_target_pairs={{0,6},{1,7},{2,4},{3,5},{4,2},{5,3},{6,0},{7,1},{8,14},{9,15},{10,... | collective-permute-start | bytes 393224 | tf_op jit(solution)/shard_map/ppermute | solution.py:649
  33.2 7.7 %collective-permute-start.10 = (bf16[128,512]{1,0:T(8,128)(2,1)S(1)}, bf16[128,512]{1,0:T(8,128)(2,1)S(1)}, u32[]{:S(2)}, u32[]{:S(2)}) collective-permute-start(bf16[128,512]{1,0:T(8,128)(2,1)S(1)} %get-tuple-element.46), channel_id=1, source_target_pairs={{0,6},{1,7},{2,4},{3,5},{4,2},{5,3},{6,0},{7,1},{8,14},{9,15},{10,... | collective-permute-start | bytes 393224 | tf_op jit(solution)/shard_map/ppermute | solution.py:649
  34.4 6.5 %collective-permute-start.9 = (bf16[128,512]{1,0:T(8,128)(2,1)S(1)}, bf16[128,512]{1,0:T(8,128)(2,1)S(1)}, u32[]{:S(2)}, u32[]{:S(2)}) collective-permute-start(bf16[128,512]{1,0:T(8,128)(2,1)S(1)} %get-tuple-element.45), channel_id=1, source_target_pairs={{0,2},{1,3},{2,0},{3,1},{4,6},{5,7},{6,4},{7,5},{8,10},{9,11},{10,... | collective-permute-start | bytes 393224 | tf_op jit(solution)/shard_map/ppermute | solution.py:649
  34.7 8.0 %collective-permute-start.14 = (bf16[128,512]{1,0:T(8,128)(2,1)S(1)}, bf16[128,512]{1,0:T(8,128)(2,1)S(1)}, u32[]{:S(2)}, u32[]{:S(2)}) collective-permute-start(bf16[128,512]{1,0:T(8,128)(2,1)S(1)} %relay.3), channel_id=1, source_target_pairs={{0,6},{1,7},{2,4},{3,5},{4,2},{5,3},{6,0},{7,1},{8,14},{9,15},{10,... | collective-permute-start | bytes 393224 | tf_op jit(solution)/shard_map/ppermute | solution.py:649
  37.6 5.1 %collective-permute-start.12 = (bf16[128,512]{1,0:T(8,128)(2,1)S(1)}, bf16[128,512]{1,0:T(8,128)(2,1)S(1)}, u32[]{:S(2)}, u32[]{:S(2)}) collective-permute-start(bf16[128,512]{1,0:T(8,128)(2,1)S(1)} %relay.2), channel_id=1, source_target_pairs={{0,2},{1,3},{2,0},{3,1},{4,6},{5,7},{6,4},{7,5},{8,10},{9,11},{10,... | collective-permute-start | bytes 393224 | tf_op jit(solution)/shard_map/ppermute | solution.py:649

commit v5 on v4

--- a/solution.py
+++ b/solution.py
@@ -580,6 +580,23 @@
     return call(kernel, "sides", out)(near, other, far)
 
 
+def opposite(near, other, far):
+    half = near.shape[0] // 2
+    columns = far.shape[1] // lax.axis_size("ch")
+
+    def kernel(near_ref, other_ref, far_ref, over3, over1):
+        block = lax.axis_index("ch") ^ 4
+        there = pl.ds(pl.multiple_of(block * columns, columns), columns)
+        total = near_ref[:, 2 * columns : 3 * columns] + jnp.dot(
+            other_ref[...], far_ref[:, there], preferred_element_type=F32
+        )
+        over1[...] = total[:half].astype(BF16)
+        over3[...] = total[half:].astype(BF16)
+
+    out = [jax.ShapeDtypeStruct((half, columns), BF16)] * 2
+    return call(kernel, "opposite", out)(near, other, far)
+
+
 def relay_kernel(passing, own, out):
     out[...] = (passing[...].astype(F32) + own[...]).astype(BF16)
 
@@ -649,7 +666,7 @@
         return lax.ppermute(value, "ch", [(i, i ^ (2 * k)) for i in range(n_ch)])
 
     operands = (near_sums(own, weight), other, far)
-    over3, over1 = project(*operands, "opposite", [[(2, 1)], [(2, 0)]], BF16)
+    over3, over1 = opposite(*operands)
     over3, over1 = swap(over3, 3), swap(over1, 1)
     direct3, direct1, mine3, mine1 = sides(*operands)
     direct3, direct1 = swap(direct3, 3), swap(direct1, 1)

time: 43.9 us -> 43.9 us (level)
  no operation moved by 1% of the time
where the time goes in v5:
time: 43.9 us; the launch traced here: 43.7 us
  starting transfers between devices  22.8 us (52%)
  Pallas kernels  10.5 us (24%)
  waiting for transfers between devices  10.4 us (24%)
    ppermute x7, starting transfers between devices, across(): return lax.ppermute(value, 'ctx', [(i, i ^ by) for i in range(n_ctx)])  14.3 us
    pallas_call x14, Pallas kernels, run(): pl.pallas_call(kernel, in_specs=[pl.BlockSpec(memory_space=space) for spa...  10.5 us
    ppermute x6, starting transfers between devices, swap(): return lax.ppermute(value, 'ch', [(i, i ^ 2 * k) for i in range(n_ch)])  8.32 us
    ppermute x7, waiting for transfers between devices, across(): return lax.ppermute(value, 'ctx', [(i, i ^ by) for i in range(n_ctx)])  5.03 us
    ppermute x6, waiting for transfers between devices, swap(): return lax.ppermute(value, 'ch', [(i, i ^ 2 * k) for i in range(n_ch)])  4.52 us
  transfers between devices with their start and end apart: 15, of which 8 were waited for; matrix products, arithmetic and copies ran while one was open for 0% of the time, Pallas kernels for 15%

profile of v5, /device:TPU:32, one launch (start us, length us, event | category | flops | bytes accessed | tf_op | source)
XLA Modules:
  0.0 43.7 jit_solution(669787661536627769)
XLA Ops:
  0.0 2.4 %states.1 = (bf16[32,512]{1,0:T(8,128)(2,1)S(1)}, f32[256,512]{1,0:T(8,128)S(1)}, f32[16,512]{1,0:T(8,128)S(1)}, f32[4,16,512]{2,1,0:T(8,128)S(1)}, f32[2,16,512...) custom-call(bf16[512,256]{1,0:T(8,128)(2,1)} %key_hbm.1, bf16[512,256]{1,0:T(8,128)(2,1)} %value_hbm.1, ...), custom_call_target="tpu_custom_call" | custom-call | tf_op jit(solution)/shard_map/states/pallas_call | solution.py:37
  2.4 2.0 %collective-permute-start = (bf16[32,512]{1,0:T(8,128)(2,1)S(1)}, bf16[32,512]{1,0:T(8,128)(2,1)S(1)}, u32[]{:S(2)}, u32[]{:S(2)}) collective-permute-start(bf16[32,512]{1,0:T(8,128)(2,1)S(1)} %get-tuple-element.28.mine), channel_id=1, source_target_pairs={{0,24},{8,16},{16,8},{24,0},{32,56},{40,48},{48,40},{56,32},{64,88... | collective-permute-start | bytes 98312 | tf_op jit(solution)/shard_map/ppermute | solution.py:649
  4.4 2.3 %collective-permute-start.1 = (bf16[32,512]{1,0:T(8,128)(2,1)S(1)}, bf16[32,512]{1,0:T(8,128)(2,1)S(1)}, u32[]{:S(2)}, u32[]{:S(2)}) collective-permute-start(bf16[32,512]{1,0:T(8,128)(2,1)S(1)} %get-tuple-element.28.mine), channel_id=1, source_target_pairs={{0,16},{8,24},{16,0},{24,8},{32,48},{40,56},{48,32},{56,40},{64,80... | collective-permute-start | bytes 98312 | tf_op jit(solution)/shard_map/ppermute | solution.py:649
  6.7 0.5 %collective-permute-start.2 = (bf16[32,512]{1,0:T(8,128)(2,1)S(1)}, bf16[32,512]{1,0:T(8,128)(2,1)S(1)}, u32[]{:S(2)}, u32[]{:S(2)}) collective-permute-start(bf16[32,512]{1,0:T(8,128)(2,1)S(1)} %get-tuple-element.28.mine), channel_id=1, source_target_pairs={{0,8},{8,0},{16,24},{24,16},{32,40},{40,32},{48,56},{56,48},{64,72... | collective-permute-start | bytes 98312 | tf_op jit(solution)/shard_map/ppermute | solution.py:649
  7.2 0.1 tables.1
  7.4 0.0 collective-permute-done.three
  7.4 2.0 %collective-permute-done.1.two = bf16[32,512]{1,0:T(8,128)(2,1)S(1)} collective-permute-done((bf16[32,512]{1,0:T(8,128)(2,1)S(1)}, bf16[32,512]{1,0:T(8,128)(2,1)S(1)}, u32[]{:S(2)}, u32[]{:S(2)}) %collective-permute-start.1) | collective-permute-done | bytes 32800 | tf_op jit(solution)/shard_map/ppermute | solution.py:649
  9.3 1.3 %collective-permute-done.2.one = bf16[32,512]{1,0:T(8,128)(2,1)S(1)} collective-permute-done((bf16[32,512]{1,0:T(8,128)(2,1)S(1)}, bf16[32,512]{1,0:T(8,128)(2,1)S(1)}, u32[]{:S(2)}, u32[]{:S(2)}) %collective-permute-start.2) | collective-permute-done | bytes 32800 | tf_op jit(solution)/shard_map/ppermute | solution.py:649
  10.6 0.1 merge_four.1
  10.7 0.1 collective-permute-start.8
  10.8 5.1 %collective-permute-start.3 = (bf16[32,512]{1,0:T(8,128)(2,1)S(1)}, bf16[32,512]{1,0:T(8,128)(2,1)S(1)}, u32[]{:S(2)}, u32[]{:S(2)}) collective-permute-start(bf16[32,512]{1,0:T(8,128)(2,1)S(1)} %get-tuple-element.32.after.mine), channel_id=1, source_target_pairs={{0,56},{8,48},{16,40},{24,32},{32,24},{40,16},{48,8},{56,0},{64,12... | collective-permute-start | bytes 98312 | tf_op jit(solution)/shard_map/ppermute | solution.py:649
  15.9 1.6 %weight_blocks.1.after.weight = bf16[512,2048]{1,0:T(8,128)(2,1)S(1)} custom-call(bf16[512,4096]{1,0:T(8,128)(2,1)} %weight_hbm.1, bf16[32,512]{1,0:T(8,128)(2,1)S(1)} %get-tuple-element.32.after.mine), custom_call_target="tpu_custom_call" | custom-call | tf_op jit(solution)/shard_map/weight_blocks/pallas_call | solution.py:37
  17.5 0.4 collective-permute-done.3.theirs
  17.9 3.3 %collective-permute-start.4 = (bf16[32,512]{1,0:T(8,128)(2,1)S(1)}, bf16[32,512]{1,0:T(8,128)(2,1)S(1)}, u32[]{:S(2)}, u32[]{:S(2)}) collective-permute-start(bf16[32,512]{1,0:T(8,128)(2,1)S(1)} %get-tuple-element.35.after.mine), channel_id=1, source_target_pairs={{0,128},{8,136},{16,144},{24,152},{32,160},{40,168},{48,176},{56,1... | collective-permute-start | bytes 98312 | tf_op jit(solution)/shard_map/ppermute | solution.py:649
  21.2 1.1 %collective-permute-start.5 = (bf16[32,512]{1,0:T(8,128)(2,1)S(1)}, bf16[32,512]{1,0:T(8,128)(2,1)S(1)}, u32[]{:S(2)}, u32[]{:S(2)}) collective-permute-start(bf16[32,512]{1,0:T(8,128)(2,1)S(1)} %get-tuple-element.35.after.mine), channel_id=1, source_target_pairs={{0,192},{8,200},{16,208},{24,216},{32,224},{40,232},{48,240},{56,2... | collective-permute-start | bytes 98312 | tf_op jit(solution)/shard_map/ppermute | solution.py:649
  22.3 0.0 collective-permute-start.6
  22.3 2.7 %local_scan.1 = (f32[256,512]{1,0:T(8,128)S(1)}, f32[256,512]{1,0:T(8,128)S(1)}, f32[128,512]{1,0:T(8,128)S(1)}, f32[128,512]{1,0:T(8,128)S(1)}) custom-call(f32[256,512]{1,0:T(8,128)S(1)} %get-tuple-element.38.gated, bf16[512,256]{1,0:T(8,128)(2,1)} %query_hbm.3, f32[16,512]{1,0:T(8,128)S(1)} %get-tuple-element.29.params, f32[29,16,512]{2,1,0:T(8,128)S(1)} %tables.1, ...), custom_call_target="tpu_custom_call" | custom-call | tf_op jit(solution)/shard_map/local_scan/pallas_call | solution.py:37
  25.0 0.0 collective-permute-done.4.row2
  25.0 1.4 %collective-permute-done.5.row3 = bf16[32,512]{1,0:T(8,128)(2,1)S(1)} collective-permute-done((bf16[32,512]{1,0:T(8,128)(2,1)S(1)}, bf16[32,512]{1,0:T(8,128)(2,1)S(1)}, u32[]{:S(2)}, u32[]{:S(2)}) %collective-permute-start.5) | collective-permute-done | bytes 32800 | tf_op jit(solution)/shard_map/ppermute | solution.py:649
  26.4 0.0 collective-permute-done.6.row1
  26.4 0.8 %gated.1.mine = bf16[256,512]{1,0:T(8,128)(2,1)S(1)} custom-call(bf16[32,512]{1,0:T(8,128)(2,1)S(1)} %get-tuple-element.35.after.mine, bf16[32,512]{1,0:T(8,128)(2,1)S(1)} %collective-permute-done.4.row2, bf16[32,512]{1,0:T(8,128)(2,1)S(1)} %collective-permute-done.5.row3, bf16[32,512]{1,0:T(8,128)(2,1)S(1)} %collective-permute-done.6.row1, ...), custom_call_target="tpu_custom_call" | custom-call | tf_op jit(solution)/shard_map/gated/pallas_call | solution.py:37
  27.1 0.1 collective-permute-start.7
  27.2 0.7 %near_sums.1.near_ref = f32[256,2048]{1,0:T(8,128)S(1)} custom-call(bf16[256,512]{1,0:T(8,128)(2,1)S(1)} %gated.1.mine, bf16[512,2048]{1,0:T(8,128)(2,1)S(1)} %weight_blocks.1.after.weight), custom_call_target="tpu_custom_call" | custom-call | tf_op jit(solution)/shard_map/near_sums/pallas_call | solution.py:37
  28.0 0.8 %collective-permute-done.7.other_ref = bf16[256,512]{1,0:T(8,128)(2,1)S(1)} collective-permute-done((bf16[256,512]{1,0:T(8,128)(2,1)S(1)}, bf16[256,512]{1,0:T(8,128)(2,1)S(1)}, u32[]{:S(2)}, u32[]{:S(2)}) %collective-permute-start.7) | collective-permute-done | bytes 262176 | tf_op jit(solution)/shard_map/ppermute | solution.py:663
  28.8 0.0 collective-permute-done.8.far_ref
  28.8 0.3 opposite.1
  29.1 1.6 %collective-permute-start.13 = (bf16[128,512]{1,0:T(8,128)(2,1)S(1)}, bf16[128,512]{1,0:T(8,128)(2,1)S(1)}, u32[]{:S(2)}, u32[]{:S(2)}) collective-permute-start(bf16[128,512]{1,0:T(8,128)(2,1)S(1)} %get-tuple-element.49), channel_id=1, source_target_pairs={{0,2},{1,3},{2,0},{3,1},{4,6},{5,7},{6,4},{7,5},{8,10},{9,11},{10,... | collective-permute-start | bytes 393224 | tf_op jit(solution)/shard_map/ppermute | solution.py:666
  30.7 2.1 %collective-permute-start.11 = (bf16[128,512]{1,0:T(8,128)(2,1)S(1)}, bf16[128,512]{1,0:T(8,128)(2,1)S(1)}, u32[]{:S(2)}, u32[]{:S(2)}) collective-permute-start(bf16[128,512]{1,0:T(8,128)(2,1)S(1)} %get-tuple-element.47), channel_id=1, source_target_pairs={{0,6},{1,7},{2,4},{3,5},{4,2},{5,3},{6,0},{7,1},{8,14},{9,15},{10,... | collective-permute-start | bytes 393224 | tf_op jit(solution)/shard_map/ppermute | solution.py:666
  32.8 0.4 sides.1
  33.2 1.2 %collective-permute-start.10 = (bf16[128,512]{1,0:T(8,128)(2,1)S(1)}, bf16[128,512]{1,0:T(8,128)(2,1)S(1)}, u32[]{:S(2)}, u32[]{:S(2)}) collective-permute-start(bf16[128,512]{1,0:T(8,128)(2,1)S(1)} %get-tuple-element.46), channel_id=1, source_target_pairs={{0,6},{1,7},{2,4},{3,5},{4,2},{5,3},{6,0},{7,1},{8,14},{9,15},{10,... | collective-permute-start | bytes 393224 | tf_op jit(solution)/shard_map/ppermute | solution.py:666
  34.4 0.0 collective-permute-start.9
  34.4 0.3 collective-permute-done.13.passing
  34.7 2.8 %collective-permute-start.14 = (bf16[128,512]{1,0:T(8,128)(2,1)S(1)}, bf16[128,512]{1,0:T(8,128)(2,1)S(1)}, u32[]{:S(2)}, u32[]{:S(2)}) collective-permute-start(bf16[128,512]{1,0:T(8,128)(2,1)S(1)} %relay.3), channel_id=1, source_target_pairs={{0,6},{1,7},{2,4},{3,5},{4,2},{5,3},{6,0},{7,1},{8,14},{9,15},{10,... | collective-permute-start | bytes 393224 | tf_op jit(solution)/shard_map/ppermute | solution.py:666
  37.6 0.0 collective-permute-done.11.passing
  37.6 0.6 %collective-permute-start.12 = (bf16[128,512]{1,0:T(8,128)(2,1)S(1)}, bf16[128,512]{1,0:T(8,128)(2,1)S(1)}, u32[]{:S(2)}, u32[]{:S(2)}) collective-permute-start(bf16[128,512]{1,0:T(8,128)(2,1)S(1)} %relay.2), channel_id=1, source_target_pairs={{0,2},{1,3},{2,0},{3,1},{4,6},{5,7},{6,4},{7,5},{8,10},{9,11},{10,... | collective-permute-start | bytes 393224 | tf_op jit(solution)/shard_map/ppermute | solution.py:666
  38.2 0.3 kept.1.own
  38.5 2.4 %collective-permute-done.10.direct3 = bf16[128,512]{1,0:T(8,128)(2,1)S(1)} collective-permute-done((bf16[128,512]{1,0:T(8,128)(2,1)S(1)}, bf16[128,512]{1,0:T(8,128)(2,1)S(1)}, u32[]{:S(2)}, u32[]{:S(2)}) %collective-permute-start.10) | collective-permute-done | bytes 131104 | tf_op jit(solution)/shard_map/ppermute | solution.py:666
  40.9 0.0 collective-permute-done.9.direct1
  40.9 1.8 %collective-permute-done.14.joined3 = bf16[128,512]{1,0:T(8,128)(2,1)S(1)} collective-permute-done((bf16[128,512]{1,0:T(8,128)(2,1)S(1)}, bf16[128,512]{1,0:T(8,128)(2,1)S(1)}, u32[]{:S(2)}, u32[]{:S(2)}) %collective-permute-start.14) | collective-permute-done | bytes 131104 | tf_op jit(solution)/shard_map/ppermute | solution.py:666
  42.7 0.0 collective-permute-done.12.joined1
  42.7 1.0 %finish.1 = bf16[512,256]{1,0:T(8,128)(2,1)} custom-call(f32[256,512]{1,0:T(8,128)S(1)} %kept.1.own, bf16[128,512]{1,0:T(8,128)(2,1)S(1)} %collective-permute-done.9.direct1, bf16[128,512]{1,0:T(8,128)(2,1)S(1)} %collective-permute-done.10.direct3, bf16[128,512]{1,0:T(8,128)(2,1)S(1)} %collective-permute-done.12.joined1, ...), custom_call_target="tpu_custom_call" | custom-call | tf_op jit(solution)/shard_map/finish/pallas_call | solution.py:37
  (3 shorter events, 0.1 us)
Async XLA Ops:
  2.4 5.0 %collective-permute-start = (bf16[32,512]{1,0:T(8,128)(2,1)S(1)}, bf16[32,512]{1,0:T(8,128)(2,1)S(1)}, u32[]{:S(2)}, u32[]{:S(2)}) collective-permute-start(bf16[32,512]{1,0:T(8,128)(2,1)S(1)} %get-tuple-element.28.mine), channel_id=1, source_target_pairs={{0,24},{8,16},{16,8},{24,0},{32,56},{40,48},{48,40},{56,32},{64,88... | collective-permute-start | bytes 98312 | tf_op jit(solution)/shard_map/ppermute | solution.py:649
  4.4 4.9 %collective-permute-start.1 = (bf16[32,512]{1,0:T(8,128)(2,1)S(1)}, bf16[32,512]{1,0:T(8,128)(2,1)S(1)}, u32[]{:S(2)}, u32[]{:S(2)}) collective-permute-start(bf16[32,512]{1,0:T(8,128)(2,1)S(1)} %get-tuple-element.28.mine), channel_id=1, source_target_pairs={{0,16},{8,24},{16,0},{24,8},{32,48},{40,56},{48,32},{56,40},{64,80... | collective-permute-start | bytes 98312 | tf_op jit(solution)/shard_map/ppermute | solution.py:649
  6.7 3.9 %collective-permute-start.2 = (bf16[32,512]{1,0:T(8,128)(2,1)S(1)}, bf16[32,512]{1,0:T(8,128)(2,1)S(1)}, u32[]{:S(2)}, u32[]{:S(2)}) collective-permute-start(bf16[32,512]{1,0:T(8,128)(2,1)S(1)} %get-tuple-element.28.mine), channel_id=1, source_target_pairs={{0,8},{8,0},{16,24},{24,16},{32,40},{40,32},{48,56},{56,48},{64,72... | collective-permute-start | bytes 98312 | tf_op jit(solution)/shard_map/ppermute | solution.py:649
  10.7 18.0 %collective-permute-start.8 = (bf16[512,4096]{1,0:T(8,128)(2,1)}, bf16[512,4096]{1,0:T(8,128)(2,1)S(1)}, u32[]{:S(2)}, u32[]{:S(2)}) collective-permute-start(bf16[512,4096]{1,0:T(8,128)(2,1)} %weight_hbm.1), channel_id=1, source_target_pairs={{0,1},{1,0},{2,3},{3,2},{4,5},{5,4},{6,7},{7,6},{8,9},{9,8},{10,11... | collective-permute-start | bytes 12582920 | tf_op jit(solution)/shard_map/ppermute | solution.py:655
  10.8 7.1 %collective-permute-start.3 = (bf16[32,512]{1,0:T(8,128)(2,1)S(1)}, bf16[32,512]{1,0:T(8,128)(2,1)S(1)}, u32[]{:S(2)}, u32[]{:S(2)}) collective-permute-start(bf16[32,512]{1,0:T(8,128)(2,1)S(1)} %get-tuple-element.32.after.mine), channel_id=1, source_target_pairs={{0,56},{8,48},{16,40},{24,32},{32,24},{40,16},{48,8},{56,0},{64,12... | collective-permute-start | bytes 98312 | tf_op jit(solution)/shard_map/ppermute | solution.py:649
  17.9 7.0 %collective-permute-start.4 = (bf16[32,512]{1,0:T(8,128)(2,1)S(1)}, bf16[32,512]{1,0:T(8,128)(2,1)S(1)}, u32[]{:S(2)}, u32[]{:S(2)}) collective-permute-start(bf16[32,512]{1,0:T(8,128)(2,1)S(1)} %get-tuple-element.35.after.mine), channel_id=1, source_target_pairs={{0,128},{8,136},{16,144},{24,152},{32,160},{40,168},{48,176},{56,1... | collective-permute-start | bytes 98312 | tf_op jit(solution)/shard_map/ppermute | solution.py:649
  21.2 5.1 %collective-permute-start.5 = (bf16[32,512]{1,0:T(8,128)(2,1)S(1)}, bf16[32,512]{1,0:T(8,128)(2,1)S(1)}, u32[]{:S(2)}, u32[]{:S(2)}) collective-permute-start(bf16[32,512]{1,0:T(8,128)(2,1)S(1)} %get-tuple-element.35.after.mine), channel_id=1, source_target_pairs={{0,192},{8,200},{16,208},{24,216},{32,224},{40,232},{48,240},{56,2... | collective-permute-start | bytes 98312 | tf_op jit(solution)/shard_map/ppermute | solution.py:649
  22.3 4.1 %collective-permute-start.6 = (bf16[32,512]{1,0:T(8,128)(2,1)S(1)}, bf16[32,512]{1,0:T(8,128)(2,1)S(1)}, u32[]{:S(2)}, u32[]{:S(2)}) collective-permute-start(bf16[32,512]{1,0:T(8,128)(2,1)S(1)} %get-tuple-element.35.after.mine), channel_id=1, source_target_pairs={{0,64},{8,72},{16,80},{24,88},{32,96},{40,104},{48,112},{56,120},{... | collective-permute-start | bytes 98312 | tf_op jit(solution)/shard_map/ppermute | solution.py:649
  27.1 1.6 %collective-permute-start.7 = (bf16[256,512]{1,0:T(8,128)(2,1)S(1)}, bf16[256,512]{1,0:T(8,128)(2,1)S(1)}, u32[]{:S(2)}, u32[]{:S(2)}) collective-permute-start(bf16[256,512]{1,0:T(8,128)(2,1)S(1)} %gated.1.mine), channel_id=1, source_target_pairs={{0,1},{1,0},{2,3},{3,2},{4,5},{5,4},{6,7},{7,6},{8,9},{9,8},{10,11... | collective-permute-start | bytes 786440 | tf_op jit(solution)/shard_map/ppermute | solution.py:663
  29.1 5.6 %collective-permute-start.13 = (bf16[128,512]{1,0:T(8,128)(2,1)S(1)}, bf16[128,512]{1,0:T(8,128)(2,1)S(1)}, u32[]{:S(2)}, u32[]{:S(2)}) collective-permute-start(bf16[128,512]{1,0:T(8,128)(2,1)S(1)} %get-tuple-element.49), channel_id=1, source_target_pairs={{0,2},{1,3},{2,0},{3,1},{4,6},{5,7},{6,4},{7,5},{8,10},{9,11},{10,... | collective-permute-start | bytes 393224 | tf_op jit(solution)/shard_map/ppermute | solution.py:666
  30.7 6.9 %collective-permute-start.11 = (bf16[128,512]{1,0:T(8,128)(2,1)S(1)}, bf16[128,512]{1,0:T(8,128)(2,1)S(1)}, u32[]{:S(2)}, u32[]{:S(2)}) collective-permute-start(bf16[128,512]{1,0:T(8,128)(2,1)S(1)} %get-tuple-element.47), channel_id=1, source_target_pairs={{0,6},{1,7},{2,4},{3,5},{4,2},{5,3},{6,0},{7,1},{8,14},{9,15},{10,... | collective-permute-start | bytes 393224 | tf_op jit(solution)/shard_map/ppermute | solution.py:666
  33.2 7.7 %collective-permute-start.10 = (bf16[128,512]{1,0:T(8,128)(2,1)S(1)}, bf16[128,512]{1,0:T(8,128)(2,1)S(1)}, u32[]{:S(2)}, u32[]{:S(2)}) collective-permute-start(bf16[128,512]{1,0:T(8,128)(2,1)S(1)} %get-tuple-element.46), channel_id=1, source_target_pairs={{0,6},{1,7},{2,4},{3,5},{4,2},{5,3},{6,0},{7,1},{8,14},{9,15},{10,... | collective-permute-start | bytes 393224 | tf_op jit(solution)/shard_map/ppermute | solution.py:666
  34.4 6.5 %collective-permute-start.9 = (bf16[128,512]{1,0:T(8,128)(2,1)S(1)}, bf16[128,512]{1,0:T(8,128)(2,1)S(1)}, u32[]{:S(2)}, u32[]{:S(2)}) collective-permute-start(bf16[128,512]{1,0:T(8,128)(2,1)S(1)} %get-tuple-element.45), channel_id=1, source_target_pairs={{0,2},{1,3},{2,0},{3,1},{4,6},{5,7},{6,4},{7,5},{8,10},{9,11},{10,... | collective-permute-start | bytes 393224 | tf_op jit(solution)/shard_map/ppermute | solution.py:666
  34.7 8.0 %collective-permute-start.14 = (bf16[128,512]{1,0:T(8,128)(2,1)S(1)}, bf16[128,512]{1,0:T(8,128)(2,1)S(1)}, u32[]{:S(2)}, u32[]{:S(2)}) collective-permute-start(bf16[128,512]{1,0:T(8,128)(2,1)S(1)} %relay.3), channel_id=1, source_target_pairs={{0,6},{1,7},{2,4},{3,5},{4,2},{5,3},{6,0},{7,1},{8,14},{9,15},{10,... | collective-permute-start | bytes 393224 | tf_op jit(solution)/shard_map/ppermute | solution.py:666
  37.6 5.1 %collective-permute-start.12 = (bf16[128,512]{1,0:T(8,128)(2,1)S(1)}, bf16[128,512]{1,0:T(8,128)(2,1)S(1)}, u32[]{:S(2)}, u32[]{:S(2)}) collective-permute-start(bf16[128,512]{1,0:T(8,128)(2,1)S(1)} %relay.2), channel_id=1, source_target_pairs={{0,2},{1,3},{2,0},{3,1},{4,6},{5,7},{6,4},{7,5},{8,10},{9,11},{10,... | collective-permute-start | bytes 393224 | tf_op jit(solution)/shard_map/ppermute | solution.py:666
